TPU v7x, 32 devices: a whole 2x2x4 slice. The times are simulated.
32 devices in a mesh: dp: 8 (over z, y), lab: 4 (over x, core).
Axes of the slice: x: 2, y: 2, z: 4, core: 2. Of those that a mesh axis runs over, the one named last changes fastest.
Arguments:
- frames_in: bfloat16 [64, 64, 512], P(('dp', 'lab')), may hold values from -6 to 6
- predictor: bfloat16 [64, 4, 16, 640], P('dp', None, 'lab'), may hold values from -6 to 6
- seg_lengths: int32 [64, 4], P('dp'), may hold values from 1 to 32, 64 in all within a row
- label_counts: int32 [64, 4], P('dp'), may hold values from 1 to 15, 32 in all within a row
- label_ids: int32 [64, 4, 16], P('dp', None, 'lab'), may hold values from 0 to 1023
- gain_ffn: bfloat16 [512], P('dp'), may hold values from 0.5 to 1.5
- w_ffn_in: bfloat16 [512, 2048], P(None, 'dp'), may hold values from -0.25 to 0.25
- w_ffn_out: bfloat16 [2048, 512], P('dp'), may hold values from -0.125 to 0.125
- gain_att: bfloat16 [512], P('dp'), may hold values from 0.5 to 1.5
- w_qkv: bfloat16 [512, 1536], P(None, 'dp'), may hold values from -0.25 to 0.25
- w_att_out: bfloat16 [512, 512], P('dp'), may hold values from -1 to 1
- gain_conv: bfloat16 [512], P('dp'), may hold values from 0.5 to 1.5
- w_point_in: bfloat16 [512, 1024], P(None, 'dp'), may hold values from -0.25 to 0.25
- w_depth: bfloat16 [9, 512], P(None, 'dp'), may hold values from -2 to 2
- gain_depth: bfloat16 [512], P('dp'), may hold values from 0.5 to 1.5
- w_point_out: bfloat16 [512, 512], P('dp'), may hold values from -0.25 to 0.25
- gain_out: bfloat16 [512], P('dp'), may hold values from 0.5 to 1.5
- w_enc: bfloat16 [512, 640], P(None, 'dp'), may hold values from -0.25 to 0.25
- w_pred: bfloat16 [640, 640], P(None, 'dp'), may hold values from -0.25 to 0.25
- bias_joint: bfloat16 [640], P('dp'), may hold values from -3 to 3
- w_joint_out: bfloat16 [640, 1030], P('dp'), may hold values from -0.5 to 0.5
- bias_out: bfloat16 [1030], replicated, may hold values from -5 to 5
Outputs:
- loss_frame: float32 [64, 4], P('dp')
- encoded: bfloat16 [64, 64, 512], P(('dp', 'lab'))
- grad_frames: float32 [64, 64, 512], P(('dp', 'lab'))
- grad_predictor: float32 [64, 4, 16, 640], P('dp', None, 'lab')
- grad_gain_ffn: float32 [512], P('dp')
- grad_w_ffn_in: float32 [512, 2048], P(None, 'dp')
- grad_w_ffn_out: float32 [2048, 512], P('dp')
- grad_gain_att: float32 [512], P('dp')
- grad_w_qkv: float32 [512, 1536], P(None, 'dp')
- grad_w_att_out: float32 [512, 512], P('dp')
- grad_gain_conv: float32 [512], P('dp')
- grad_w_point_in: float32 [512, 1024], P(None, 'dp')
- grad_w_depth: float32 [9, 512], P(None, 'dp')
- grad_gain_depth: float32 [512], P('dp')
- grad_w_point_out: float32 [512, 512], P('dp')
- grad_gain_out: float32 [512], P('dp')
- grad_w_enc: float32 [512, 640], P(None, 'dp')
- grad_w_pred: float32 [640, 640], P(None, 'dp')
- grad_bias_joint: float32 [640], P('dp')
- grad_w_joint_out: float32 [640, 1030], P('dp')
- grad_bias_out: float32 [1030], replicated
Inputs may be any that keep to these rules, and one draw needn't show every extreme that they name: `seg_lengths`: the 4 lengths of a row sum to 64; in every row one utterance has 32 frames. `label_counts`: the 4 counts of a row sum to 32; in every row one utterance has 15 labels. `label_ids`: ids past an utterance's label count are drawn too and do not count; the blank never appears.
All inputs are finite; a program needn't handle non-finite values.
Results may differ from a plain program's by a relative error of at most 0.025.
Values may be sent and summed in bfloat16 or wider, within the bound.
A program may use at most 128 MiB of HBM per device.

v0:
```python
import functools

import jax
import jax.numpy as jnp
from jax import lax
from jax.experimental import pallas as pl
from jax.experimental.pallas import tpu as pltpu
from jax.sharding import PartitionSpec as P


MESH = pl.DeviceIdType.MESH
F32 = jnp.float32
BF = jnp.bfloat16
TILE = 16


def ring_place(dp, n):
    odd = dp % 2
    return (1 - odd) * (dp // 2) + odd * (n - 1 - dp // 2)


def ring_device(place, n):
    place = (place + 2 * n) % n
    high = place // (n // 2)
    return (1 - high) * (2 * place) + high * (2 * (n - 1 - place) + 1)


def x_rows(rows, share):
    tiles = rows // TILE
    return min(tiles // 2, int(tiles * share + 0.5)) * TILE


class Where:
    def __init__(self, n):
        self.n = n
        self.dp = lax.axis_index("dp")
        self.lab = lax.axis_index("lab")
        self.core = self.lab % 2
        self.side = self.lab // 2
        self.place = ring_place(self.dp, n)
        self.right = (ring_device(self.place + 1, n), self.lab)
        self.left = (ring_device(self.place - 1, n), self.lab)
        self.twin = (self.dp, self.side * 2 + 1 - self.core)
        self.across = (self.dp, (1 - self.side) * 2 + self.core)
        self.far = (
            ring_device(self.place + 1 - 2 * self.core, n),
            self.lab,
        )

    def at(self, distance):
        return ring_device(self.place + distance, self.n)

    def greet(self):
        barrier = pltpu.get_barrier_semaphore()
        for other in (self.right, self.left, self.twin, self.across):
            pl.semaphore_signal(barrier, inc=1, device_id=other, device_id_type=MESH)
        pl.semaphore_wait(barrier, 4)


def remote(src, dst, send_sem, recv_sem, device):
    return pltpu.make_async_remote_copy(
        src_ref=src,
        dst_ref=dst,
        send_sem=send_sem,
        recv_sem=recv_sem,
        device_id=device,
        device_id_type=MESH,
    )


class Gather:
    def __init__(self, where, source, target, rows, ring_recv, x_recv, sems):
        self.w, self.source, self.target, self.rows = where, source, target, rows
        self.width = target.shape[1]
        self.half = self.width // 2
        self.cut = x_rows(rows, 0.3)
        self.ring_recv, self.x_recv, self.sems = ring_recv, x_recv, sems
        self.steps = where.n // 2

    def lanes(self):
        return pl.ds(pl.multiple_of(self.w.core * self.half, 128), self.half)

    def rows_at(self, shard, offset, size):
        base = shard * self.rows if shard is not None else 0
        return pl.ds(pl.multiple_of(base + offset, TILE), size)

    def ring_part(self, ref, shard):
        return ref.at[self.rows_at(shard, self.w.side * self.cut, self.rows - self.cut), self.lanes()]

    def x_part(self, ref, shard, side):
        return ref.at[self.rows_at(shard, side * (self.rows - self.cut), self.cut), self.lanes()]

    def slot(self, distance):
        return distance + self.steps - 1 if distance < 0 else distance + self.steps - 2

    def hop(self, distance, first):
        w = self.w
        if distance == self.steps:
            shard = w.at((2 * w.core - 1) * (self.steps - 1))
            device = w.far
        else:
            shard = w.at(distance + 1) if distance < 0 else w.at(distance - 1)
            device = w.right if distance < 0 else w.left
        src = self.ring_part(self.source, None) if first else self.ring_part(self.target, shard)
        slot = 2 * self.steps - 2 if distance == self.steps else self.slot(distance)
        remote(src, self.ring_part(self.target, shard), self.sems.at[1], self.ring_recv.at[slot], device).start()

    def own(self):
        pltpu.make_async_copy(
            self.source, self.target.at[self.rows_at(self.w.dp, 0, self.rows), :], self.sems.at[4]
        ).start()

    def arrived(self, distance):
        w = self.w
        shard = w.at(distance)
        slot = 2 * self.steps - 2 if distance == self.steps else self.slot(distance)
        part = self.ring_part(self.target, shard)
        remote(part, part, self.sems.at[1], self.ring_recv.at[slot], w.right).wait_recv()

    def spread(self, distance):
        w = self.w
        shard = w.at(distance)
        slot = 2 * self.steps - 2 if distance == self.steps else self.slot(distance)
        if self.cut:
            part = self.x_part(self.target, shard, w.side)
            remote(part, part, self.sems.at[2], self.x_recv.at[slot], w.across).start()
        part = self.ring_part(self.target, shard)
        remote(part, part, self.sems.at[3], self.sems.at[0], w.twin).start()

    def crossed(self, distance):
        if not self.cut:
            return
        w = self.w
        shard = w.at(distance)
        slot = 2 * self.steps - 2 if distance == self.steps else self.slot(distance)
        part = self.x_part(self.target, shard, 1 - w.side)
        remote(part, part, self.sems.at[2], self.x_recv.at[slot], w.across).wait_recv()
        remote(part, part, self.sems.at[3], self.sems.at[0], w.twin).start()

    def whole(self):
        part = self.target.at[pl.ds(0, (self.w.n - 1) * self.rows), pl.ds(0, self.half)]
        remote(part, part, self.sems.at[3], self.sems.at[0], self.w.twin).wait_recv()
        pltpu.make_async_copy(
            self.source, self.target.at[self.rows_at(self.w.dp, 0, self.rows), :], self.sems.at[4]
        ).wait()

    def drain(self):
        count = self.w.n - 1
        for sem, rows in ((1, self.rows - self.cut), (2, self.cut), (3, self.rows)):
            if rows:
                part = self.target.at[pl.ds(0, count * rows), pl.ds(0, self.half)]
                remote(part, part, self.sems.at[sem], self.sems.at[sem], self.w.twin).wait_send()

    def step(self, s):
        if s == 0:
            self.own()
        if 1 <= s < self.steps:
            self.arrived(-s)
            self.arrived(s)
        if s == self.steps:
            self.arrived(self.steps)
        if s < self.steps - 1:
            self.hop(-s - 1, s == 0)
            self.hop(s + 1, s == 0)
        elif s == self.steps - 1:
            self.hop(self.steps, False)
        if 1 <= s < self.steps:
            self.spread(-s)
            self.spread(s)
        if s == self.steps:
            self.spread(self.steps)
        if 2 <= s <= self.steps:
            self.crossed(-s + 1)
            self.crossed(s - 1)
        if s == self.steps + 1:
            self.crossed(self.steps)


def gather_kernel(n, rows_list, *refs):
    k = len(rows_list)
    sources, targets = refs[:k], refs[k : 2 * k]
    ring_recv, x_recv, sems = refs[2 * k :]
    w = Where(n)
    w.greet()
    parts = [
        Gather(w, sources[i], targets[i], rows_list[i], ring_recv.at[i], x_recv.at[i], sems.at[i])
        for i in range(k)
    ]
    turns = n // 2 + 2
    for tick in range(k + turns - 1):
        for s in range(turns - 1, -1, -1):
            g = tick - s
            if 0 <= g < k:
                parts[g].step(s)
    for part in parts:
        part.whole()
        part.drain()


def gather_all(n, shards):
    k = len(shards)
    rows_list = [s.shape[0] for s in shards]
    return pl.pallas_call(
        functools.partial(gather_kernel, n, rows_list),
        out_shape=[jax.ShapeDtypeStruct((n * s.shape[0], s.shape[1]), s.dtype) for s in shards],
        in_specs=[pl.BlockSpec(memory_space=pltpu.VMEM)] * k,
        out_specs=[pl.BlockSpec(memory_space=pltpu.VMEM)] * k,
        scratch_shapes=[
            pltpu.SemaphoreType.DMA((k, n - 1)),
            pltpu.SemaphoreType.DMA((k, n - 1)),
            pltpu.SemaphoreType.DMA((k, 5)),
        ],
        compiler_params=pltpu.CompilerParams(
            collective_id=0, has_side_effects=True, vmem_limit_bytes=56 * 2**20
        ),
    )(*shards)


class Scatter:
    STAGES = 9

    def __init__(self, where, grads, out, rows, bufs, send, recv):
        self.w, self.grads, self.out, self.rows = where, grads, out, rows
        self.held, self.xbuf, self.rbuf, self.final = bufs
        self.half = grads.shape[1] // 2
        self.cut = x_rows(rows, SHARE_RS)
        self.send, self.recv = send, recv
        self.depth = where.n // 2 - 1
        self.started = []

    def lanes(self, core):
        return pl.ds(pl.multiple_of(core * self.half, 128), self.half)

    def rows_at(self, shard, offset, size):
        return pl.ds(pl.multiple_of(shard * self.rows + offset, TILE), size)

    def go(self, sem, src, dst, device):
        copy = remote(src, dst, self.send.at[sem], self.recv.at[sem], device)
        copy.start()
        self.started.append(copy)

    def got(self, sem, dst):
        remote(dst, dst, self.send.at[sem], self.recv.at[sem], self.w.twin).wait_recv()

    def mine(self, shard):
        return self.held[self.rows_at(shard, self.w.side * self.cut, self.rows - self.cut), :].astype(F32)

    def stage(self, s):
        w, rows, cut, depth = self.w, self.rows, self.cut, self.depth
        n, keep = w.n, self.rows - self.cut
        if s == 0:
            self.go(0, self.grads.at[:, self.lanes(1 - w.core)], self.held, w.twin)
        elif s == 1:
            self.got(0, self.held)

            def add(i, _):
                at = self.rows_at(i, 0, rows)
                self.held[at, :] = (
                    self.held[at, :].astype(F32) + self.grads[at, self.lanes(w.core)].astype(F32)
                ).astype(BF)
                return 0

            lax.fori_loop(0, n, add, 0)
            if cut:
                for i in range(n):
                    src = self.held.at[self.rows_at(i, (1 - w.side) * keep, cut), :]
                    remote(src, self.xbuf.at[i], self.send.at[1], self.recv.at[1], w.across).start()
        elif s == 2:
            if cut:
                self.got(1, self.xbuf)

                def add(i, _):
                    at = self.rows_at(i, w.side * keep, cut)
                    self.held[at, :] = (
                        self.held[at, :].astype(F32) + self.xbuf[i].astype(F32)
                    ).astype(BF)
                    return 0

                lax.fori_loop(0, n, add, 0)
            dest = w.at((2 * w.core - 1) * (depth + 1))
            src = self.held.at[self.rows_at(dest, w.side * cut, keep), :]
            self.go(2, src, self.rbuf.at[2 * depth], w.far_back)
        elif s < 3 + depth:
            hop = s - 3
            for way in (0, 1):
                sign = 1 - 2 * way
                own = self.mine(w.at(sign * (depth - hop)))
                slot = 2 * hop + way
                if hop == 0:
                    if way == 0:
                        self.got(2, self.rbuf.at[2 * depth])
                    far = self.rbuf[2 * depth].astype(F32)
                    pick = w.core if way == 0 else 1 - w.core
                    own = own + jnp.where(pick == 1, far, 0.0)
                    at = 2 * depth + 1 + way
                else:
                    at = slot - 2
                    self.got(3 + at, self.rbuf.at[at])
                    own = own + self.rbuf[at].astype(F32)
                self.rbuf[at] = own.astype(BF)
                self.go(3 + slot, self.rbuf.at[at], self.rbuf.at[slot], w.right if way == 0 else w.left)
        elif s == 3 + depth:
            total = self.mine(w.dp)
            for way in (0, 1):
                at = 2 * depth - 2 + way
                self.got(3 + at, self.rbuf.at[at])
                total = total + self.rbuf[at].astype(F32)
            self.final[0] = total.astype(BF)
            self.go(3 + 2 * depth, self.final.at[0], self.final.at[1], w.across)
        elif s == 4 + depth:
            self.got(3 + 2 * depth, self.final.at[1])
            lanes = self.lanes(w.core)
            own, other = self.final[0].astype(F32), self.final[1].astype(F32)
            if cut:
                first = w.side == 0
                low, high = jnp.where(first, own, other), jnp.where(first, other, own)
                self.out[:cut, lanes] = low[:cut].astype(BF)
                if keep > cut:
                    self.out[cut:keep, lanes] = (low[cut:] + high[: keep - cut]).astype(BF)
                self.out[keep:, lanes] = high[keep - cut :].astype(BF)
            else:
                self.out[:, lanes] = (own + other).astype(BF)
            part = self.out.at[:, lanes]
            self.go(4 + 2 * depth, part, part, w.twin)
        elif s == 5 + depth:
            self.got(4 + 2 * depth, self.out.at[:, self.lanes(1 - w.core)])

    def drain(self):
        for copy in self.started:
            copy.wait_send()
        if self.cut:
            remote(self.xbuf, self.xbuf, self.send.at[1], self.recv.at[1], self.w.across).wait_send()


SHARE_RS = 0.25


def scatter_scratch(n, rows, width, k_index=None):
    half, cut, depth = width // 2, x_rows(rows, SHARE_RS), n // 2 - 1
    return [
        pltpu.VMEM((n * rows, half), BF),
        pltpu.VMEM((n, max(cut, TILE), half), BF),
        pltpu.VMEM((2 * depth + 3, rows - cut, half), BF),
        pltpu.VMEM((2, rows - cut, half), BF),
    ]


def scatter_sems(n, k):
    return [pltpu.SemaphoreType.DMA((k, n + 3)), pltpu.SemaphoreType.DMA((k, n + 3))]


def scatter_kernel(n, rows_list, skew, *refs):
    k = len(rows_list)
    grads, outs = refs[:k], refs[k : 2 * k]
    bufs = refs[2 * k : 2 * k + 4 * k]
    send, recv = refs[6 * k :]
    w = Where(n)
    w.far_back = (ring_device(w.place + 2 * w.core - 1, n), w.lab)
    w.greet()
    parts = [
        Scatter(w, grads[i], outs[i], rows_list[i], bufs[4 * i : 4 * i + 4], send.at[i], recv.at[i])
        for i in range(k)
    ]
    stages = n // 2 + 5
    for tick in range(k + skew * (stages - 1)):
        for s in range(stages - 1, -1, -1):
            g = tick - skew * s
            if 0 <= g < k:
                parts[g].stage(s)
    for part in parts:
        part.drain()


def scatter_all(n, grads, skew=1):
    k = len(grads)
    rows_list = [g.shape[0] // n for g in grads]
    scratch = []
    for g, rows in zip(grads, rows_list):
        scratch += scatter_scratch(n, rows, g.shape[1])
    return pl.pallas_call(
        functools.partial(scatter_kernel, n, rows_list, skew),
        out_shape=[jax.ShapeDtypeStruct((rows, g.shape[1]), BF) for g, rows in zip(grads, rows_list)],
        in_specs=[pl.BlockSpec(memory_space=pltpu.VMEM)] * k,
        out_specs=[pl.BlockSpec(memory_space=pltpu.VMEM)] * k,
        scratch_shapes=scratch + scatter_sems(n, k),
        compiler_params=pltpu.CompilerParams(
            collective_id=1, has_side_effects=True, vmem_limit_bytes=60 * 2**20
        ),
    )(*grads)


LOW = -100000.0
TOK = 1024
KINDS = 7
BIAS_LANE = 6


def mm(a, b):
    return lax.dot_general(a, b, (((1,), (0,)), ((), ())), preferred_element_type=F32)


def mm_t(a, b):
    return lax.dot_general(a, b, (((1,), (1,)), ((), ())), preferred_element_type=F32)


def t_mm(a, b):
    return lax.dot_general(a, b, (((0,), (0,)), ((), ())), preferred_element_type=F32)


def lane_ids(shape):
    return lax.broadcasted_iota(jnp.int32, shape, len(shape) - 1)


def row_ids(shape):
    return lax.broadcasted_iota(jnp.int32, shape, 0)


class Peers:
    def __init__(self):
        self.dp, self.lab = lax.axis_index("dp"), lax.axis_index("lab")
        self.core, self.side = self.lab % 2, self.lab // 2

    def owner(self, j):
        return ((self.side + j // 2) % 2) * 2 + (self.core + j % 2) % 2

    def device(self, j):
        return (self.dp, self.owner(j))


def seg_of(t, ends):
    return sum((t >= e).astype(jnp.int32) for e in ends[:-1])


def pick(seg, values):
    out = values[0]
    for s in range(1, len(values)):
        out = jnp.where(seg == s, values[s], out)
    return out


def scalar_ends(lengths, r, segs):
    ends, total = [], 0
    for s in range(segs):
        total = total + lengths[r, s]
        ends.append(total)
    return ends


def lse_of(terms):
    top = functools.reduce(jnp.maximum, terms)
    return top, functools.reduce(jnp.add, [jnp.exp(v - top) for v in terms])


def lattice(peers, lengths, counts, terms, skewed, hist, grads, loss, dims):
    frames, rows, segs, own_u, labs = dims
    wide = (frames, 128)
    lane = lane_ids(wide)
    group = rows * own_u
    j, row, u = lane % own_u, (lane % group) // own_u, (lane // group) * own_u + lane % own_u
    t = row_ids(wide)
    all_ends = [scalar_ends(lengths, r, segs) for r in range(rows)]

    def per_lane(values):
        out = jnp.zeros(wide, jnp.int32)
        for r in range(rows):
            out = jnp.where(row == r, values[r], out)
        return out

    ends = [per_lane([all_ends[r][s] for r in range(rows)]) for s in range(segs)]
    labels_in = [per_lane([counts[r, s] for r in range(rows)]) for s in range(segs)]
    seg = seg_of(t, ends)
    stop = pick(seg, ends)
    begin = pick(seg, [jnp.zeros(wide, jnp.int32)] + ends[:-1])
    target = pick(seg, labels_in)
    remain, first = stop - t, t == begin

    kinds = []
    per_vreg = 128 // group
    for k in range(KINDS):
        value = None
        for dev in range(labs):
            part = terms[dev, :, (k // per_vreg) * 128 : (k // per_vreg) * 128 + 128]
            shift = (dev - k % per_vreg) * group % 128
            part = pltpu.roll(part, shift, 1) if shift else part
            value = part if value is None else jnp.where(lane // group == dev, part, value)
        kinds.append(value)
    blank_lp, durs, label_lp = kinds[0], kinds[1:6], kinds[6]
    last_u = own_u * labs - 1
    emit, blank, blank_raw = [], [None], [None]
    for d in range(5):
        ok = (u < last_u) & (d <= remain - 1)
        emit.append(jnp.where(ok, label_lp + durs[d], LOW))
        if d:
            blank_raw.append(blank_lp + durs[d])
            blank.append(jnp.where(d <= remain - 1, blank_raw[d], LOW))
    final = (u == target) & (remain <= 4)
    closing = jnp.zeros(wide, F32)
    for d in range(1, 5):
        closing = jnp.where(remain == d, blank_raw[d], closing)
    closing = jnp.where(final, closing, LOW)
    start = jnp.where(first & (u == 0), 0.0, LOW)

    tall = frames + 16
    tall_u = (lane_ids((tall, 128)) // group) * own_u + lane_ids((tall, 128)) % own_u
    tall_j = lane_ids((tall, 128)) % own_u
    pad = jnp.full((16, 128), LOW, F32)

    def skew(value):
        value = jnp.concatenate([value, pad], axis=0)
        for bit in (1, 2, 4, 8):
            value = jnp.where((tall_u // bit) % 2 == 1, pltpu.roll(value, bit, 0), value)
        return value

    def unskew(value):
        for bit in (1, 2, 4, 8):
            value = jnp.where((tall_u // bit) % 2 == 1, pltpu.roll(value, tall - bit, 0), value)
        return value[:frames]

    up = 128 - (group - own_u + 1)

    def next_up(value, jj):
        return jnp.where(jj == 0, pltpu.roll(value, group - own_u + 1, 1), pltpu.roll(value, 1, 1))

    def next_down(value, jj):
        return jnp.where(jj == own_u - 1, pltpu.roll(value, up, 1), pltpu.roll(value, 127, 1))

    lead = jnp.full((8, 128), LOW, F32)

    def keep(i, value):
        skewed[i, 0:8, :] = lead
        skewed[i, 8 : 8 + tall, :] = value

    for d in range(1, 5):
        keep(d - 1, skew(blank[d]))
    for d in range(5):
        value = skew(emit[d])
        keep(4 + d, value)
        keep(9 + d, next_up(value, tall_j))
    keep(14, skew(start))
    keep(15, skew(closing))
    waves = frames + last_u
    one_j = lane_ids((1, 128)) % own_u
    low_row = skewed[0, 0:1, :]

    def at(i, w):
        return skewed[i, pl.ds(w + 8, 1), :]

    def combine(old, near):
        top_old, sum_old = lse_of(old)
        top = functools.reduce(jnp.maximum, near, top_old)
        total = sum_old * jnp.exp(top_old - top)
        for v in near:
            total = total + jnp.exp(v - top)
        return top + jnp.log(total)

    def wave(i, carry):
        a, ra, b, rb = carry
        old = [at(14, i)]
        for d in range(2, 5):
            old.append(a[d - 1] + at(d - 1, i - d))
        for d in range(2, 6):
            old.append(ra[d - 1] + at(8 + d, i - d))
        new_a = combine(old, [a[0] + at(0, i - 1), ra[0] + at(9, i - 1)])
        back = waves - 1 - i
        old = [at(15, back)]
        for d in range(2, 5):
            old.append(b[d - 1] + at(d - 1, back))
        for d in range(2, 6):
            old.append(rb[d - 1] + at(3 + d, back))
        new_b = combine(old, [b[0] + at(0, back), rb[0] + at(4, back)])
        hist[0, pl.ds(i, 1), :] = new_a
        hist[1, pl.ds(back, 1), :] = new_b
        return (
            (new_a,) + a[:-1],
            (next_up(new_a, one_j),) + ra[:-1],
            (new_b,) + b[:-1],
            (next_down(new_b, one_j),) + rb[:-1],
        )

    hist[...] = jnp.full(hist.shape, LOW, F32)
    lax.fori_loop(
        0, waves, wave, ((low_row,) * 4, (low_row,) * 5, (low_row,) * 4, (low_row,) * 5)
    )
    alpha, beta = unskew(hist[0]), unskew(hist[1])
    ahead = next_down(beta, j)
    norm = jnp.zeros(wide, F32)
    heads = jnp.where(first & (u == 0), beta, 0.0)
    for s in range(segs):
        value = jnp.sum(jnp.where(seg == s, heads, 0.0), axis=0, keepdims=True)
        step = 1
        while step < own_u:
            value = value + pltpu.roll(value, step, 1)
            step *= 2
        step = group
        while step < 128:
            value = value + pltpu.roll(value, step, 1)
            step *= 2
        norm = jnp.where(seg == s, value, norm)
        length = ends[s] - (ends[s - 1] if s else 0)
        loss[pl.ds(s, 1), :] = -value / length[:1].astype(F32)
    base = alpha - norm
    total_a, total_b = None, None
    for d in range(5):
        there = pltpu.roll(ahead, frames - d, 0) if d else ahead
        g = -jnp.exp(base + emit[d] + there)
        total_a = g if d == 0 else total_a + g
        if d:
            gb = -jnp.exp(base + blank[d] + pltpu.roll(beta, frames - d, 0))
            gb = gb - jnp.exp(jnp.where(final & (remain == d), base + blank_raw[d], LOW))
            total_b = gb if d == 1 else total_b + gb
            g = g + gb
        grads[1 + d] = g
    grads[0] = total_b
    grads[6] = total_a


def joint_kernel(
    dims,
    enc_own, pred, lengths, counts, labels, predx, tok, tail, bias,
    g_enc, g_predictor, g_pack, g_mix, g_bias, loss,
    enc_all, proj, hid, slope, prob, prob_tail, mine, terms, skewed, hist, grads, g_pred, part, came,
    send, recv,
):
    frames, rows, segs, own_u, labs = dims
    micro = rows // labs
    peers = Peers()
    barrier = pltpu.get_barrier_semaphore()
    for j in range(1, labs):
        pl.semaphore_signal(barrier, inc=1, device_id=peers.device(j), device_id_type=MESH)
    pl.semaphore_wait(barrier, labs - 1)
    width = enc_own.shape[-1]
    span = own_u * frames
    own_rows = pl.ds(peers.lab * micro, micro)

    def enc_copy(j, source):
        return remote(enc_own, enc_all.at[pl.ds(source * micro, micro)], send.at[0, j], recv.at[0, j], peers.device(j))

    for j in range(1, labs):
        enc_copy(j, peers.lab).start()
    enc_all[own_rows] = enc_own[...]
    proj[...] = mm_t(pred[...], predx[...])
    lane_t = lane_ids((frames, 128))
    lane_w = lane_ids((frames, TOK))
    group = rows * own_u
    per_vreg = 128 // group

    def row_of(k):
        return peers.owner(k // micro) * micro + k % micro

    def forward(k, _):
        for j in range(1, labs):
            @pl.when(k == j * micro)
            def _():
                enc_copy(j, peers.owner(j)).wait_recv()
        r = row_of(k)
        seg = seg_of(row_ids((frames, width)), scalar_ends(lengths, r, segs))
        enc = enc_all[r].astype(F32)
        for u in range(own_u):
            per_frame = pick(
                seg, [proj[pl.ds(r * segs * own_u + s * own_u + u, 1), :] for s in range(segs)]
            )
            value = jnp.tanh(enc + per_frame)
            hid[r, u * frames : (u + 1) * frames, :] = value.astype(BF)
            slope[r, u * frames : (u + 1) * frames, :] = (1.0 - value * value).astype(BF)
        h = hid[r]
        end = mm(h, tail[...]) + bias[:, TOK:]
        wide = mm(h, tok[...]) + bias[:, :TOK]
        seg_l = seg_of(row_ids((frames, TOK)), scalar_ends(lengths, r, segs))
        for u in range(own_u):
            logit, last = wide[u * frames : (u + 1) * frames], end[u * frames : (u + 1) * frames]
            top = jnp.maximum(jnp.max(logit, axis=1, keepdims=True), last[:, 0:1])
            top_dur = jnp.max(
                jnp.where((lane_t >= 1) & (lane_t <= 5), last, -jnp.inf), axis=1, keepdims=True
            )
            is_tok = lane_t == 0
            e_last = jnp.where(
                lane_t < 6, jnp.exp(jnp.where(lane_t < 6, last - jnp.where(is_tok, top, top_dur), 0.0)), 0.0
            )
            e = jnp.exp(logit - top)
            total = jnp.sum(e, axis=1, keepdims=True) + e_last[:, 0:1]
            total_dur = jnp.sum(jnp.where(is_tok, 0.0, e_last), axis=1, keepdims=True)
            prob[r, u * frames : (u + 1) * frames, :] = (e * (1.0 / total)).astype(BF)
            prob_tail[r, u * frames : (u + 1) * frames, :] = e_last * (1.0 / jnp.where(is_tok, total, total_dur))
            norm_tok, norm_dur = top + jnp.log(total), top_dur + jnp.log(total_dur)
            label = pick(seg_l, [labels[r, s * own_u + u] for s in range(segs)])
            at_label = jnp.sum(jnp.where(lane_w == label, logit, 0.0), axis=1, keepdims=True) - norm_tok
            lp = last - jnp.where(is_tok, norm_tok, norm_dur)
            for kind in range(KINDS):
                column = at_label if kind == 6 else lp[:, kind : kind + 1]
                cols = slice((kind // per_vreg) * 128, (kind // per_vreg) * 128 + 128)
                place = (kind % per_vreg) * group + r * own_u + u
                mine[:, cols] = jnp.where(lane_t == place, column, mine[:, cols])
        return 0

    mine[...] = jnp.zeros(mine.shape, F32)
    lax.fori_loop(0, rows, forward, 0)
    terms[peers.lab] = mine[...]

    def term_copy(j, source):
        return remote(mine, terms.at[source], send.at[1, j], recv.at[1, j], peers.device(j))

    for j in range(1, labs):
        term_copy(j, peers.lab).start()
    for j in range(1, labs):
        term_copy(j, peers.owner(j)).wait_recv()
    lattice(peers, lengths, counts, terms, skewed, hist, grads, loss, dims)

    def part_copy(j):
        return remote(part.at[j], came.at[j], send.at[2, j], recv.at[2, j], peers.device(j))

    def backward(i, sums):
        k = rows - 1 - i
        r = row_of(k)
        shift = (256 - peers.lab * group - r * own_u) % 128
        rolled = [pltpu.roll(grads[kind], shift, 1) for kind in range(KINDS)]
        seg_l = seg_of(row_ids((frames, TOK)), scalar_ends(lengths, r, segs))
        sum_tok, sum_tail = sums
        for u in range(own_u):
            at = slice(u * frames, (u + 1) * frames)
            a, b = rolled[6][:, u : u + 1], rolled[0][:, u : u + 1]
            both = a + b
            label = pick(seg_l, [labels[r, s * own_u + u] for s in range(segs)])
            g = (jnp.where(lane_w == label, a, 0.0) - prob[r, at, :].astype(F32) * both).astype(BF)
            prob[r, at, :] = g
            aim = jnp.zeros((frames, 128), F32)
            for kind in range(6):
                aim = jnp.where(lane_t == kind, rolled[kind][:, u : u + 1], aim)
            gt = (aim - prob_tail[r, at, :] * both).astype(BF)
            prob_tail[r, at, :] = gt.astype(F32)
            sum_tok = sum_tok + jnp.sum(g.astype(F32).reshape(frames // 8, 8, TOK), axis=0)
            sum_tail = sum_tail + jnp.sum(gt.astype(F32).reshape(frames // 8, 8, 128), axis=0)
        back = mm_t(prob[r], tok[...]) + mm_t(prob_tail[r].astype(BF), tail[...])
        back = back * slope[r].astype(F32)
        summed = back[:frames]
        for u in range(1, own_u):
            summed = summed + back[u * frames : (u + 1) * frames]
        part[k // micro, k % micro] = summed.astype(BF)
        shape = (segs * own_u, span)
        lanes = lane_ids(shape)
        seg_t = seg_of(lanes % frames, scalar_ends(lengths, r, segs))
        hit = (row_ids(shape) == seg_t * own_u + lanes // frames).astype(BF)
        g_pred[pl.ds(r * segs * own_u, segs * own_u), :] = mm(hit, back.astype(BF)).astype(BF)
        for j in range(1, labs):
            @pl.when(k == j * micro)
            def _():
                part_copy(j).start()
        return sum_tok, sum_tail

    zero = (jnp.zeros((8, TOK), F32), jnp.zeros((8, 128), F32))
    sum_tok, sum_tail = lax.fori_loop(0, rows, backward, zero)
    sum_tok = jnp.sum(sum_tok, axis=0, keepdims=True).astype(BF)
    sum_tail = jnp.sum(sum_tail, axis=0, keepdims=True).astype(BF)
    g_bias[...] = jnp.zeros(g_bias.shape, F32)
    for i in range(4):
        g_bias[i : i + 1, :] = sum_tok[:, 256 * i : 256 * i + 256].astype(F32)
    g_bias[4:5, :128] = sum_tail.astype(F32)
    gp = g_pred[...]
    g_predictor[...] = mm(gp, predx[:, : g_predictor.shape[1]])
    shards = lax.axis_size("dp")
    block = width // shards
    h_all = hid[...].reshape(rows * span, width)
    from_pred = t_mm(gp, pred[...])
    for i in range(2):
        piece = t_mm(h_all, prob[:, :, i * 512 : i * 512 + 512].reshape(rows * span, 512)).astype(BF)
        for d in range(shards):
            g_pack[d * 3 * block + (i + 1) * block : d * 3 * block + (i + 2) * block, :] = piece[d * block : (d + 1) * block]
    ends_w = t_mm(h_all, prob_tail[...].reshape(rows * span, 128).astype(BF)) + from_pred[:, 640:768]
    for d in range(shards):
        at = slice(d * block, (d + 1) * block)
        g_pack[d * 3 * block : d * 3 * block + block, :] = from_pred[at, :512].astype(BF)
        g_mix[at, :128] = from_pred[at, 512:640].astype(BF)
        g_mix[at, 128:] = ends_w[at].astype(BF)
    for j in range(1, labs):
        part_copy(j).wait_recv()
    total = part[0].astype(F32)
    for j in range(1, labs):
        total = total + came[j].astype(F32)
    g_enc[...] = total.astype(BF)
    for j in range(1, labs):
        enc_copy(j, peers.lab).wait_send()
        term_copy(j, peers.lab).wait_send()
        part_copy(j).wait_send()


def joint_call(enc_own, pred, lengths, counts, labels, predx, tok, tail, bias, dims):
    frames, rows, segs, own_u, labs = dims
    width = enc_own.shape[-1]
    span = own_u * frames
    micro = rows // labs
    vm = pl.BlockSpec(memory_space=pltpu.VMEM)
    sm = pl.BlockSpec(memory_space=pltpu.SMEM)
    return pl.pallas_call(
        functools.partial(joint_kernel, dims),
        out_shape=[
            jax.ShapeDtypeStruct((micro, frames, width), BF),
            jax.ShapeDtypeStruct((rows * segs * own_u, 640), F32),
            jax.ShapeDtypeStruct((3 * width, 512), BF),
            jax.ShapeDtypeStruct((width, 256), BF),
            jax.ShapeDtypeStruct((16, 256), F32),
            jax.ShapeDtypeStruct((8, 128), F32),
        ],
        in_specs=[vm, vm, sm, sm, sm, vm, vm, vm, vm],
        out_specs=[vm] * 6,
        scratch_shapes=[
            pltpu.VMEM((rows, frames, width), BF),
            pltpu.VMEM((rows * segs * own_u, width), F32),
            pltpu.VMEM((rows, span, width), BF),
            pltpu.VMEM((rows, span, width), BF),
            pltpu.VMEM((rows, span, TOK), BF),
            pltpu.VMEM((rows, span, 128), F32),
            pltpu.VMEM((frames, 256), F32),
            pltpu.VMEM((labs, frames, 256), F32),
            pltpu.VMEM((16, frames + 24, 128), F32),
            pltpu.VMEM((2, frames + 16, 128), F32),
            pltpu.VMEM((KINDS, frames, 128), F32),
            pltpu.VMEM((rows * segs * own_u, width), BF),
            pltpu.VMEM((labs, micro, frames, width), BF),
            pltpu.VMEM((labs, micro, frames, width), BF),
            pltpu.SemaphoreType.DMA((3, labs)),
            pltpu.SemaphoreType.DMA((3, labs)),
        ],
        compiler_params=pltpu.CompilerParams(
            collective_id=2, has_side_effects=True, vmem_limit_bytes=60 * 2**20
        ),
    )(enc_own, pred, lengths, counts, labels, predx, tok, tail, bias)


HEADS = 8
HD = 64
H = 8
epsilon = 1e-05
very_low = -100000.0


def product(first_op, second_op):
    return jnp.dot(first_op, second_op, preferred_element_type=jnp.float32)


def contract_rows(first_op, second_op):
    return lax.dot_general(
        first_op, second_op, (((0,), (0,)), ((), ())), preferred_element_type=jnp.float32
    )


def against(first_op, second_op):
    return lax.dot_general(
        first_op, second_op, (((1,), (1,)), ((), ())), preferred_element_type=jnp.float32
    )


def layer_norm(inputs, gain_vec):
    centre = inputs - jnp.mean(inputs, axis=-1, keepdims=True)
    spread = jnp.mean(centre * centre, axis=-1, keepdims=True)
    return centre * lax.rsqrt(spread + epsilon) * gain_vec


def segments(lengths, frames):
    seg_ends = jnp.cumsum(lengths, axis=-1)
    starts = seg_ends - lengths
    position = jnp.arange(frames, dtype=jnp.int32)
    passed = position[:, None] >= seg_ends[..., None, :]
    seg_index = jnp.sum(passed.astype(jnp.int32), axis=-1)
    member = seg_index[..., None] == jnp.arange(lengths.shape[-1], dtype=jnp.int32)
    seg_start = jnp.sum(jnp.where(member, starts[..., None, :], 0), axis=-1)
    seg_stop = jnp.sum(jnp.where(member, seg_ends[..., None, :], 0), axis=-1)
    return (seg_index, member, position - seg_start, seg_stop - position)


def conv_piece(conv_pre, w_depth, gain_depth, seg_index):
    width_in = w_depth.shape[1]
    frames = conv_pre.shape[0]
    half_taps = w_depth.shape[0] // 2
    gated = conv_pre[:, :width_in] * jax.nn.sigmoid(conv_pre[:, width_in:])
    padded = jnp.pad(gated, ((half_taps, half_taps), (0, 0)))
    seg_pad = jnp.pad(seg_index, (half_taps, half_taps), constant_values=-1)
    summed = jnp.zeros_like(gated)
    for tap_index in range(w_depth.shape[0]):
        same_seg = (seg_pad[tap_index : tap_index + frames] == seg_index).astype(gated.dtype)
        summed = (
            summed + w_depth[tap_index] * padded[tap_index : tap_index + frames] * same_seg[:, None]
        )
    return jax.nn.silu(layer_norm(summed, gain_depth))


def attend_scores(queries, keys, same_seg, score_scale):
    raw = (
        jnp.einsum("thd,shd->hts", queries, keys, preferred_element_type=jnp.float32) * score_scale
    )
    return jnp.where(same_seg[None], raw, very_low)


def block_forward(frames_bf, seg_index, all_weights):
    (
        gain_ffn,
        w_ffn_in,
        w_ffn_out,
        gain_att,
        w_qkv,
        w_att_out,
        gain_conv,
        w_point_in,
        w_depth,
        gain_depth,
        w_point_out,
        gain_out,
        w_enc,
    ) = all_weights[:13]
    frames = frames_bf.shape[0]
    inputs = frames_bf.astype(jnp.float32)
    normed, norm_back_one = jax.vjp(layer_norm, inputs, gain_ffn.astype(jnp.float32))
    ffn_in = normed.astype(jnp.bfloat16)
    ffn_pre = product(ffn_in, w_ffn_in)
    ffn_act = jax.nn.silu(ffn_pre).astype(jnp.bfloat16)
    after_ffn = inputs + 0.5 * product(ffn_act, w_ffn_out)
    normed, norm_back_two = jax.vjp(layer_norm, after_ffn, gain_att.astype(jnp.float32))
    att_in = normed.astype(jnp.bfloat16)
    qkv_all = product(att_in, w_qkv).astype(jnp.bfloat16).reshape(frames, 3, H, HD)
    queries, keys, values = (qkv_all[:, 0], qkv_all[:, 1], qkv_all[:, 2])
    same_seg = seg_index[:, None] == seg_index[None, :]
    scores = attend_scores(queries, keys, same_seg, HD ** (-0.5))
    largest = jnp.max(scores, axis=-1, keepdims=True)
    weights = jnp.exp(scores - largest)
    totals = jnp.sum(weights, axis=-1, keepdims=True)
    norm_log = largest + jnp.log(totals)
    probs = (weights / totals).astype(jnp.bfloat16)
    context = (
        jnp.einsum("hts,shd->thd", probs, values, preferred_element_type=jnp.float32)
        .astype(jnp.bfloat16)
        .reshape(frames, H * HD)
    )
    after_att = after_ffn + product(context, w_att_out)
    normed, norm_back_three = jax.vjp(layer_norm, after_att, gain_conv.astype(jnp.float32))
    conv_in = normed.astype(jnp.bfloat16)
    conv_pre = product(conv_in, w_point_in)
    conv_out, conv_back = jax.vjp(
        functools.partial(conv_piece, seg_index=seg_index),
        conv_pre,
        w_depth.astype(jnp.float32),
        gain_depth.astype(jnp.float32),
    )
    conv_act = conv_out.astype(jnp.bfloat16)
    after_conv = after_att + product(conv_act, w_point_out)
    encoded, norm_back_four = jax.vjp(layer_norm, after_conv, gain_out.astype(jnp.float32))
    enc_in = encoded.astype(jnp.bfloat16)
    enc_proj = product(enc_in, w_enc).astype(jnp.bfloat16)
    kept_state = (
        ffn_in,
        ffn_pre,
        ffn_act,
        att_in,
        queries,
        keys,
        values,
        same_seg,
        norm_log,
        context,
        conv_in,
        conv_act,
        enc_in,
        norm_back_one,
        norm_back_two,
        norm_back_three,
        norm_back_four,
        conv_back,
    )
    return (enc_in, enc_proj, kept_state)


def block_backward(enc_grad, kept_state, all_weights):
    w_ffn_in, w_ffn_out, w_qkv, w_att_out, w_point_in, w_point_out, w_enc = (
        all_weights[1],
        all_weights[2],
        all_weights[4],
        all_weights[5],
        all_weights[7],
        all_weights[10],
        all_weights[12],
    )
    (
        ffn_in,
        ffn_pre,
        ffn_act,
        att_in,
        queries,
        keys,
        values,
        same_seg,
        norm_log,
        context,
        conv_in,
        conv_act,
        enc_in,
        norm_back_one,
        norm_back_two,
        norm_back_three,
        norm_back_four,
        conv_back,
    ) = kept_state
    frames = ffn_in.shape[0]
    score_scale = HD ** (-0.5)
    grad_enc_w = contract_rows(enc_in, enc_grad)
    grad_conv_sum, grad_gain_out = norm_back_four(against(enc_grad, w_enc))
    branch = grad_conv_sum.astype(jnp.bfloat16)
    grad_point_out = contract_rows(conv_act, branch)
    grad_pre, grad_depth, grad_gain_depth = conv_back(against(branch, w_point_out))
    grad_pre_low = grad_pre.astype(jnp.bfloat16)
    grad_point_in = contract_rows(conv_in, grad_pre_low)
    grad_normed, grad_gain_conv = norm_back_three(against(grad_pre_low, w_point_in))
    grad_att_sum = grad_conv_sum + grad_normed
    branch = grad_att_sum.astype(jnp.bfloat16)
    grad_att_out = contract_rows(context, branch)
    grad_context = against(branch, w_att_out).astype(jnp.bfloat16).reshape(frames, H, HD)
    scores = attend_scores(queries, keys, same_seg, score_scale)
    probs = jnp.exp(scores - norm_log)
    grad_probs = jnp.einsum(
        "thd,shd->hts", grad_context, values, preferred_element_type=jnp.float32
    )
    grad_values = jnp.einsum(
        "hts,thd->shd", probs.astype(jnp.bfloat16), grad_context, preferred_element_type=jnp.float32
    )
    grad_scores = (
        probs * (grad_probs - jnp.sum(grad_probs * probs, axis=-1, keepdims=True))
    ).astype(jnp.bfloat16)
    grad_queries = (
        jnp.einsum("hts,shd->thd", grad_scores, keys, preferred_element_type=jnp.float32)
        * score_scale
    )
    grad_keys = (
        jnp.einsum("hts,thd->shd", grad_scores, queries, preferred_element_type=jnp.float32)
        * score_scale
    )
    grad_qkv_all = (
        jnp.stack([grad_queries, grad_keys, grad_values], axis=1)
        .astype(jnp.bfloat16)
        .reshape(frames, 3 * H * HD)
    )
    grad_w_qkv = contract_rows(att_in, grad_qkv_all)
    grad_normed, grad_gain_att = norm_back_two(against(grad_qkv_all, w_qkv))
    grad_ffn_sum = grad_att_sum + grad_normed
    branch = (0.5 * grad_ffn_sum).astype(jnp.bfloat16)
    grad_ffn_out = contract_rows(ffn_act, branch)
    grad_act = against(branch, w_ffn_out)
    grad_pre = jax.vjp(jax.nn.silu, ffn_pre)[1](grad_act)[0]
    grad_pre_low = grad_pre.astype(jnp.bfloat16)
    grad_ffn_in = contract_rows(ffn_in, grad_pre_low)
    grad_normed, grad_gain_ffn = norm_back_one(against(grad_pre_low, w_ffn_in))
    grad_inputs = grad_ffn_sum + grad_normed
    return (
        grad_inputs,
        (
            grad_gain_ffn,
            grad_ffn_in,
            grad_ffn_out,
            grad_gain_att,
            grad_w_qkv,
            grad_att_out,
            grad_gain_conv,
            grad_point_in,
            grad_depth,
            grad_gain_depth,
            grad_point_out,
            grad_gain_out,
            grad_enc_w,
        ),
    )


def pad_rows(value, rows):
    return jnp.pad(value, ((0, rows - value.shape[0]), (0, 0)))


def pad_lanes(value, lanes):
    return jnp.pad(value, ((0, 0), (0, lanes - value.shape[1])))


def pick_rows(gathered, n, first, rows):
    per = gathered.shape[0] // n
    return gathered.reshape(n, per, -1)[:, first : first + rows].reshape(n * rows, -1)


def local(
    frames_in, predictor, seg_lengths, label_counts, label_ids, gain_ffn, w_ffn_in, w_ffn_out, gain_att, w_qkv,
    w_att_out, gain_conv, w_point_in, w_depth, gain_depth, w_point_out, gain_out, w_enc, w_pred, bias_joint,
    w_joint_out, bias_out,
):
    n, labs = lax.axis_size("dp"), lax.axis_size("lab")
    micro, frames, model = frames_in.shape
    rows, segs, own_u, joint = predictor.shape
    ds, js = model // n, w_pred.shape[1]
    jr = -(-js // TILE) * TILE
    ff, qk, pi = w_ffn_in.shape[1], w_qkv.shape[1], w_point_in.shape[1]
    pred_t = pad_rows(w_pred.T, jr)
    tail = jnp.concatenate([w_joint_out[:, TOK:], bias_joint[:, None]], axis=1)
    small = jnp.concatenate(
        [pad_lanes(w_depth.T, 128), pad_lanes(jnp.stack([gain_ffn, gain_att, gain_conv, gain_depth, gain_out], 1), 128)],
        axis=1,
    )
    mix = jnp.concatenate(
        [pred_t[:, 512:], pad_rows(pad_lanes(tail, 128), jr), pad_rows(small, jr)], axis=1
    )
    shards = [
        jnp.concatenate([mix, w_ffn_in.T], 0),
        jnp.concatenate([w_ffn_out, w_qkv.T], 0),
        jnp.concatenate([w_att_out, w_point_in.T, w_point_out, pad_rows(w_enc.T, jr)], 0),
        jnp.concatenate(
            [pred_t[:, :512], pad_rows(w_joint_out[:, :512], jr), pad_rows(w_joint_out[:, 512:TOK], jr)], 0
        ),
    ]
    full = gather_all(n, shards)
    mixes = pick_rows(full[0], n, 0, jr)
    smalls = mixes.reshape(n, jr, 512)[:, :ds, 256:].reshape(model, 256)
    gains = smalls[:, 128:133].T
    weights = (
        gains[0], pick_rows(full[0], n, jr, ff).T, pick_rows(full[1], n, 0, ff), gains[1],
        pick_rows(full[1], n, ff, qk).T, pick_rows(full[2], n, 0, ds), gains[2], pick_rows(full[2], n, ds, pi).T,
        smalls[:, :9].T, gains[3], pick_rows(full[2], n, ds + pi, ds), gains[4],
        pick_rows(full[2], n, 2 * ds + pi, jr).T,
    )
    predx = jnp.concatenate([pick_rows(full[3], n, 0, jr), mixes[:, :256]], axis=1)
    tok = jnp.concatenate([pick_rows(full[3], n, jr, jr), pick_rows(full[3], n, 2 * jr, jr)], axis=1)
    tail_w = mixes[:, 128:256]
    lab = lax.axis_index("lab")
    own_lengths = lax.dynamic_slice_in_dim(seg_lengths, lab * micro, micro)
    seg_index = segments(own_lengths, frames)[0]
    enc_low, enc_proj, kept = jax.vmap(functools.partial(block_forward, all_weights=weights))(frames_in, seg_index)
    pred_ext = pad_lanes(predictor.reshape(-1, joint), 768)
    pred_ext = jnp.where(lax.broadcasted_iota(jnp.int32, pred_ext.shape, 1) == joint + BIAS_LANE, 1.0, pred_ext).astype(BF)
    bias = jnp.pad(bias_out.astype(F32), (0, TOK + 128 - bias_out.shape[0]))[None]
    dims = (frames, rows, segs, own_u, labs)
    g_enc, g_predictor, g_pack, g_mix, g_bias, loss = joint_call(
        enc_proj, pred_ext, seg_lengths, label_counts, label_ids.reshape(rows, -1), predx, tok, tail_w, bias, dims
    )
    grad_frames, block = jax.vmap(functools.partial(block_backward, all_weights=weights))(g_enc, kept)
    block = [jnp.sum(g, axis=0).astype(BF) for g in block]
    (gg_ffn, g_in, g_out, gg_att, g_qkv, g_att, gg_conv, g_pin, g_depth, gg_depth, g_pout, gg_out, g_encw) = block

    def by(value, rows_each):
        return value.reshape(n, rows_each, -1)

    small = jnp.concatenate(
        [pad_lanes(g_depth.T, 128), pad_lanes(jnp.stack([gg_ffn, gg_att, gg_conv, gg_depth, gg_out], 1), 128)], axis=1
    ).reshape(n, ds, 256)
    biases = jnp.broadcast_to(g_bias[None, : jr - ds].astype(BF), (n, min(16, jr - ds), 256))
    small = jnp.concatenate([small, biases, jnp.zeros((n, jr - ds - biases.shape[1], 256), BF)], axis=1)
    mix = jnp.concatenate([by(g_mix, jr), small], axis=2)
    packs = [
        g_pack,
        jnp.concatenate([by(g_att, ds), by(g_pin.T, pi), by(g_pout, ds), by(g_encw.T, jr)], 1).reshape(-1, 512),
        jnp.concatenate([by(g_out, ff), by(g_qkv.T, qk)], 1).reshape(-1, 512),
        jnp.concatenate([mix, by(g_in.T, ff)], 1).reshape(-1, 512),
    ]
    own = [g.astype(F32) for g in scatter_all(n, packs)]
    mix, small = own[3][:jr], own[3][:ds, 256:]
    g_pred_t = jnp.concatenate([own[0][:js], mix[:js, :128]], axis=1)
    g_joint = jnp.concatenate([own[0][jr : jr + js], own[0][2 * jr : 2 * jr + js], mix[:js, 128:134]], axis=1)
    g_bias_out = jnp.concatenate([mix[ds : ds + 4, 256:].reshape(-1), mix[ds + 4, 256:262]])
    loss_out = loss[:segs, : rows * own_u : own_u].T
    return (
        loss_out, enc_low, grad_frames, g_predictor.reshape(predictor.shape),
        small[:, 128], own[3][jr:].T, own[2][:ff], small[:, 129], own[2][ff:].T, own[1][:ds], small[:, 130],
        own[1][ds : ds + pi].T, small[:, :9].T, small[:, 131], own[1][ds + pi : 2 * ds + pi], small[:, 132],
        own[1][2 * ds + pi : 2 * ds + pi + js].T, g_pred_t.T, mix[:js, 128 + BIAS_LANE], g_joint, g_bias_out,
    )


def solution(mesh):
    rows, whole = P(("dp", "lab"), None, None), P()
    predictor, columns, lines, vector = P("dp", None, "lab", None), P(None, "dp"), P("dp", None), P("dp")
    params = (
        vector, columns, lines, vector, columns, lines, vector, columns, columns, vector, lines, vector, columns,
        columns, vector, lines, whole,
    )
    return jax.shard_map(
        local,
        mesh=mesh,
        in_specs=(rows, predictor, lines, lines, P("dp", None, "lab")) + params,
        out_specs=(lines, rows, rows, predictor) + params,
        check_vma=False,
    )
```

profile of v0, /device:TPU:0, one launch (start us, length us, event | category | flops | bytes accessed | tf_op | source)
XLA Modules:
  0.0 305.7 jit_solution(2575198015000242413)
XLA Ops:
  0.7 1.1 convert_reduce_fusion
  1.8 1.1 fusion.35
  4.7 1.3 copy.192.counts
  6.0 1.3 copy.193.labels
  7.4 1.3 copy.191.lengths
  11.5 0.8 copy.181
  14.6 0.9 slice.330
  15.5 1.0 copy.184
  16.6 1.0 reshape.470
  18.2 0.9 fusion.82
  20.1 0.9 fusion.29
  21.0 0.8 pad_maximum_fusion.5.refs_1_
  21.8 58.3 %shard_map.373 = (bf16[2688,512]{1,0:T(8,128)(2,1)}, bf16[3584,512]{1,0:T(8,128)(2,1)}, bf16[2688,512]{1,0:T(8,128)(2,1)}, bf16[1920,512]{1,0:T(8,128)(2,1)}) custom-call(bf16[336,512]{1,0:T(8,128)(2,1)} %get-tuple-element.251.refs_0_, bf16[448,512]{1,0:T(8,128)(2,1)} %pad_maximum_fusion.5.refs_1_, bf16[336,512]{1,0:T(8,128)(2,1)} %get-tuple-element.252.refs_2_, ...), custom_call_target="tpu_custom_call" | custom-call | tf_op jit(solution)/shard_map/pallas_call | solution.py:203
  80.0 1.1 slice.331
  81.2 0.9 convert_reduce_fusion.1
  82.1 1.8 slice_reduce_fusion.8
  85.8 0.9 slice.359
  86.8 0.8 fusion.54
  87.7 1.1 fusion.77
  88.8 1.6 copy-done.13
  91.3 0.9 copy-done.21
  93.6 1.4 convolution_convert_fusion
  95.0 2.3 reshape.465
  97.3 2.0 fusion.79
  99.3 1.2 copy.225
  100.5 1.4 fusion.84
  102.5 1.5 fusion.85
  108.5 1.0 convolution_convert_fusion.2.enc_own
  109.7 1.2 pad_maximum_fusion.3.tok
  110.9 1.0 pad_maximum_fusion.4.predx
  111.9 47.6 %shard_map.374 = (bf16[2,64,640]{2,1,0:T(8,128)(2,1)}, f32[128,640]{1,0:T(8,128)}, bf16[1920,512]{1,0:T(8,128)(2,1)}, bf16[640,256]{1,0:T(8,128)(2,1)}, f32[16,256]{1,0:T(8,128)}, /*index=5*/f32[8,128]{1,0:T(8,128)}) custom-call(bf16[2,64,640]{2,1,0:T(8,128)(2,1)} %convolution_convert_fusion.2.enc_own, bf16[128,768]{1,0:T(8,128)(2,1)} %pad_select_fusion.pred, ...), custom_call_target="tpu_custom_call" | custom-call | tf_op jit(solution)/shard_map/pallas_call | solution.py:792
  159.6 2.1 multiply_reduce_fusion.1
  161.9 2.2 multiply_reduce_fusion.16
  164.7 1.3 slice.307
  166.0 1.3 convert_element_type.354
  167.3 1.3 multiply_reduce_fusion.2
  169.1 3.8 %multiply_reduce_fusion.13 = (f32[2,512]{1,0:T(2,128)S(1)}, f32[2,512]{1,0:T(2,128)S(1)}, f32[2,512]{1,0:T(2,128)S(1)}, f32[2,512]{1,0:T(2,128)S(1)}, f32[2,512]...) fusion(f32[2,64,512]{2,1,0:T(8,128)} %copy-done.16, ...), kind=kLoop, calls=%fused_computation.147 | loop fusion | flops 2153472 | bytes 1093632 | tf_op jit(solution)/shard_map/vmap(transpose(jvp()))/reduce_sum | solution.py:880
  173.6 1.3 convert_element_type.355
  174.9 2.3 fusion.2
  177.2 1.8 reshape.479
  179.0 1.5 pad.146.clone
  180.5 2.2 fusion.1
  182.8 1.2 multiply_multiply_fusion.7
  186.1 1.0 convolution_convert_fusion.3
  187.1 1.1 copy.228
  188.2 2.6 bitcast_convert_fusion.2
  192.3 1.4 copy.205
  193.7 2.0 convert_element_type.334
  195.7 2.0 multiply_reduce_fusion.4
  198.7 0.9 fusion.11
  202.0 1.8 add_add_fusion.5
  203.8 1.3 fusion.3
  205.2 3.2 %pad_maximum_fusion.1 = bf16[8,336,512]{2,1,0:T(8,128)(2,1)} fusion(bf16[8,80,512]{2,1,0:T(8,128)(2,1)S(1)} %bitcast.215, bf16[8,64,512]{2,1,0:T(8,128)(2,1)} %bitcast.235, bf16[8,128,512]{2,1,0:T(8,128)(2,1)S(1)} %bitcast.203, bf16[8,64,512]{2,1,0:T(8,128)(2,1)S(1)} %bitcast.223), kind=kLoop, calls=%fused_computation.5 | loop fusion | flops 11010048 | bytes 5505024 | tf_op jit(solution)/shard_map/concatenate | solution.py:1148
  209.1 2.0 bitcast_convert_fusion.1
  211.1 2.1 pad_maximum_fusion
  213.3 0.8 bitcast_convert_fusion
  214.3 2.2 pad_maximum_fusion.2
  216.6 76.2 %shard_map.375 = (bf16[240,512]{1,0:T(8,128)(2,1)}, bf16[336,512]{1,0:T(8,128)(2,1)}, bf16[448,512]{1,0:T(8,128)(2,1)}, bf16[336,512]{1,0:T(8,128)(2,1)}) custom-call(bf16[1920,512]{1,0:T(8,128)(2,1)} %get-tuple-element.42.refs_0_, bf16[2688,512]{1,0:T(8,128)(2,1)} %bitcast.195, bf16[3584,512]{1,0:T(8,128)(2,1)} %bitcast.192, bf16[2688,512]{1,0:T(8,128)(2,1)} %bitcast.196), custom_call_target="tpu_custom_call" | custom-call | tf_op jit(solution)/shard_map/pallas_call | solution.py:380
  292.8 0.8 slice.384
  294.3 1.0 fusion.81
  296.8 1.6 fusion.80
  301.3 1.0 copy.208
  303.1 0.8 copy.209
  303.9 0.9 slice.368
  (297 shorter events, 33.9 us)
Async XLA Ops:
  0.7 19.4 %copy-start.46 = (bf16[512,80]{0,1:T(8,128)(2,1)S(1)}, bf16[512,80]{0,1:T(8,128)(2,1)}, u32[]{:S(2)}) copy-start(bf16[512,80]{0,1:T(8,128)(2,1)} %param.39) | copy-start | bytes 245764
  0.7 19.4 %copy-start.48 = (bf16[64,512]{1,0:T(8,128)(2,1)S(1)}, bf16[64,512]{1,0:T(8,128)(2,1)}, u32[]{:S(2)}) copy-start(bf16[64,512]{1,0:T(8,128)(2,1)} %param.37) | copy-start | bytes 196612
  0.7 19.4 %copy-start.49 = (bf16[64,512]{1,0:T(8,128)(2,1)S(1)}, bf16[64,512]{1,0:T(8,128)(2,1)}, u32[]{:S(2)}) copy-start(bf16[64,512]{1,0:T(8,128)(2,1)} %param.32) | copy-start | bytes 196612
  0.7 20.3 %copy-start.45 = (bf16[512,192]{0,1:T(8,128)(2,1)S(1)}, bf16[512,192]{0,1:T(8,128)(2,1)}, u32[]{:S(2)}) copy-start(bf16[512,192]{0,1:T(8,128)(2,1)} %param.31) | copy-start | bytes 589828
  0.7 20.3 %copy-start.43 = (bf16[256,512]{1,0:T(8,128)(2,1)S(1)}, bf16[256,512]{1,0:T(8,128)(2,1)}, u32[]{:S(2)}) copy-start(bf16[256,512]{1,0:T(8,128)(2,1)} %param.29) | copy-start | bytes 786436
  0.7 19.2 %copy-start.44 = (bf16[512,256]{1,0:T(8,128)(2,1)S(1)}, bf16[512,256]{1,0:T(8,128)(2,1)}, u32[]{:S(2)}) copy-start(bf16[512,256]{1,0:T(8,128)(2,1)} %param.28) | copy-start | bytes 786436
  1.8 85.0 %copy-start.54 = (f32[2,64]{1,0:T(2,128)}, f32[2,64]{1,0:T(2,128)S(1)}, u32[]{:S(2)}) copy-start(f32[2,64]{1,0:T(2,128)S(1)} %broadcast_multiply_fusion.5) | copy-start | bytes 1540
  2.9 4.5 %copy-start.86 = (f32[2,64]{1,0:T(2,128)}, f32[2,64]{1,0:T(2,128)S(1)}, u32[]{:S(2)}) copy-start(f32[2,64]{1,0:T(2,128)S(1)} %fusion.35) | copy-start | bytes 1540
  2.9 83.9 %copy-start.61 = (f32[2,64]{1,0:T(2,128)}, f32[2,64]{1,0:T(2,128)S(1)}, u32[]{:S(2)}) copy-start(f32[2,64]{1,0:T(2,128)S(1)} %fusion.65) | copy-start | bytes 1540
  80.0 3.9 %copy-start.14 = (bf16[2688,512]{1,0:T(8,128)(2,1)S(1)}, bf16[2688,512]{1,0:T(8,128)(2,1)}, u32[]{:S(2)}) copy-start(bf16[2688,512]{1,0:T(8,128)(2,1)} %get-tuple-element.35) | copy-start | bytes 8257540
  82.1 10.8 %copy-start.50 = (f32[512]{0:T(512)}, f32[512]{0:T(512)S(1)}, u32[]{:S(2)}) copy-start(f32[512]{0:T(512)S(1)} %get-tuple-element.190) | copy-start | bytes 6148
  84.0 2.8 copy-start.8
  87.6 3.1 %copy-start.35 = (f32[2,64,2048]{2,1,0:T(8,128)}, f32[2,64,2048]{2,1,0:T(8,128)S(1)}, u32[]{:S(2)}) copy-start(f32[2,64,2048]{2,1,0:T(8,128)S(1)} %fusion.54) | copy-start | bytes 3145732
  87.6 2.8 copy-start.13
  90.5 2.4 copy-start
  92.2 7.1 %copy-start.1 = (f32[2,64,512]{2,1,0:T(8,128)}, f32[2,64,512]{2,1,0:T(8,128)S(1)}, u32[]{:S(2)}) copy-start(f32[2,64,512]{2,1,0:T(8,128)S(1)} %get-tuple-element.234) | copy-start | bytes 786436
  92.2 7.1 %copy-start.56 = (f32[2,64]{1,0:T(2,128)}, f32[2,64]{1,0:T(2,128)S(1)}, u32[]{:S(2)}) copy-start(f32[2,64]{1,0:T(2,128)S(1)} %broadcast_multiply_fusion.4) | copy-start | bytes 1540
  102.3 3.8 %copy-start.68 = (f32[512]{0:T(512)S(1)}, f32[512]{0:T(512)}, u32[]{:S(2)}) copy-start(f32[512]{0:T(512)} %get-tuple-element.178) | copy-start | bytes 6148
  102.3 3.8 %copy-start.69 = (f32[512]{0:T(512)S(1)}, f32[512]{0:T(512)}, u32[]{:S(2)}) copy-start(f32[512]{0:T(512)} %get-tuple-element.179) | copy-start | bytes 6148
  102.3 3.8 %copy-start.70 = (f32[512]{0:T(512)S(1)}, f32[512]{0:T(512)}, u32[]{:S(2)}) copy-start(f32[512]{0:T(512)} %get-tuple-element.180) | copy-start | bytes 6148
  102.3 3.8 %copy-start.71 = (f32[512]{0:T(512)S(1)}, f32[512]{0:T(512)}, u32[]{:S(2)}) copy-start(f32[512]{0:T(512)} %get-tuple-element.181) | copy-start | bytes 6148
  102.4 3.8 %copy-start.72 = (f32[512]{0:T(512)S(1)}, f32[512]{0:T(512)}, u32[]{:S(2)}) copy-start(f32[512]{0:T(512)} %get-tuple-element.182) | copy-start | bytes 6148
  102.4 3.8 %copy-start.73 = (f32[512]{0:T(512)S(1)}, f32[512]{0:T(512)}, u32[]{:S(2)}) copy-start(f32[512]{0:T(512)} %get-tuple-element.183) | copy-start | bytes 6148
  102.4 3.8 %copy-start.74 = (f32[512]{0:T(512)S(1)}, f32[512]{0:T(512)}, u32[]{:S(2)}) copy-start(f32[512]{0:T(512)} %get-tuple-element.184) | copy-start | bytes 6148
  102.4 3.8 %copy-start.75 = (f32[512]{0:T(512)S(1)}, f32[512]{0:T(512)}, u32[]{:S(2)}) copy-start(f32[512]{0:T(512)} %get-tuple-element.185) | copy-start | bytes 6148
  102.4 3.8 %copy-start.76 = (f32[512]{0:T(512)S(1)}, f32[512]{0:T(512)}, u32[]{:S(2)}) copy-start(f32[512]{0:T(512)} %get-tuple-element.186) | copy-start | bytes 6148
  102.4 3.8 %copy-start.77 = (f32[2,64]{1,0:T(2,128)S(1)}, f32[2,64]{1,0:T(2,128)}, u32[]{:S(2)}) copy-start(f32[2,64]{1,0:T(2,128)} %get-tuple-element.225) | copy-start | bytes 1540
  102.4 3.8 %copy-start.78 = (f32[2,64]{1,0:T(2,128)S(1)}, f32[2,64]{1,0:T(2,128)}, u32[]{:S(2)}) copy-start(f32[2,64]{1,0:T(2,128)} %get-tuple-element.226) | copy-start | bytes 1540
  102.4 3.8 %copy-start.79 = (f32[2,64]{1,0:T(2,128)S(1)}, f32[2,64]{1,0:T(2,128)}, u32[]{:S(2)}) copy-start(f32[2,64]{1,0:T(2,128)} %get-tuple-element.227) | copy-start | bytes 1540
  102.4 3.8 %copy-start.80 = (f32[2,64]{1,0:T(2,128)S(1)}, f32[2,64]{1,0:T(2,128)}, u32[]{:S(2)}) copy-start(f32[2,64]{1,0:T(2,128)} %get-tuple-element.228) | copy-start | bytes 1540
  102.4 3.8 %copy-start.81 = (f32[2,64]{1,0:T(2,128)S(1)}, f32[2,64]{1,0:T(2,128)}, u32[]{:S(2)}) copy-start(f32[2,64]{1,0:T(2,128)} %get-tuple-element.229) | copy-start | bytes 1540
  102.5 3.8 %copy-start.82 = (f32[2,64]{1,0:T(2,128)S(1)}, f32[2,64]{1,0:T(2,128)}, u32[]{:S(2)}) copy-start(f32[2,64]{1,0:T(2,128)} %get-tuple-element.230) | copy-start | bytes 1540
  102.5 3.8 %copy-start.83 = (f32[2,64]{1,0:T(2,128)S(1)}, f32[2,64]{1,0:T(2,128)}, u32[]{:S(2)}) copy-start(f32[2,64]{1,0:T(2,128)} %get-tuple-element.231) | copy-start | bytes 1540
  102.5 3.8 %copy-start.84 = (f32[2,64]{1,0:T(2,128)S(1)}, f32[2,64]{1,0:T(2,128)}, u32[]{:S(2)}) copy-start(f32[2,64]{1,0:T(2,128)} %get-tuple-element.232) | copy-start | bytes 1540
  102.5 4.6 %copy-start.41 = (bf16[8,64,512]{2,1,0:T(8,128)(2,1)S(1)}, bf16[8,64,512]{2,1,0:T(8,128)(2,1)}, u32[]{:S(2)}) copy-start(bf16[8,64,512]{2,1,0:T(8,128)(2,1)} %get-tuple-element.202) | copy-start | bytes 1572868
  102.5 4.6 %copy-start.67 = (f32[512]{0:T(512)S(1)}, f32[512]{0:T(512)}, u32[]{:S(2)}) copy-start(f32[512]{0:T(512)} %get-tuple-element.188) | copy-start | bytes 6148
  104.8 2.7 copy-start.59
  104.8 2.9 copy-start.58
  104.8 3.7 %copy-start.9 = (bf16[8,80,512]{2,1,0:T(8,128)(2,1)S(1)}, bf16[8,80,512]{2,1,0:T(8,128)(2,1)}, u32[]{:S(2)}) copy-start(bf16[8,80,512]{2,1,0:T(8,128)(2,1)} %slice.359) | copy-start | bytes 1966084
  106.1 3.4 %copy-start.26 = (bf16[1920,512]{1,0:T(8,128)(2,1)S(1)}, bf16[1920,512]{1,0:T(8,128)(2,1)}, u32[]{:S(2)}) copy-start(bf16[1920,512]{1,0:T(8,128)(2,1)} %get-tuple-element.38) | copy-start | bytes 5898244
  106.8 55.1 %copy-start.11 = (f32[2,64,512]{2,1,0:T(8,128)}, f32[2,64,512]{2,1,0:T(8,128)S(1)}, u32[]{:S(2)}) copy-start(f32[2,64,512]{2,1,0:T(8,128)S(1)} %get-tuple-element.200) | copy-start | bytes 786436
  106.8 55.1 %copy-start.85 = (f32[2,64]{1,0:T(2,128)}, f32[2,64]{1,0:T(2,128)S(1)}, u32[]{:S(2)}) copy-start(f32[2,64]{1,0:T(2,128)S(1)} %broadcast_multiply_fusion.2) | copy-start | bytes 1540
  107.1 54.9 %copy-start.92 = (f32[2,64]{1,0:T(2,128)}, f32[2,64]{1,0:T(2,128)S(1)}, u32[]{:S(2)}) copy-start(f32[2,64]{1,0:T(2,128)S(1)} %fusion.68) | copy-start | bytes 1540
  161.9 2.2 copy-start.31
  161.9 2.8 copy-start.94
  179.0 5.1 %copy-start.7 = (f32[2,64,1024]{2,1,0:T(8,128)S(1)}, f32[2,64,1024]{2,1,0:T(8,128)}, u32[]{:S(2)}) copy-start(f32[2,64,1024]{2,1,0:T(8,128)} %copy-done.6) | copy-start | bytes 1572868
  185.1 5.7 %copy-start.5 = (f32[2,8,64,64]{2,3,1,0:T(8,128)S(1)}, f32[2,8,64,64]{2,3,1,0:T(8,128)}, u32[]{:S(2)}) copy-start(f32[2,8,64,64]{2,3,1,0:T(8,128)} %copy-done.4) | copy-start | bytes 786436
  188.2 2.9 copy-start.34
  188.2 3.3 %copy-start.38 = (bf16[2,64,1,8,64]{4,3,2,1,0:T(8,128)(2,1)S(1)}, bf16[2,64,1,8,64]{4,3,2,1,0:T(8,128)(2,1)}, u32[]{:S(2)}) copy-start(bf16[2,64,1,8,64]{4,3,2,1,0:T(8,128)(2,1)} %get-tuple-element.208) | copy-start | bytes 393220
  191.8 3.9 %copy-start.3 = (f32[2,64,512]{2,1,0:T(8,128)S(1)}, f32[2,64,512]{2,1,0:T(8,128)}, u32[]{:S(2)}) copy-start(f32[2,64,512]{2,1,0:T(8,128)} %copy-done.1) | copy-start | bytes 786436
  191.8 3.9 %copy-start.51 = (f32[512]{0:T(512)S(1)}, f32[512]{0:T(512)}, u32[]{:S(2)}) copy-start(f32[512]{0:T(512)} %copy-done.50) | copy-start | bytes 6148
  191.8 3.9 %copy-start.57 = (f32[2,64]{1,0:T(2,128)S(1)}, f32[2,64]{1,0:T(2,128)}, u32[]{:S(2)}) copy-start(f32[2,64]{1,0:T(2,128)} %copy-done.56) | copy-start | bytes 1540
  191.8 3.9 %copy-start.65 = (f32[2,64]{1,0:T(2,128)S(1)}, f32[2,64]{1,0:T(2,128)}, u32[]{:S(2)}) copy-start(f32[2,64]{1,0:T(2,128)} %copy-done.64) | copy-start | bytes 1540
  192.3 5.5 %copy-start.89 = (f32[2,64]{1,0:T(2,128)S(1)}, f32[2,64]{1,0:T(2,128)}, u32[]{:S(2)}) copy-start(f32[2,64]{1,0:T(2,128)} %copy-done.88) | copy-start | bytes 1540
  195.7 3.0 copy-start.22
  195.7 3.0 copy-start.36
  200.3 4.8 %copy-start.10 = (bf16[1024,512]{1,0:T(8,128)(2,1)S(1)}, bf16[1024,512]{1,0:T(8,128)(2,1)}, u32[]{:S(2)}) copy-start(bf16[1024,512]{1,0:T(8,128)(2,1)} %bitcast_convert_fusion.2) | copy-start | bytes 3145732
  200.3 4.8 %copy-start.15 = (bf16[640,512]{1,0:T(8,128)(2,1)S(1)}, bf16[640,512]{1,0:T(8,128)(2,1)}, u32[]{:S(2)}) copy-start(bf16[640,512]{1,0:T(8,128)(2,1)} %fusion.1) | copy-start | bytes 1966084
  205.1 3.2 %copy-start.47 = (bf16[9,512]{1,0:T(8,128)(2,1)S(1)}, bf16[9,512]{1,0:T(8,128)(2,1)}, u32[]{:S(2)}) copy-start(bf16[9,512]{1,0:T(8,128)(2,1)} %add_reduce_fusion) | copy-start | bytes 27652
  205.1 3.3 %copy-start.66 = (f32[2,64]{1,0:T(2,128)S(1)}, f32[2,64]{1,0:T(2,128)}, u32[]{:S(2)}) copy-start(f32[2,64]{1,0:T(2,128)} %copy-done.64) | copy-start | bytes 1540
  211.1 2.1 copy-start.25
  292.8 5.6 %copy-start.40 = (bf16[336,512]{1,0:T(8,128)(2,1)S(1)}, bf16[336,512]{1,0:T(8,128)(2,1)}, u32[]{:S(2)}) copy-start(bf16[336,512]{1,0:T(8,128)(2,1)} %get-tuple-element.45) | copy-start | bytes 1032196
  295.3 7.0 %copy-start.30 = (bf16[336,512]{1,0:T(8,128)(2,1)S(1)}, bf16[336,512]{1,0:T(8,128)(2,1)}, u32[]{:S(2)}) copy-start(bf16[336,512]{1,0:T(8,128)(2,1)} %get-tuple-element.47) | copy-start | bytes 1032196
  298.5 5.4 %copy-start.20 = (bf16[448,512]{1,0:T(8,128)(2,1)S(1)}, bf16[448,512]{1,0:T(8,128)(2,1)}, u32[]{:S(2)}) copy-start(bf16[448,512]{1,0:T(8,128)(2,1)} %get-tuple-element.46) | copy-start | bytes 1376260
  (32 other events, 39.2 us)
where the time goes:
time: 307 us; the launch traced here: 306 us
  Pallas kernels  182 us (59%)
  local copies, waits for them, and re-layouts  56.1 us (18%)
  other arithmetic  35.4 us (12%)
  matrix products  29.8 us (10%)
    pallas_call x1, Pallas kernels, scatter_all(): pl.pallas_call(functools.partial(scatter_kernel, n, rows_list, skew), out...  76.2 us
    pallas_call x1, Pallas kernels, gather_all(): pl.pallas_call(functools.partial(gather_kernel, n, rows_list), out_shape=...  58.3 us
    pallas_call x1, Pallas kernels, joint_call(): pl.pallas_call(functools.partial(joint_kernel, dims), out_shape=[jax.Shap...  47.6 us
    unnamed x204, local copies, waits for them, and re-layouts  15.7 us
    dot_general x7, matrix products, contract_rows(): lax.dot_general(first_op, second_op, (((0,), (0,)), ((), ())), preferred_...  11.8 us
    dot_general x7, matrix products, against(): lax.dot_general(first_op, second_op, (((1,), (1,)), ((), ())), preferred_...  9.14 us
    dot_general x7, matrix products, product(): return jnp.dot(first_op, second_op, preferred_element_type=jnp.float32)  6.2 us

commit v1 on v0

--- a/solution.py
+++ b/solution.py
@@ -438,10 +438,10 @@
     return out
 
 
-def scalar_ends(lengths, r, segs):
+def scalar_ends(ints, r, segs):
     ends, total = [], 0
     for s in range(segs):
-        total = total + lengths[r, s]
+        total = total + ints[r, s]
         ends.append(total)
     return ends
 
@@ -451,14 +451,14 @@
     return top, functools.reduce(jnp.add, [jnp.exp(v - top) for v in terms])
 
 
-def lattice(peers, lengths, counts, terms, skewed, hist, grads, loss, dims):
+def lattice(peers, ints, terms, skewed, hist, grads, loss, dims):
     frames, rows, segs, own_u, labs = dims
     wide = (frames, 128)
     lane = lane_ids(wide)
     group = rows * own_u
     j, row, u = lane % own_u, (lane % group) // own_u, (lane // group) * own_u + lane % own_u
     t = row_ids(wide)
-    all_ends = [scalar_ends(lengths, r, segs) for r in range(rows)]
+    all_ends = [scalar_ends(ints, r, segs) for r in range(rows)]
 
     def per_lane(values):
         out = jnp.zeros(wide, jnp.int32)
@@ -467,7 +467,7 @@
         return out
 
     ends = [per_lane([all_ends[r][s] for r in range(rows)]) for s in range(segs)]
-    labels_in = [per_lane([counts[r, s] for r in range(rows)]) for s in range(segs)]
+    labels_in = [per_lane([ints[r, segs + s] for r in range(rows)]) for s in range(segs)]
     seg = seg_of(t, ends)
     stop = pick(seg, ends)
     begin = pick(seg, [jnp.zeros(wide, jnp.int32)] + ends[:-1])
@@ -616,7 +616,7 @@
 
 def joint_kernel(
     dims,
-    enc_own, pred, lengths, counts, labels, predx, tok, tail, bias,
+    enc_own, pred, ints, predx, tok, tail, bias,
     g_enc, g_predictor, g_pack, g_mix, g_bias, loss,
     enc_all, proj, hid, slope, prob, prob_tail, mine, terms, skewed, hist, grads, g_pred, part, came,
     send, recv,
@@ -653,7 +653,7 @@
             def _():
                 enc_copy(j, peers.owner(j)).wait_recv()
         r = row_of(k)
-        seg = seg_of(row_ids((frames, width)), scalar_ends(lengths, r, segs))
+        seg = seg_of(row_ids((frames, width)), scalar_ends(ints, r, segs))
         enc = enc_all[r].astype(F32)
         for u in range(own_u):
             per_frame = pick(
@@ -665,7 +665,7 @@
         h = hid[r]
         end = mm(h, tail[...]) + bias[:, TOK:]
         wide = mm(h, tok[...]) + bias[:, :TOK]
-        seg_l = seg_of(row_ids((frames, TOK)), scalar_ends(lengths, r, segs))
+        seg_l = seg_of(row_ids((frames, TOK)), scalar_ends(ints, r, segs))
         for u in range(own_u):
             logit, last = wide[u * frames : (u + 1) * frames], end[u * frames : (u + 1) * frames]
             top = jnp.maximum(jnp.max(logit, axis=1, keepdims=True), last[:, 0:1])
@@ -682,7 +682,7 @@
             prob[r, u * frames : (u + 1) * frames, :] = (e * (1.0 / total)).astype(BF)
             prob_tail[r, u * frames : (u + 1) * frames, :] = e_last * (1.0 / jnp.where(is_tok, total, total_dur))
             norm_tok, norm_dur = top + jnp.log(total), top_dur + jnp.log(total_dur)
-            label = pick(seg_l, [labels[r, s * own_u + u] for s in range(segs)])
+            label = pick(seg_l, [ints[r, 2 * segs + s * own_u + u] for s in range(segs)])
             at_label = jnp.sum(jnp.where(lane_w == label, logit, 0.0), axis=1, keepdims=True) - norm_tok
             lp = last - jnp.where(is_tok, norm_tok, norm_dur)
             for kind in range(KINDS):
@@ -703,7 +703,7 @@
         term_copy(j, peers.lab).start()
     for j in range(1, labs):
         term_copy(j, peers.owner(j)).wait_recv()
-    lattice(peers, lengths, counts, terms, skewed, hist, grads, loss, dims)
+    lattice(peers, ints, terms, skewed, hist, grads, loss, dims)
 
     def part_copy(j):
         return remote(part.at[j], came.at[j], send.at[2, j], recv.at[2, j], peers.device(j))
@@ -713,13 +713,13 @@
         r = row_of(k)
         shift = (256 - peers.lab * group - r * own_u) % 128
         rolled = [pltpu.roll(grads[kind], shift, 1) for kind in range(KINDS)]
-        seg_l = seg_of(row_ids((frames, TOK)), scalar_ends(lengths, r, segs))
+        seg_l = seg_of(row_ids((frames, TOK)), scalar_ends(ints, r, segs))
         sum_tok, sum_tail = sums
         for u in range(own_u):
             at = slice(u * frames, (u + 1) * frames)
             a, b = rolled[6][:, u : u + 1], rolled[0][:, u : u + 1]
             both = a + b
-            label = pick(seg_l, [labels[r, s * own_u + u] for s in range(segs)])
+            label = pick(seg_l, [ints[r, 2 * segs + s * own_u + u] for s in range(segs)])
             g = (jnp.where(lane_w == label, a, 0.0) - prob[r, at, :].astype(F32) * both).astype(BF)
             prob[r, at, :] = g
             aim = jnp.zeros((frames, 128), F32)
@@ -737,7 +737,7 @@
         part[k // micro, k % micro] = summed.astype(BF)
         shape = (segs * own_u, span)
         lanes = lane_ids(shape)
-        seg_t = seg_of(lanes % frames, scalar_ends(lengths, r, segs))
+        seg_t = seg_of(lanes % frames, scalar_ends(ints, r, segs))
         hit = (row_ids(shape) == seg_t * own_u + lanes // frames).astype(BF)
         g_pred[pl.ds(r * segs * own_u, segs * own_u), :] = mm(hit, back.astype(BF)).astype(BF)
         for j in range(1, labs):
@@ -782,7 +782,7 @@
         part_copy(j).wait_send()
 
 
-def joint_call(enc_own, pred, lengths, counts, labels, predx, tok, tail, bias, dims):
+def joint_call(enc_own, pred, ints, predx, tok, tail, bias, dims):
     frames, rows, segs, own_u, labs = dims
     width = enc_own.shape[-1]
     span = own_u * frames
@@ -799,7 +799,7 @@
             jax.ShapeDtypeStruct((16, 256), F32),
             jax.ShapeDtypeStruct((8, 128), F32),
         ],
-        in_specs=[vm, vm, sm, sm, sm, vm, vm, vm, vm],
+        in_specs=[vm, vm, sm, vm, vm, vm, vm],
         out_specs=[vm] * 6,
         scratch_shapes=[
             pltpu.VMEM((rows, frames, width), BF),
@@ -822,260 +822,441 @@
         compiler_params=pltpu.CompilerParams(
             collective_id=2, has_side_effects=True, vmem_limit_bytes=60 * 2**20
         ),
-    )(enc_own, pred, lengths, counts, labels, predx, tok, tail, bias)
+    )(enc_own, pred, ints, predx, tok, tail, bias)
 
 
 HEADS = 8
-HD = 64
-H = 8
-epsilon = 1e-05
-very_low = -100000.0
-
-
-def product(first_op, second_op):
-    return jnp.dot(first_op, second_op, preferred_element_type=jnp.float32)
-
-
-def contract_rows(first_op, second_op):
-    return lax.dot_general(
-        first_op, second_op, (((0,), (0,)), ((), ())), preferred_element_type=jnp.float32
-    )
-
-
-def against(first_op, second_op):
-    return lax.dot_general(
-        first_op, second_op, (((1,), (1,)), ((), ())), preferred_element_type=jnp.float32
-    )
-
-
-def layer_norm(inputs, gain_vec):
-    centre = inputs - jnp.mean(inputs, axis=-1, keepdims=True)
-    spread = jnp.mean(centre * centre, axis=-1, keepdims=True)
-    return centre * lax.rsqrt(spread + epsilon) * gain_vec
-
-
-def segments(lengths, frames):
-    seg_ends = jnp.cumsum(lengths, axis=-1)
-    starts = seg_ends - lengths
-    position = jnp.arange(frames, dtype=jnp.int32)
-    passed = position[:, None] >= seg_ends[..., None, :]
-    seg_index = jnp.sum(passed.astype(jnp.int32), axis=-1)
-    member = seg_index[..., None] == jnp.arange(lengths.shape[-1], dtype=jnp.int32)
-    seg_start = jnp.sum(jnp.where(member, starts[..., None, :], 0), axis=-1)
-    seg_stop = jnp.sum(jnp.where(member, seg_ends[..., None, :], 0), axis=-1)
-    return (seg_index, member, position - seg_start, seg_stop - position)
-
-
-def conv_piece(conv_pre, w_depth, gain_depth, seg_index):
-    width_in = w_depth.shape[1]
-    frames = conv_pre.shape[0]
-    half_taps = w_depth.shape[0] // 2
-    gated = conv_pre[:, :width_in] * jax.nn.sigmoid(conv_pre[:, width_in:])
-    padded = jnp.pad(gated, ((half_taps, half_taps), (0, 0)))
-    seg_pad = jnp.pad(seg_index, (half_taps, half_taps), constant_values=-1)
-    summed = jnp.zeros_like(gated)
-    for tap_index in range(w_depth.shape[0]):
-        same_seg = (seg_pad[tap_index : tap_index + frames] == seg_index).astype(gated.dtype)
-        summed = (
-            summed + w_depth[tap_index] * padded[tap_index : tap_index + frames] * same_seg[:, None]
+EPS = 1e-05
+TAPS = 9
+GAIN_ROW = 9
+STATE = (
+    ("n_ffn", 512, F32), ("n_att", 512, F32), ("n_conv", 512, F32), ("n_depth", 512, F32), ("n_out", 512, F32),
+    ("scales", 128, F32), ("act", 2048, BF), ("slope", 2048, BF), ("qkv", 1536, BF), ("context", 512, BF),
+    ("value", 512, F32), ("gate", 512, F32),
+)
+
+
+def sigmoid(v):
+    return 0.5 * jnp.tanh(0.5 * v) + 0.5
+
+
+def norm_parts(v):
+    c = v - jnp.mean(v, axis=1, keepdims=True)
+    r = lax.rsqrt(jnp.mean(c * c, axis=1, keepdims=True) + EPS)
+    return c * r, r
+
+
+def norm_back(gy, n, r, gain):
+    gg = gy * gain
+    gain_grad = jnp.sum(gy * n, axis=0, keepdims=True)
+    inner = gg - jnp.mean(gg, axis=1, keepdims=True) - n * jnp.mean(gg * n, axis=1, keepdims=True)
+    return r * inner, gain_grad
+
+
+def rows_of(ref, n, first, count):
+    per = ref.shape[0] // n
+    return jnp.concatenate([ref[d * per + first : d * per + first + count, :] for d in range(n)], axis=0)
+
+
+def put_rows(ref, n, first, count, value):
+    per = ref.shape[0] // n
+    for d in range(n):
+        ref[d * per + first : d * per + first + count, :] = value[d * count : (d + 1) * count].astype(ref.dtype)
+
+
+def own_ends(ints, micro, segs):
+    first = lax.axis_index("lab") * micro
+    return [scalar_ends(ints, first + m, segs) for m in range(micro)]
+
+
+def seg_id(position, ends, frames):
+    t, row = position % frames, position // frames
+    out = seg_of(t, ends[0])
+    for m in range(1, len(ends)):
+        out = jnp.where(row == m, seg_of(t, ends[m]), out)
+    return out + row * len(ends[0])
+
+
+def shifted(value, step):
+    rows = value.shape[0]
+    return pltpu.roll(value, (-step) % rows, 0) if step % rows else value
+
+
+def assemble_small(target, n, per, ds):
+    lane = lane_ids((16, 128))
+    columns = [jnp.zeros((16, 128), F32) for _ in range(n * ds // 128)]
+    for d in range(n):
+        piece = jnp.where(lane < ds, target[d * per : d * per + 16, 256:384].astype(F32), 0.0)
+        at = d * ds % 128
+        columns[d * ds // 128] = columns[d * ds // 128] + (pltpu.roll(piece, at, 1) if at else piece)
+    return jnp.concatenate(columns, axis=1)
+
+
+def split_small(value, d, ds):
+    at = d * ds % 128
+    piece = value[:, d * ds // 128 * 128 : d * ds // 128 * 128 + 128]
+    piece = pltpu.roll(piece, 128 - at, 1) if at else piece
+    return jnp.where(lane_ids((16, 128)) < ds, piece, 0.0)
+
+
+class Sizes:
+    def __init__(self, n, ds, ff, qk, pi, jr):
+        self.n, self.ds, self.ff, self.qk, self.pi, self.jr = n, ds, ff, qk, pi, jr
+        self.rows = (jr + ff, ff + qk, 2 * ds + pi + jr, 3 * jr)
+        self.model = n * ds
+
+
+def head_pair(ref, block, pair):
+    at = block * 512 + pair * 128
+    return ref[:, at : at + 128]
+
+
+def forward_pieces(z, x_ref, ints, dims, full, small_ref, st, probs, encoded, enc_proj):
+    frames, rows, segs, own_u, labs = dims
+    n, micro = z.n, rows // labs
+    count = micro * frames
+    ends = own_ends(ints, micro, segs)
+    ids_r = seg_id(row_ids((count, 128)), ends, frames)
+    ids_c = seg_id(lane_ids((count, count)), ends, frames)
+    scale_lane = lane_ids((count, 128))
+
+    def norm(v, name, which):
+        nv, r = norm_parts(v)
+        st[name][...] = nv
+        st["scales"][...] = jnp.where(scale_lane == which, r, st["scales"][...])
+        return nv * small_ref[GAIN_ROW + which : GAIN_ROW + which + 1, :]
+
+    small_ref[...] = assemble_small(full[0], n, z.rows[0], z.ds)
+    st["scales"][...] = jnp.zeros((count, 128), F32)
+    x = x_ref[...].reshape(count, z.model).astype(F32)
+    ffn_in = norm(x, "n_ffn", 0).astype(BF)
+    half = n // 2
+    per = z.rows[0]
+    for part in range(2):
+        w = jnp.concatenate(
+            [full[0][d * per + z.jr : d * per + z.jr + z.ff, :] for d in range(part * half, part * half + half)], axis=0
         )
-    return jax.nn.silu(layer_norm(summed, gain_depth))
-
-
-def attend_scores(queries, keys, same_seg, score_scale):
-    raw = (
-        jnp.einsum("thd,shd->hts", queries, keys, preferred_element_type=jnp.float32) * score_scale
-    )
-    return jnp.where(same_seg[None], raw, very_low)
-
-
-def block_forward(frames_bf, seg_index, all_weights):
-    (
-        gain_ffn,
-        w_ffn_in,
-        w_ffn_out,
-        gain_att,
-        w_qkv,
-        w_att_out,
-        gain_conv,
-        w_point_in,
-        w_depth,
-        gain_depth,
-        w_point_out,
-        gain_out,
-        w_enc,
-    ) = all_weights[:13]
-    frames = frames_bf.shape[0]
-    inputs = frames_bf.astype(jnp.float32)
-    normed, norm_back_one = jax.vjp(layer_norm, inputs, gain_ffn.astype(jnp.float32))
-    ffn_in = normed.astype(jnp.bfloat16)
-    ffn_pre = product(ffn_in, w_ffn_in)
-    ffn_act = jax.nn.silu(ffn_pre).astype(jnp.bfloat16)
-    after_ffn = inputs + 0.5 * product(ffn_act, w_ffn_out)
-    normed, norm_back_two = jax.vjp(layer_norm, after_ffn, gain_att.astype(jnp.float32))
-    att_in = normed.astype(jnp.bfloat16)
-    qkv_all = product(att_in, w_qkv).astype(jnp.bfloat16).reshape(frames, 3, H, HD)
-    queries, keys, values = (qkv_all[:, 0], qkv_all[:, 1], qkv_all[:, 2])
-    same_seg = seg_index[:, None] == seg_index[None, :]
-    scores = attend_scores(queries, keys, same_seg, HD ** (-0.5))
-    largest = jnp.max(scores, axis=-1, keepdims=True)
-    weights = jnp.exp(scores - largest)
-    totals = jnp.sum(weights, axis=-1, keepdims=True)
-    norm_log = largest + jnp.log(totals)
-    probs = (weights / totals).astype(jnp.bfloat16)
-    context = (
-        jnp.einsum("hts,shd->thd", probs, values, preferred_element_type=jnp.float32)
-        .astype(jnp.bfloat16)
-        .reshape(frames, H * HD)
-    )
-    after_att = after_ffn + product(context, w_att_out)
-    normed, norm_back_three = jax.vjp(layer_norm, after_att, gain_conv.astype(jnp.float32))
-    conv_in = normed.astype(jnp.bfloat16)
-    conv_pre = product(conv_in, w_point_in)
-    conv_out, conv_back = jax.vjp(
-        functools.partial(conv_piece, seg_index=seg_index),
-        conv_pre,
-        w_depth.astype(jnp.float32),
-        gain_depth.astype(jnp.float32),
-    )
-    conv_act = conv_out.astype(jnp.bfloat16)
-    after_conv = after_att + product(conv_act, w_point_out)
-    encoded, norm_back_four = jax.vjp(layer_norm, after_conv, gain_out.astype(jnp.float32))
-    enc_in = encoded.astype(jnp.bfloat16)
-    enc_proj = product(enc_in, w_enc).astype(jnp.bfloat16)
-    kept_state = (
-        ffn_in,
-        ffn_pre,
-        ffn_act,
-        att_in,
-        queries,
-        keys,
-        values,
-        same_seg,
-        norm_log,
-        context,
-        conv_in,
-        conv_act,
-        enc_in,
-        norm_back_one,
-        norm_back_two,
-        norm_back_three,
-        norm_back_four,
-        conv_back,
-    )
-    return (enc_in, enc_proj, kept_state)
-
-
-def block_backward(enc_grad, kept_state, all_weights):
-    w_ffn_in, w_ffn_out, w_qkv, w_att_out, w_point_in, w_point_out, w_enc = (
-        all_weights[1],
-        all_weights[2],
-        all_weights[4],
-        all_weights[5],
-        all_weights[7],
-        all_weights[10],
-        all_weights[12],
-    )
-    (
-        ffn_in,
-        ffn_pre,
-        ffn_act,
-        att_in,
-        queries,
-        keys,
-        values,
-        same_seg,
-        norm_log,
-        context,
-        conv_in,
-        conv_act,
-        enc_in,
-        norm_back_one,
-        norm_back_two,
-        norm_back_three,
-        norm_back_four,
-        conv_back,
-    ) = kept_state
-    frames = ffn_in.shape[0]
-    score_scale = HD ** (-0.5)
-    grad_enc_w = contract_rows(enc_in, enc_grad)
-    grad_conv_sum, grad_gain_out = norm_back_four(against(enc_grad, w_enc))
-    branch = grad_conv_sum.astype(jnp.bfloat16)
-    grad_point_out = contract_rows(conv_act, branch)
-    grad_pre, grad_depth, grad_gain_depth = conv_back(against(branch, w_point_out))
-    grad_pre_low = grad_pre.astype(jnp.bfloat16)
-    grad_point_in = contract_rows(conv_in, grad_pre_low)
-    grad_normed, grad_gain_conv = norm_back_three(against(grad_pre_low, w_point_in))
-    grad_att_sum = grad_conv_sum + grad_normed
-    branch = grad_att_sum.astype(jnp.bfloat16)
-    grad_att_out = contract_rows(context, branch)
-    grad_context = against(branch, w_att_out).astype(jnp.bfloat16).reshape(frames, H, HD)
-    scores = attend_scores(queries, keys, same_seg, score_scale)
-    probs = jnp.exp(scores - norm_log)
-    grad_probs = jnp.einsum(
-        "thd,shd->hts", grad_context, values, preferred_element_type=jnp.float32
-    )
-    grad_values = jnp.einsum(
-        "hts,thd->shd", probs.astype(jnp.bfloat16), grad_context, preferred_element_type=jnp.float32
-    )
-    grad_scores = (
-        probs * (grad_probs - jnp.sum(grad_probs * probs, axis=-1, keepdims=True))
-    ).astype(jnp.bfloat16)
-    grad_queries = (
-        jnp.einsum("hts,shd->thd", grad_scores, keys, preferred_element_type=jnp.float32)
-        * score_scale
-    )
-    grad_keys = (
-        jnp.einsum("hts,thd->shd", grad_scores, queries, preferred_element_type=jnp.float32)
-        * score_scale
-    )
-    grad_qkv_all = (
-        jnp.stack([grad_queries, grad_keys, grad_values], axis=1)
-        .astype(jnp.bfloat16)
-        .reshape(frames, 3 * H * HD)
-    )
-    grad_w_qkv = contract_rows(att_in, grad_qkv_all)
-    grad_normed, grad_gain_att = norm_back_two(against(grad_qkv_all, w_qkv))
-    grad_ffn_sum = grad_att_sum + grad_normed
-    branch = (0.5 * grad_ffn_sum).astype(jnp.bfloat16)
-    grad_ffn_out = contract_rows(ffn_act, branch)
-    grad_act = against(branch, w_ffn_out)
-    grad_pre = jax.vjp(jax.nn.silu, ffn_pre)[1](grad_act)[0]
-    grad_pre_low = grad_pre.astype(jnp.bfloat16)
-    grad_ffn_in = contract_rows(ffn_in, grad_pre_low)
-    grad_normed, grad_gain_ffn = norm_back_one(against(grad_pre_low, w_ffn_in))
-    grad_inputs = grad_ffn_sum + grad_normed
-    return (
-        grad_inputs,
-        (
-            grad_gain_ffn,
-            grad_ffn_in,
-            grad_ffn_out,
-            grad_gain_att,
-            grad_w_qkv,
-            grad_att_out,
-            grad_gain_conv,
-            grad_point_in,
-            grad_depth,
-            grad_gain_depth,
-            grad_point_out,
-            grad_gain_out,
-            grad_enc_w,
-        ),
-    )
-
-
-def pad_rows(value, rows):
-    return jnp.pad(value, ((0, rows - value.shape[0]), (0, 0)))
-
-
-def pad_lanes(value, lanes):
-    return jnp.pad(value, ((0, 0), (0, lanes - value.shape[1])))
-
-
-def pick_rows(gathered, n, first, rows):
-    per = gathered.shape[0] // n
-    return gathered.reshape(n, per, -1)[:, first : first + rows].reshape(n * rows, -1)
+        pre = mm_t(ffn_in, w)
+        sg = sigmoid(pre)
+        at = slice(part * half * z.ff, (part + 1) * half * z.ff)
+        st["act"][:, at] = (pre * sg).astype(BF)
+        st["slope"][:, at] = (sg * (1.0 + pre * (1.0 - sg))).astype(BF)
+    yield
+    after_ffn = x + 0.5 * mm(st["act"][...], rows_of(full[1], n, 0, z.ff))
+    att_in = norm(after_ffn, "n_att", 1).astype(BF)
+    st["qkv"][...] = mm_t(att_in, rows_of(full[1], n, z.ff, z.qk)).astype(BF)
+    same = ids_r == ids_c
+    low_half = lane_ids((count, 128)) < 64
+    for pair in range(HEADS // 2):
+        q, k, v = (head_pair(st["qkv"], b, pair) for b in range(3))
+        total = None
+        for side in range(2):
+            keep = low_half if side == 0 else ~low_half
+            score = mm_t(jnp.where(keep, q, 0), k) * (64 ** -0.5)
+            score = jnp.where(same, score, LOW)
+            e = jnp.exp(score - jnp.max(score, axis=1, keepdims=True))
+            p = (e * (1.0 / jnp.sum(e, axis=1, keepdims=True))).astype(BF)
+            probs[2 * pair + side] = p
+            part = mm(p, jnp.where(keep, v, 0))
+            total = part if total is None else total + part
+        st["context"][:, pair * 128 : pair * 128 + 128] = total.astype(BF)
+    yield
+    after_att = after_ffn + mm(st["context"][...], rows_of(full[2], n, 0, z.ds))
+    conv_in = norm(after_att, "n_conv", 2).astype(BF)
+    conv_pre = mm_t(conv_in, rows_of(full[2], n, z.ds, z.pi))
+    st["value"][...] = conv_pre[:, : z.model]
+    st["gate"][...] = sigmoid(conv_pre[:, z.model :])
+    depth = []
+    for c in range(z.model // 128):
+        at = slice(c * 128, c * 128 + 128)
+        gated = st["value"][:, at] * st["gate"][:, at]
+        total = jnp.zeros((count, 128), F32)
+        for j in range(TAPS):
+            ok = shifted(ids_r, j - TAPS // 2) == ids_r
+            total = total + jnp.where(ok, shifted(gated, j - TAPS // 2), 0.0) * small_ref[j : j + 1, at]
+        depth.append(total)
+    dn = norm(jnp.concatenate(depth, axis=1), "n_depth", 3)
+    conv_act = (dn * sigmoid(dn)).astype(BF)
+    after_conv = after_att + mm(conv_act, rows_of(full[2], n, z.ds + z.pi, z.ds))
+    out = norm(after_conv, "n_out", 4).astype(BF)
+    encoded[...] = out.reshape(encoded.shape)
+    enc_proj[...] = mm_t(out, rows_of(full[2], n, 2 * z.ds + z.pi, z.jr)).astype(BF).reshape(enc_proj.shape)
+    yield
+
+
+def backward_pieces(z, g_enc, ints, dims, full, small_ref, st, probs, grads, small_grad, grad_frames):
+    frames, rows, segs, own_u, labs = dims
+    n, micro = z.n, rows // labs
+    count = micro * frames
+    ends = own_ends(ints, micro, segs)
+    ids_r = seg_id(row_ids((count, 128)), ends, frames)
+
+    def gain(which):
+        return small_ref[GAIN_ROW + which : GAIN_ROW + which + 1, :]
+
+    def back(gy, name, which):
+        g, gain_grad = norm_back(gy, st[name][...], st["scales"][:, which : which + 1], gain(which))
+        small_grad[GAIN_ROW + which : GAIN_ROW + which + 1, :] = gain_grad
+        return g
+
+    def normed(name, which):
+        return (st[name][...] * gain(which)).astype(BF)
+
+    small_grad[...] = jnp.zeros(small_grad.shape, F32)
+    ge = g_enc[...].reshape(count, -1)
+    off = 2 * z.ds + z.pi
+    put_rows(grads[2], n, off, z.jr, t_mm(ge, normed("n_out", 4)))
+    g_conv_sum = back(mm(ge, rows_of(full[2], n, off, z.jr)), "n_out", 4)
+    branch = g_conv_sum.astype(BF)
+    dn = st["n_depth"][...] * gain(3)
+    sg = sigmoid(dn)
+    put_rows(grads[2], n, z.ds + z.pi, z.ds, t_mm((dn * sg).astype(BF), branch))
+    g_act = mm_t(branch, rows_of(full[2], n, z.ds + z.pi, z.ds))
+    g_depth = back(g_act * (sg * (1.0 + dn * (1.0 - sg))), "n_depth", 3)
+    yield
+    low_a, low_b = [], []
+    for c in range(z.model // 128):
+        at = slice(c * 128, c * 128 + 128)
+        value, gate = st["value"][:, at], st["gate"][:, at]
+        gated, gd = value * gate, g_depth[:, at]
+        total = jnp.zeros((count, 128), F32)
+        for j in range(TAPS):
+            step = j - TAPS // 2
+            ok = shifted(ids_r, step) == ids_r
+            small_grad[j : j + 1, at] = jnp.sum(jnp.where(ok, shifted(gated, step), 0.0) * gd, axis=0, keepdims=True)
+            ok = shifted(ids_r, -step) == ids_r
+            total = total + jnp.where(ok, shifted(gd, -step), 0.0) * small_ref[j : j + 1, at]
+        low_a.append((total * gate).astype(BF))
+        low_b.append((total * value * gate * (1.0 - gate)).astype(BF))
+    low = jnp.concatenate(low_a + low_b, axis=1)
+    put_rows(grads[2], n, z.ds, z.pi, t_mm(low, normed("n_conv", 2)))
+    g_att_sum = g_conv_sum + back(mm(low, rows_of(full[2], n, z.ds, z.pi)), "n_conv", 2)
+    branch = g_att_sum.astype(BF)
+    put_rows(grads[2], n, 0, z.ds, t_mm(st["context"][...], branch))
+    g_context = mm_t(branch, rows_of(full[2], n, 0, z.ds)).astype(BF)
+    yield
+    low_half = lane_ids((count, 128)) < 64
+    columns = [[], [], []]
+    for pair in range(HEADS // 2):
+        q, k, v = (head_pair(st["qkv"], b, pair) for b in range(3))
+        gc = g_context[:, pair * 128 : pair * 128 + 128]
+        sums = [None, None, None]
+        for side in range(2):
+            keep = low_half if side == 0 else ~low_half
+            p = probs[2 * pair + side]
+            gc_h = jnp.where(keep, gc, 0)
+            gp = mm_t(gc_h, v)
+            pf = p.astype(F32)
+            gs = (pf * (gp - jnp.sum(gp * pf, axis=1, keepdims=True))).astype(BF)
+            parts = (
+                mm(gs, jnp.where(keep, k, 0)) * (64 ** -0.5),
+                t_mm(gs, jnp.where(keep, q, 0)) * (64 ** -0.5),
+                t_mm(p, gc_h),
+            )
+            sums = [b if a is None else a + b for a, b in zip(sums, parts)]
+        for b in range(3):
+            columns[b].append(sums[b].astype(BF))
+    g_qkv = jnp.concatenate(columns[0] + columns[1] + columns[2], axis=1)
+    yield
+    put_rows(grads[1], n, z.ff, z.qk, t_mm(g_qkv, normed("n_att", 1)))
+    g_ffn_sum = g_att_sum + back(mm(g_qkv, rows_of(full[1], n, z.ff, z.qk)), "n_att", 1)
+    branch = (0.5 * g_ffn_sum).astype(BF)
+    put_rows(grads[1], n, 0, z.ff, t_mm(st["act"][...], branch))
+    yield
+    g_pre = (mm_t(branch, rows_of(full[1], n, 0, z.ff)) * st["slope"][...].astype(F32)).astype(BF)
+    put_rows(grads[0], n, z.jr, z.ff, t_mm(g_pre, normed("n_ffn", 0)))
+    gx = g_ffn_sum + back(mm(g_pre, rows_of(full[0], n, z.jr, z.ff)), "n_ffn", 0)
+    grad_frames[...] = gx.reshape(grad_frames.shape)
+    yield
+
+
+def encode_kernel(
+    z, dims, x_ref, ints, w_in, w_out, w_qkv, w_att, w_pin, w_pout, w_enc, w_pred, tail, small_in, w_joint,
+    full0, full1, full2, predx, tok, tail_out, small_out, encoded, enc_proj, *rest,
+):
+    k = len(STATE)
+    st = {name: ref for (name, _, _), ref in zip(STATE, rest[:k])}
+    probs, rest = rest[k], rest[k + 1 :]
+    sources, full = rest[0:4], rest[4:8]
+    ring_recv, x_recv, sems, out_sem = rest[8:]
+    n = z.n
+    w = Where(n)
+    w.greet()
+    jr, js, ds = z.jr, w_pred.shape[1], z.ds
+
+    def down(value, count):
+        return jnp.concatenate([value, jnp.zeros((count - value.shape[0],) + value.shape[1:], value.dtype)], 0) if count > value.shape[0] else value
+
+    pred_t = down(w_pred[...].astype(F32).T.astype(BF), jr)
+    sources[0][jr:, :] = w_in[...].astype(F32).T.astype(BF)
+    sources[0][:jr, 0:128] = pred_t[:, 512:]
+    sources[0][:jr, 128:256] = tail[...]
+    sources[0][:jr, 256:] = jnp.zeros((jr, 256), BF)
+    sources[0][:16, 256:384] = small_in[...]
+    parts = [
+        Gather(w, sources[i], full[i], z.rows[i], ring_recv.at[i], x_recv.at[i], sems.at[i]) for i in range(4)
+    ]
+    turns = n // 2 + 2
+    skew = 2
+
+    def fill(g):
+        if g == 1:
+            sources[1][: z.ff, :] = w_out[...]
+            sources[1][z.ff :, :] = w_qkv[...].astype(F32).T.astype(BF)
+        elif g == 2:
+            sources[2][:ds, :] = w_att[...]
+            sources[2][ds : ds + z.pi, :] = w_pin[...].astype(F32).T.astype(BF)
+            sources[2][ds + z.pi : 2 * ds + z.pi, :] = w_pout[...]
+            sources[2][2 * ds + z.pi :, :] = down(w_enc[...].astype(F32).T.astype(BF), jr)
+        elif g == 3:
+            sources[3][:jr, :] = pred_t[:, :512]
+            sources[3][jr : 2 * jr, :] = down(w_joint[:, :512], jr)
+            sources[3][2 * jr :, :] = down(w_joint[:, 512:1024], jr)
+
+    def tick(i):
+        for s in range(turns - 1, -1, -1):
+            g = i - skew * s
+            if 0 <= g < 4:
+                if s == 0:
+                    fill(g)
+                parts[g].step(s)
+
+    outs = (full0, full1, full2)
+
+    def finish(g):
+        parts[g].whole()
+        if g < 3:
+            pltpu.make_async_copy(full[g], outs[g], out_sem.at[g]).start()
+
+    last = 4 + skew * (turns - 1)
+    compute = forward_pieces(z, x_ref, ints, dims, full, small_out, st, probs, encoded, enc_proj)
+    done = 0
+    for i in range(last):
+        tick(i)
+        g = i - skew * (turns - 1)
+        if g >= 0:
+            finish(g)
+            if g < 3:
+                next(compute)
+    predx[:, :512] = rows_of(full[3], n, 0, jr)
+    tok[:, :512] = rows_of(full[3], n, jr, jr)
+    tok[:, 512:] = rows_of(full[3], n, 2 * jr, jr)
+    mixes = rows_of(full[0], n, 0, jr)
+    predx[:, 512:] = mixes[:, :256]
+    tail_out[...] = mixes[:, 128:256]
+    for part in parts:
+        part.drain()
+    for g in range(3):
+        pltpu.make_async_copy(full[g], outs[g], out_sem.at[g]).wait()
+
+
+def encode_call(z, dims, x, ints, w_in, w_out, w_qkv, w_att, w_pin, w_pout, w_enc, w_pred, tail, small, w_joint):
+    frames, rows, segs, own_u, labs = dims
+    n, micro = z.n, rows // labs
+    count, width = micro * frames, n * z.jr
+    vm, sm, hbm = (pl.BlockSpec(memory_space=m) for m in (pltpu.VMEM, pltpu.SMEM, pl.ANY))
+    shape = jax.ShapeDtypeStruct
+    outs = [shape((n * z.rows[i], 512), BF) for i in range(3)]
+    outs += [shape((width, 768), BF), shape((width, 1024), BF), shape((width, 128), BF), shape((16, z.model), F32)]
+    outs += [shape((micro, frames, z.model), BF), shape((micro, frames, width), BF)]
+    outs += [shape((count, lanes), dtype) for _, lanes, dtype in STATE]
+    outs += [shape((HEADS, count, count), BF)]
+    return pl.pallas_call(
+        functools.partial(encode_kernel, z, dims),
+        out_shape=outs,
+        in_specs=[vm, sm] + [vm] * 11,
+        out_specs=[hbm] * 3 + [vm] * (len(outs) - 3),
+        scratch_shapes=[pltpu.VMEM((r, 512), BF) for r in z.rows]
+        + [pltpu.VMEM((n * r, 512), BF) for r in z.rows]
+        + [
+            pltpu.SemaphoreType.DMA((4, n - 1)),
+            pltpu.SemaphoreType.DMA((4, n - 1)),
+            pltpu.SemaphoreType.DMA((4, 5)),
+            pltpu.SemaphoreType.DMA((3,)),
+        ],
+        compiler_params=pltpu.CompilerParams(collective_id=0, has_side_effects=True, vmem_limit_bytes=60 * 2**20),
+    )(x, ints, w_in, w_out, w_qkv, w_att, w_pin, w_pout, w_enc, w_pred, tail, small, w_joint)
+
+
+def grad_kernel(z, dims, skew, *refs):
+    g_enc, ints, small_ref, g_pack, g_mix, g_bias = refs[:6]
+    hbm = refs[6:9]
+    refs = refs[9:]
+    k = len(STATE)
+    st = {name: ref for (name, _, _), ref in zip(STATE, refs[:k])}
+    probs, refs = refs[k], refs[k + 1 :]
+    outs, grad_frames, refs = refs[:4], refs[4], refs[5:]
+    full, refs = refs[:3], refs[3:]
+    grads, refs = list(refs[:3]) + [g_pack], refs[3:]
+    small_grad, bufs, (send, recv, in_sem) = refs[0], refs[1:17], refs[17:]
+    n = z.n
+    w = Where(n)
+    w.far_back = (ring_device(w.place + 2 * w.core - 1, n), w.lab)
+    for g in (2, 1, 0):
+        pltpu.make_async_copy(hbm[g], full[g], in_sem.at[g]).start()
+    w.greet()
+    order = (3, 2, 1, 0)
+    parts = [
+        Scatter(w, grads[g], outs[g], z.rows[g], bufs[4 * g : 4 * g + 4], send.at[g], recv.at[g]) for g in order
+    ]
+    stages = n // 2 + 5
+    compute = backward_pieces(z, g_enc, ints, dims, full, small_ref, st, probs, grads, small_grad, grad_frames)
+
+    def load(g):
+        pltpu.make_async_copy(hbm[g], full[g], in_sem.at[g]).wait()
+
+    def work(i):
+        if i == 1:
+            load(2)
+            next(compute)
+            next(compute)
+        elif i == 2:
+            load(1)
+            next(compute)
+            next(compute)
+        elif i == 3:
+            load(0)
+            next(compute)
+            per, ds = z.rows[0], z.ds
+            for d in range(n):
+                at = d * per
+                grads[0][at : at + z.jr, :256] = g_mix[d * z.jr : (d + 1) * z.jr, :]
+                if z.jr > 32:
+                    grads[0][at + 32 : at + z.jr, 256:] = jnp.zeros((z.jr - 32, 256), BF)
+                grads[0][at : at + 16, 256:384] = split_small(small_grad[...], d, ds).astype(BF)
+                grads[0][at : at + 16, 384:] = jnp.zeros((16, 128), BF)
+                grads[0][at + 16 : at + 32, 256:] = g_bias[...].astype(BF)
+
+    for tick in range(4 + skew * (stages - 1)):
+        for s in range(stages - 1, -1, -1):
+            g = tick - skew * s
+            if 0 <= g < 4:
+                if s == 0:
+                    work(g)
+                parts[g].stage(s)
+    for part in parts:
+        part.drain()
+
+
+def grad_call(z, dims, g_enc, ints, small, g_pack, g_mix, g_bias, full, state, probs, skew=1):
+    frames, rows, segs, own_u, labs = dims
+    n, micro = z.n, rows // labs
+    vm, sm, hbm = (pl.BlockSpec(memory_space=m) for m in (pltpu.VMEM, pltpu.SMEM, pl.ANY))
+    shape = jax.ShapeDtypeStruct
+    scratch = [pltpu.VMEM((n * z.rows[g], 512), BF) for g in range(3)] * 2 + [pltpu.VMEM((16, z.model), F32)]
+    for r in z.rows:
+        scratch += scatter_scratch(n, r, 512)
+    return pl.pallas_call(
+        functools.partial(grad_kernel, z, dims, skew),
+        out_shape=[shape((r, 512), BF) for r in z.rows] + [shape((micro, frames, z.model), F32)],
+        in_specs=[vm, sm, vm, vm, vm, vm] + [hbm] * 3 + [vm] * (len(STATE) + 1),
+        out_specs=[vm] * 5,
+        scratch_shapes=scratch + scatter_sems(n, 4) + [pltpu.SemaphoreType.DMA((3,))],
+        compiler_params=pltpu.CompilerParams(collective_id=1, has_side_effects=True, vmem_limit_bytes=60 * 2**20),
+    )(g_enc, ints, small, g_pack, g_mix, g_bias, *full, *state, probs)
+
+def pad_to(value, rows, lanes):
+    return jnp.pad(value, ((0, rows - value.shape[0]), (0, lanes - value.shape[1])))
 
 
 def local(
@@ -1087,79 +1268,40 @@
     micro, frames, model = frames_in.shape
     rows, segs, own_u, joint = predictor.shape
     ds, js = model // n, w_pred.shape[1]
-    jr = -(-js // TILE) * TILE
-    ff, qk, pi = w_ffn_in.shape[1], w_qkv.shape[1], w_point_in.shape[1]
-    pred_t = pad_rows(w_pred.T, jr)
-    tail = jnp.concatenate([w_joint_out[:, TOK:], bias_joint[:, None]], axis=1)
-    small = jnp.concatenate(
-        [pad_lanes(w_depth.T, 128), pad_lanes(jnp.stack([gain_ffn, gain_att, gain_conv, gain_depth, gain_out], 1), 128)],
-        axis=1,
+    jr = max(-(-js // TILE), 2) * TILE
+    z = Sizes(n, ds, w_ffn_in.shape[1], w_qkv.shape[1], w_point_in.shape[1], jr)
+    dims = (frames, rows, segs, own_u, labs)
+    tail = pad_to(jnp.concatenate([w_joint_out[:, TOK:], bias_joint[:, None]], axis=1), jr, 128)
+    gains = jnp.stack([gain_ffn, gain_att, gain_conv, gain_depth, gain_out])
+    small = pad_to(jnp.concatenate([w_depth, gains]), 16, 128)
+    ints = jnp.concatenate([seg_lengths, label_counts, label_ids.reshape(rows, segs * own_u)], axis=1)
+    out = encode_call(
+        z, dims, frames_in, ints, w_ffn_in, w_ffn_out, w_qkv, w_att_out, w_point_in, w_point_out, w_enc, w_pred,
+        tail, small, w_joint_out,
     )
-    mix = jnp.concatenate(
-        [pred_t[:, 512:], pad_rows(pad_lanes(tail, 128), jr), pad_rows(small, jr)], axis=1
-    )
-    shards = [
-        jnp.concatenate([mix, w_ffn_in.T], 0),
-        jnp.concatenate([w_ffn_out, w_qkv.T], 0),
-        jnp.concatenate([w_att_out, w_point_in.T, w_point_out, pad_rows(w_enc.T, jr)], 0),
-        jnp.concatenate(
-            [pred_t[:, :512], pad_rows(w_joint_out[:, :512], jr), pad_rows(w_joint_out[:, 512:TOK], jr)], 0
-        ),
-    ]
-    full = gather_all(n, shards)
-    mixes = pick_rows(full[0], n, 0, jr)
-    smalls = mixes.reshape(n, jr, 512)[:, :ds, 256:].reshape(model, 256)
-    gains = smalls[:, 128:133].T
-    weights = (
-        gains[0], pick_rows(full[0], n, jr, ff).T, pick_rows(full[1], n, 0, ff), gains[1],
-        pick_rows(full[1], n, ff, qk).T, pick_rows(full[2], n, 0, ds), gains[2], pick_rows(full[2], n, ds, pi).T,
-        smalls[:, :9].T, gains[3], pick_rows(full[2], n, ds + pi, ds), gains[4],
-        pick_rows(full[2], n, 2 * ds + pi, jr).T,
-    )
-    predx = jnp.concatenate([pick_rows(full[3], n, 0, jr), mixes[:, :256]], axis=1)
-    tok = jnp.concatenate([pick_rows(full[3], n, jr, jr), pick_rows(full[3], n, 2 * jr, jr)], axis=1)
-    tail_w = mixes[:, 128:256]
-    lab = lax.axis_index("lab")
-    own_lengths = lax.dynamic_slice_in_dim(seg_lengths, lab * micro, micro)
-    seg_index = segments(own_lengths, frames)[0]
-    enc_low, enc_proj, kept = jax.vmap(functools.partial(block_forward, all_weights=weights))(frames_in, seg_index)
-    pred_ext = pad_lanes(predictor.reshape(-1, joint), 768)
+    full, (predx, tok, tail_w, small_w, encoded, enc_proj) = out[:3], out[3:9]
+    state, probs = out[9:-1], out[-1]
+    pred_ext = pad_to(predictor.reshape(-1, joint), rows * segs * own_u, 768)
     pred_ext = jnp.where(lax.broadcasted_iota(jnp.int32, pred_ext.shape, 1) == joint + BIAS_LANE, 1.0, pred_ext).astype(BF)
     bias = jnp.pad(bias_out.astype(F32), (0, TOK + 128 - bias_out.shape[0]))[None]
-    dims = (frames, rows, segs, own_u, labs)
     g_enc, g_predictor, g_pack, g_mix, g_bias, loss = joint_call(
-        enc_proj, pred_ext, seg_lengths, label_counts, label_ids.reshape(rows, -1), predx, tok, tail_w, bias, dims
+        enc_proj, pred_ext, ints, predx, tok, tail_w, bias, dims
     )
-    grad_frames, block = jax.vmap(functools.partial(block_backward, all_weights=weights))(g_enc, kept)
-    block = [jnp.sum(g, axis=0).astype(BF) for g in block]
-    (gg_ffn, g_in, g_out, gg_att, g_qkv, g_att, gg_conv, g_pin, g_depth, gg_depth, g_pout, gg_out, g_encw) = block
-
-    def by(value, rows_each):
-        return value.reshape(n, rows_each, -1)
-
-    small = jnp.concatenate(
-        [pad_lanes(g_depth.T, 128), pad_lanes(jnp.stack([gg_ffn, gg_att, gg_conv, gg_depth, gg_out], 1), 128)], axis=1
-    ).reshape(n, ds, 256)
-    biases = jnp.broadcast_to(g_bias[None, : jr - ds].astype(BF), (n, min(16, jr - ds), 256))
-    small = jnp.concatenate([small, biases, jnp.zeros((n, jr - ds - biases.shape[1], 256), BF)], axis=1)
-    mix = jnp.concatenate([by(g_mix, jr), small], axis=2)
-    packs = [
-        g_pack,
-        jnp.concatenate([by(g_att, ds), by(g_pin.T, pi), by(g_pout, ds), by(g_encw.T, jr)], 1).reshape(-1, 512),
-        jnp.concatenate([by(g_out, ff), by(g_qkv.T, qk)], 1).reshape(-1, 512),
-        jnp.concatenate([mix, by(g_in.T, ff)], 1).reshape(-1, 512),
-    ]
-    own = [g.astype(F32) for g in scatter_all(n, packs)]
-    mix, small = own[3][:jr], own[3][:ds, 256:]
-    g_pred_t = jnp.concatenate([own[0][:js], mix[:js, :128]], axis=1)
-    g_joint = jnp.concatenate([own[0][jr : jr + js], own[0][2 * jr : 2 * jr + js], mix[:js, 128:134]], axis=1)
-    g_bias_out = jnp.concatenate([mix[ds : ds + 4, 256:].reshape(-1), mix[ds + 4, 256:262]])
+    own0, own1, own2, own3, grad_frames = grad_call(
+        z, dims, g_enc, ints, small_w, g_pack, g_mix, g_bias, full, state, probs
+    )
+    ff, pi = z.ff, z.pi
+    own0, own1, own2, own3 = (g.astype(F32) for g in (own0, own1, own2, own3))
+    g_small = own0[:16, 256 : 256 + ds]
+    g_pred_t = jnp.concatenate([own3[:js], own0[:js, :128]], axis=1)
+    g_joint = jnp.concatenate([own3[jr : jr + js], own3[2 * jr : 2 * jr + js], own0[:js, 128:134]], axis=1)
+    g_bias_out = jnp.concatenate([own0[16:20, 256:].reshape(-1), own0[20, 256:262]])
     loss_out = loss[:segs, : rows * own_u : own_u].T
     return (
-        loss_out, enc_low, grad_frames, g_predictor.reshape(predictor.shape),
-        small[:, 128], own[3][jr:].T, own[2][:ff], small[:, 129], own[2][ff:].T, own[1][:ds], small[:, 130],
-        own[1][ds : ds + pi].T, small[:, :9].T, small[:, 131], own[1][ds + pi : 2 * ds + pi], small[:, 132],
-        own[1][2 * ds + pi : 2 * ds + pi + js].T, g_pred_t.T, mix[:js, 128 + BIAS_LANE], g_joint, g_bias_out,
+        loss_out, encoded, grad_frames, g_predictor.reshape(predictor.shape),
+        g_small[9], own0[jr:].T, own1[:ff], g_small[10], own1[ff:].T, own2[:ds], g_small[11],
+        own2[ds : ds + pi].T, g_small[:9], g_small[12], own2[ds + pi : 2 * ds + pi], g_small[13],
+        own2[2 * ds + pi : 2 * ds + pi + js].T, g_pred_t.T, own0[:js, 128 + BIAS_LANE], g_joint, g_bias_out,
     )
 
 

time: 307 us -> 213 us (0.69)
  local copies, waits for them, and re-layouts: 56.1 us -> 25.2 us
  matrix products: 29.8 us -> 0 us
  other arithmetic: 35.4 us -> 6.07 us
    dot_general x27 -> x0, matrix products: 29.8 us -> none  [the longest x7 11.8 us: contract_rows(): lax.dot_general(first_op, second_op, (((0,), (0,)), ((), ())), preferred_...]
    slice x24 -> x8, local copies, waits for them, and re-layouts: 18.8 us -> 6.65 us  [the longest x1 1.6 us: local(): own2[ds + pi:2 * ds + pi]]
    concatenate x13 -> x4, other arithmetic: 14.2 us -> 2.72 us  [the longest x1 0.77 us: local(): jnp.concatenate([own3[jr:jr + js], own3[2 * jr:2 * jr + js], own0[:js, 12...]
    reduce_sum x16 -> x0, other arithmetic: 10.2 us -> none  [the longest x1 3.83 us: conv_piece(): w_depth[tap_index] * padded[tap_index:tap_index + frames]]
    convert_element_type x7 -> x0, local copies, waits for them, and re-layouts: 6.4 us -> none  [the longest x2 3.38 us: block_backward(): grad_qkv_all = jnp.stack([grad_queries, grad_keys, grad_values], axis=1)....]
    unnamed x204 -> x26, local copies, waits for them, and re-layouts: 15.7 us -> 9.93 us
    reshape x4 -> x2, local copies, waits for them, and re-layouts: 5.69 us -> 1.72 us  [the longest x1 0.96 us: local(): pred_ext = pad_to(predictor.reshape(-1, joint), rows * segs * own_u, 768)]
where the time goes in v1:
time: 213 us
  Pallas kernels  181 us (85%)
  local copies, waits for them, and re-layouts  25.2 us (12%)
  other arithmetic  6.07 us (3%)
    pallas_call x1, Pallas kernels, grad_call(): pl.pallas_call(functools.partial(grad_kernel, z, dims, skew), out_shape=[...  75.9 us
    pallas_call x1, Pallas kernels, encode_call(): pl.pallas_call(functools.partial(encode_kernel, z, dims), out_shape=outs,...  57.1 us
    pallas_call x1, Pallas kernels, joint_call(): pl.pallas_call(functools.partial(joint_kernel, dims), out_shape=[jax.Shap...  47.5 us
    unnamed x26, local copies, waits for them, and re-layouts  9.93 us

profile of v1, /device:TPU:0, one launch (start us, length us, event | category | flops | bytes accessed | tf_op | source)
XLA Modules:
  0.0 212.6 jit_solution(4223946452630643410)
XLA Ops:
  0.7 0.8 copy.61
  1.4 0.8 copy.62
  2.2 0.8 copy.63
  2.9 0.7 pad_add_fusion.ints.refs_1_
  3.6 1.4 concatenate.20
  5.1 0.6 pad.18.small_in
  5.7 0.7 pad_convert_fusion
  6.3 0.6 reshape.58.bias
  6.9 0.7 slice.76
  7.7 0.1 copy.71
  7.8 0.7 pad_maximum_fusion.2
  8.4 0.1 copy.65
  8.6 0.6 pad.17.tail
  9.2 1.6 copy.67.w_enc
  10.8 1.0 reshape.55
  11.8 0.7 pad_select_fusion.pred
  12.5 1.7 copy.68.w_pred
  14.2 1.8 copy.66.w_qkv
  16.0 57.1 %shard_map.373 = (bf16[2688,512]{1,0:T(8,128)(2,1)}, bf16[3584,512]{1,0:T(8,128)(2,1)}, bf16[2688,512]{1,0:T(8,128)(2,1)}, bf16[640,768]{1,0:T(8,128)(2,1)}, bf1...) custom-call(bf16[2,64,512]{2,1,0:T(8,128)(2,1)} %x_ref.1, ...), custom_call_target="tpu_custom_call" | custom-call | tf_op jit(solution)/shard_map/pallas_call | solution.py:1164
  73.1 47.5 %shard_map.374 = (bf16[2,64,640]{2,1,0:T(8,128)(2,1)}, f32[128,640]{1,0:T(8,128)}, bf16[1920,512]{1,0:T(8,128)(2,1)}, bf16[640,256]{1,0:T(8,128)(2,1)}, f32[16,256]{1,0:T(8,128)}, /*index=5*/f32[8,128]{1,0:T(8,128)}) custom-call(bf16[2,64,640]{2,1,0:T(8,128)(2,1)} %get-tuple-element.54.enc_own, bf16[128,768]{1,0:T(8,128)(2,1)} %pad_select_fusion.pred, ...), custom_call_target="tpu_custom_call" | custom-call | tf_op jit(solution)/shard_map/pallas_call | solution.py:792
  120.6 0.0 copy-start.6
  120.6 0.0 copy-start.3
  120.6 75.9 %shard_map.375 = (bf16[336,512]{1,0:T(8,128)(2,1)}, bf16[448,512]{1,0:T(8,128)(2,1)}, bf16[336,512]{1,0:T(8,128)(2,1)}, bf16[240,512]{1,0:T(8,128)(2,1)}, f32[2,64,512]{2,1,0:T(8,128)}) custom-call(bf16[2,64,640]{2,1,0:T(8,128)(2,1)} %get-tuple-element.60.refs_0_, s32[8,24]{1,0:T(8,128)} %pad_add_fusion.ints.refs_1_, f32[16,512]{1,0:T(8,128)} %get-tuple-element.61.refs_2_, ...), custom_call_target="tpu_custom_call" | custom-call | tf_op jit(solution)/shard_map/pallas_call | solution.py:1249
  196.5 0.0 copy-start.1
  196.5 0.0 copy-done.6
  196.5 0.7 slice.77
  197.2 1.3 slice.107
  198.5 0.7 slice.117
  199.2 0.7 slice.113
  199.9 1.6 fusion
  201.5 0.0 copy-done.3
  201.5 0.8 reshape.56
  202.4 0.0 copy-start.2
  202.4 1.1 convert_element_type.23
  203.5 0.7 slice_reduce_fusion
  204.2 0.5 slice_bitcast_fusion.6
  204.7 0.0 copy-start
  204.7 1.0 copy.69
  205.7 0.6 pad_maximum_fusion.1
  206.3 0.0 copy-done.1
  206.3 0.1 convert_element_type.25
  206.4 0.7 slice_bitcast_fusion.3
  207.1 0.8 copy.70
  208.0 0.0 copy-done.2
  208.0 0.0 copy-start.5
  208.0 0.0 copy-start.4
  208.0 0.8 pad_maximum_fusion
  208.8 0.7 maximum_bitcast_fusion
  209.5 0.0 copy-done
  209.5 0.9 slice.101
  210.3 0.1 convert_element_type.24
  210.5 0.8 slice_bitcast_fusion.1
  211.2 0.0 copy-done.5
  211.2 0.7 copy.75
  211.9 0.0 copy-done.4
  211.9 0.7 copy.76
  (7 shorter events, 0.1 us)
Async XLA Ops:
  120.6 75.9 %copy-start.6 = (f32[8,128]{1,0:T(8,128)S(1)}, f32[8,128]{1,0:T(8,128)}, u32[]{:S(2)}) copy-start(f32[8,128]{1,0:T(8,128)} %get-tuple-element.58) | copy-start | bytes 12292
  120.6 80.9 %copy-start.3 = (f32[128,640]{1,0:T(8,128)S(1)}, f32[128,640]{1,0:T(8,128)}, u32[]{:S(2)}) copy-start(f32[128,640]{1,0:T(8,128)} %get-tuple-element.82) | copy-start | bytes 983044
  196.5 9.8 %copy-start.1 = (bf16[336,512]{1,0:T(8,128)(2,1)S(1)}, bf16[336,512]{1,0:T(8,128)(2,1)}, u32[]{:S(2)}) copy-start(bf16[336,512]{1,0:T(8,128)(2,1)} %get-tuple-element.85) | copy-start | bytes 1032196
  202.4 5.6 %copy-start.2 = (bf16[240,512]{1,0:T(8,128)(2,1)S(1)}, bf16[240,512]{1,0:T(8,128)(2,1)}, u32[]{:S(2)}) copy-start(bf16[240,512]{1,0:T(8,128)(2,1)} %get-tuple-element.86) | copy-start | bytes 737284
  204.7 4.8 %copy-start = (bf16[448,512]{1,0:T(8,128)(2,1)S(1)}, bf16[448,512]{1,0:T(8,128)(2,1)}, u32[]{:S(2)}) copy-start(bf16[448,512]{1,0:T(8,128)(2,1)} %get-tuple-element.84) | copy-start | bytes 1376260
  208.0 3.3 %copy-start.5 = (bf16[2,64,512]{2,1,0:T(8,128)(2,1)S(1)}, bf16[2,64,512]{2,1,0:T(8,128)(2,1)}, u32[]{:S(2)}) copy-start(bf16[2,64,512]{2,1,0:T(8,128)(2,1)} %get-tuple-element.182) | copy-start | bytes 393220
  208.0 3.9 %copy-start.4 = (f32[2,64,512]{2,1,0:T(8,128)S(1)}, f32[2,64,512]{2,1,0:T(8,128)}, u32[]{:S(2)}) copy-start(f32[2,64,512]{2,1,0:T(8,128)} %get-tuple-element.183) | copy-start | bytes 786436

commit v2 on v1

--- a/solution.py
+++ b/solution.py
@@ -216,177 +216,187 @@
     )(*shards)
 
 
-class Scatter:
-    STAGES = 9
-
-    def __init__(self, where, grads, out, rows, bufs, send, recv):
-        self.w, self.grads, self.out, self.rows = where, grads, out, rows
-        self.held, self.xbuf, self.rbuf, self.final = bufs
+class Pair:
+    def __init__(self, where, grads, held, rows, send, recv):
+        self.w, self.grads, self.held, self.rows = where, grads, held, rows
         self.half = grads.shape[1] // 2
-        self.cut = x_rows(rows, SHARE_RS)
-        self.send, self.recv = send, recv
-        self.depth = where.n // 2 - 1
-        self.started = []
+        self.copy = remote(self.grads.at[:, self.lanes(1 - where.core)], held, send.at[0], recv.at[0], where.twin)
 
     def lanes(self, core):
         return pl.ds(pl.multiple_of(core * self.half, 128), self.half)
 
-    def rows_at(self, shard, offset, size):
-        return pl.ds(pl.multiple_of(shard * self.rows + offset, TILE), size)
-
-    def go(self, sem, src, dst, device):
-        copy = remote(src, dst, self.send.at[sem], self.recv.at[sem], device)
-        copy.start()
-        self.started.append(copy)
+    def give(self):
+        self.copy.start()
+
+    def add(self):
+        self.copy.wait_recv()
+
+        def body(i, _):
+            at = pl.ds(pl.multiple_of(i * self.rows, TILE), self.rows)
+            self.held[at, :] = (
+                self.held[at, :].astype(F32) + self.grads[at, self.lanes(self.w.core)].astype(F32)
+            ).astype(BF)
+            return 0
+
+        lax.fori_loop(0, self.w.n, body, 0)
+
+    def drain(self):
+        self.copy.wait_send()
+
+
+class Chain:
+    def __init__(self, pair, out, crossed, bufs, send, recv, share):
+        self.pair, self.w, self.out, self.crossed = pair, pair.w, out, crossed
+        self.cut = x_rows(pair.rows, share)
+        self.size = self.cut if crossed else pair.rows - 2 * self.cut
+        self.depth = self.w.n // 2 - 1
+        self.xbuf, self.rbuf = bufs
+        self.send, self.recv = send, recv
+        self.stages = self.depth + 5
+
+    def first(self, side):
+        return side * (self.pair.rows - self.cut) if self.crossed else self.cut
+
+    def rows_at(self, shard, side=None):
+        base = shard * self.pair.rows + self.first(self.w.side if side is None else side)
+        return pl.ds(pl.multiple_of(base, TILE), self.size)
+
+    def out_at(self, side=None):
+        at = pl.ds(pl.multiple_of(self.first(self.w.side if side is None else side), TILE), self.size)
+        return self.out.at[at, self.pair.lanes(self.w.core)]
 
     def got(self, sem, dst):
-        remote(dst, dst, self.send.at[sem], self.recv.at[sem], self.w.twin).wait_recv()
-
-    def mine(self, shard):
-        return self.held[self.rows_at(shard, self.w.side * self.cut, self.rows - self.cut), :].astype(F32)
+        remote(dst, dst, self.send.at[0], self.recv.at[sem], self.w.twin).wait_recv()
+
+    def ring(self, slot, src, device):
+        remote(src, self.rbuf.at[slot], self.send.at[1], self.recv.at[slot], device).start()
 
     def stage(self, s):
-        w, rows, cut, depth = self.w, self.rows, self.cut, self.depth
-        n, keep = w.n, self.rows - self.cut
+        if not self.size:
+            return
+        w, n, depth, held = self.w, self.w.n, self.depth, self.pair.held
+        last = 2 * depth + 1
         if s == 0:
-            self.go(0, self.grads.at[:, self.lanes(1 - w.core)], self.held, w.twin)
+            if self.crossed:
+                for i in range(n):
+                    remote(
+                        held.at[self.rows_at(i, 1 - w.side), :], self.xbuf.at[i], self.send.at[0], self.recv.at[last],
+                        w.across,
+                    ).start()
         elif s == 1:
-            self.got(0, self.held)
-
-            def add(i, _):
-                at = self.rows_at(i, 0, rows)
-                self.held[at, :] = (
-                    self.held[at, :].astype(F32) + self.grads[at, self.lanes(w.core)].astype(F32)
-                ).astype(BF)
-                return 0
-
-            lax.fori_loop(0, n, add, 0)
-            if cut:
-                for i in range(n):
-                    src = self.held.at[self.rows_at(i, (1 - w.side) * keep, cut), :]
-                    remote(src, self.xbuf.at[i], self.send.at[1], self.recv.at[1], w.across).start()
-        elif s == 2:
-            if cut:
-                self.got(1, self.xbuf)
-
-                def add(i, _):
-                    at = self.rows_at(i, w.side * keep, cut)
-                    self.held[at, :] = (
-                        self.held[at, :].astype(F32) + self.xbuf[i].astype(F32)
-                    ).astype(BF)
+            if self.crossed:
+                self.got(last, self.xbuf)
+
+                def body(i, _):
+                    at = self.rows_at(i)
+                    held[at, :] = (held[at, :].astype(F32) + self.xbuf[i].astype(F32)).astype(BF)
                     return 0
 
-                lax.fori_loop(0, n, add, 0)
+                lax.fori_loop(0, n, body, 0)
             dest = w.at((2 * w.core - 1) * (depth + 1))
-            src = self.held.at[self.rows_at(dest, w.side * cut, keep), :]
-            self.go(2, src, self.rbuf.at[2 * depth], w.far_back)
-        elif s < 3 + depth:
-            hop = s - 3
+            self.ring(2 * depth, held.at[self.rows_at(dest), :], w.far_back)
+        elif s < 2 + depth:
+            hop = s - 2
             for way in (0, 1):
                 sign = 1 - 2 * way
-                own = self.mine(w.at(sign * (depth - hop)))
+                own = held[self.rows_at(w.at(sign * (depth - hop))), :].astype(F32)
                 slot = 2 * hop + way
                 if hop == 0:
                     if way == 0:
-                        self.got(2, self.rbuf.at[2 * depth])
+                        self.got(2 * depth, self.rbuf.at[2 * depth])
                     far = self.rbuf[2 * depth].astype(F32)
                     pick = w.core if way == 0 else 1 - w.core
                     own = own + jnp.where(pick == 1, far, 0.0)
                     at = 2 * depth + 1 + way
                 else:
                     at = slot - 2
-                    self.got(3 + at, self.rbuf.at[at])
+                    self.got(at, self.rbuf.at[at])
                     own = own + self.rbuf[at].astype(F32)
                 self.rbuf[at] = own.astype(BF)
-                self.go(3 + slot, self.rbuf.at[at], self.rbuf.at[slot], w.right if way == 0 else w.left)
-        elif s == 3 + depth:
-            total = self.mine(w.dp)
+                self.ring(slot, self.rbuf.at[at], w.right if way == 0 else w.left)
+        elif s == 2 + depth:
+            total = held[self.rows_at(w.dp), :].astype(F32)
             for way in (0, 1):
                 at = 2 * depth - 2 + way
-                self.got(3 + at, self.rbuf.at[at])
+                self.got(at, self.rbuf.at[at])
                 total = total + self.rbuf[at].astype(F32)
-            self.final[0] = total.astype(BF)
-            self.go(3 + 2 * depth, self.final.at[0], self.final.at[1], w.across)
+            if self.crossed:
+                mine = self.out_at()
+                mine[...] = total.astype(BF)
+                remote(mine, mine, self.send.at[2], self.recv.at[last + 1], w.across).start()
+                remote(mine, mine, self.send.at[3], self.recv.at[last + 2], w.twin).start()
+            else:
+                self.xbuf[0] = total.astype(BF)
+                remote(self.xbuf.at[0], self.xbuf.at[1], self.send.at[2], self.recv.at[last + 1], w.across).start()
+        elif s == 3 + depth:
+            if self.crossed:
+                other = self.out_at(1 - w.side)
+                self.got(last + 1, other)
+                remote(other, other, self.send.at[4], self.recv.at[last + 3], w.twin).start()
+            else:
+                self.got(last + 1, self.xbuf.at[1])
+                mine = self.out_at()
+                mine[...] = (self.xbuf[0].astype(F32) + self.xbuf[1].astype(F32)).astype(BF)
+                remote(mine, mine, self.send.at[3], self.recv.at[last + 2], w.twin).start()
         elif s == 4 + depth:
-            self.got(3 + 2 * depth, self.final.at[1])
-            lanes = self.lanes(w.core)
-            own, other = self.final[0].astype(F32), self.final[1].astype(F32)
-            if cut:
-                first = w.side == 0
-                low, high = jnp.where(first, own, other), jnp.where(first, other, own)
-                self.out[:cut, lanes] = low[:cut].astype(BF)
-                if keep > cut:
-                    self.out[cut:keep, lanes] = (low[cut:] + high[: keep - cut]).astype(BF)
-                self.out[keep:, lanes] = high[keep - cut :].astype(BF)
-            else:
-                self.out[:, lanes] = (own + other).astype(BF)
-            part = self.out.at[:, lanes]
-            self.go(4 + 2 * depth, part, part, w.twin)
-        elif s == 5 + depth:
-            self.got(4 + 2 * depth, self.out.at[:, self.lanes(1 - w.core)])
+            part = self.out_at()
+            self.got(last + 2, part)
+            if self.crossed:
+                self.got(last + 3, part)
 
     def drain(self):
-        for copy in self.started:
-            copy.wait_send()
-        if self.cut:
-            remote(self.xbuf, self.xbuf, self.send.at[1], self.recv.at[1], self.w.across).wait_send()
-
-
-SHARE_RS = 0.25
-
-
-def scatter_scratch(n, rows, width, k_index=None):
-    half, cut, depth = width // 2, x_rows(rows, SHARE_RS), n // 2 - 1
-    return [
-        pltpu.VMEM((n * rows, half), BF),
-        pltpu.VMEM((n, max(cut, TILE), half), BF),
-        pltpu.VMEM((2 * depth + 3, rows - cut, half), BF),
-        pltpu.VMEM((2, rows - cut, half), BF),
-    ]
+        if not self.size:
+            return
+        ring = self.rbuf.at[pl.ds(0, 2 * self.depth + 1)]
+        remote(ring, ring, self.send.at[1], self.recv.at[0], self.w.twin).wait_send()
+        part = self.out_at()
+        remote(part, part, self.send.at[2], self.recv.at[0], self.w.twin).wait_send()
+        remote(part, part, self.send.at[3], self.recv.at[0], self.w.twin).wait_send()
+        if self.crossed:
+            remote(part, part, self.send.at[4], self.recv.at[0], self.w.twin).wait_send()
+            remote(self.xbuf, self.xbuf, self.send.at[0], self.recv.at[0], self.w.twin).wait_send()
+
+
+def scatter_scratch(n, rows, width, share):
+    half, cut, depth = width // 2, x_rows(rows, share), n // 2 - 1
+    out = [pltpu.VMEM((n * rows, half), BF)]
+    for count, size in ((2, rows - 2 * cut), (n, cut)):
+        out += [pltpu.VMEM((count, max(size, TILE), half), BF), pltpu.VMEM((2 * depth + 3, max(size, TILE), half), BF)]
+    return out
 
 
 def scatter_sems(n, k):
-    return [pltpu.SemaphoreType.DMA((k, n + 3)), pltpu.SemaphoreType.DMA((k, n + 3))]
-
-
-def scatter_kernel(n, rows_list, skew, *refs):
-    k = len(rows_list)
-    grads, outs = refs[:k], refs[k : 2 * k]
-    bufs = refs[2 * k : 2 * k + 4 * k]
-    send, recv = refs[6 * k :]
-    w = Where(n)
-    w.far_back = (ring_device(w.place + 2 * w.core - 1, n), w.lab)
-    w.greet()
-    parts = [
-        Scatter(w, grads[i], outs[i], rows_list[i], bufs[4 * i : 4 * i + 4], send.at[i], recv.at[i])
-        for i in range(k)
-    ]
-    stages = n // 2 + 5
-    for tick in range(k + skew * (stages - 1)):
-        for s in range(stages - 1, -1, -1):
-            g = tick - skew * s
-            if 0 <= g < k:
-                parts[g].stage(s)
+    return [pltpu.SemaphoreType.DMA((k, 11)), pltpu.SemaphoreType.DMA((k, 2 * n + 8))]
+
+
+class Scatter:
+    def __init__(self, where, grads, out, rows, bufs, send, recv, share):
+        n = where.n
+        self.pair = Pair(where, grads, bufs[0], rows, send.at[pl.ds(10, 1)], recv.at[pl.ds(2 * n + 7, 1)])
+        self.straight = Chain(self.pair, out, False, bufs[1:3], send.at[pl.ds(0, 5)], recv.at[pl.ds(0, n + 2)], share)
+        self.crossed = Chain(self.pair, out, True, bufs[3:5], send.at[pl.ds(5, 5)], recv.at[pl.ds(n + 2, n + 3)], share)
+
+    def drain(self):
+        for part in (self.pair, self.straight, self.crossed):
+            part.drain()
+
+
+def sum_up(parts, work, order):
+    depth = parts[0].straight.depth
+    for what, g, stage in order:
+        part = parts[g]
+        if what == 0:
+            work(g)
+            part.pair.give()
+        elif what == 1:
+            part.pair.add()
+        else:
+            chain = part.straight if what == 2 else part.crossed
+            stages = [stage] if stage < 4 else range(4, depth + 2) if stage == 4 else [stage + depth - 3]
+            for s in stages:
+                chain.stage(s)
     for part in parts:
         part.drain()
-
-
-def scatter_all(n, grads, skew=1):
-    k = len(grads)
-    rows_list = [g.shape[0] // n for g in grads]
-    scratch = []
-    for g, rows in zip(grads, rows_list):
-        scratch += scatter_scratch(n, rows, g.shape[1])
-    return pl.pallas_call(
-        functools.partial(scatter_kernel, n, rows_list, skew),
-        out_shape=[jax.ShapeDtypeStruct((rows, g.shape[1]), BF) for g, rows in zip(grads, rows_list)],
-        in_specs=[pl.BlockSpec(memory_space=pltpu.VMEM)] * k,
-        out_specs=[pl.BlockSpec(memory_space=pltpu.VMEM)] * k,
-        scratch_shapes=scratch + scatter_sems(n, k),
-        compiler_params=pltpu.CompilerParams(
-            collective_id=1, has_side_effects=True, vmem_limit_bytes=60 * 2**20
-        ),
-    )(*grads)
 
 
 LOW = -100000.0
@@ -438,10 +448,10 @@
     return out
 
 
-def scalar_ends(ints, r, segs):
+def scalar_ends(lengths, r, segs):
     ends, total = [], 0
     for s in range(segs):
-        total = total + ints[r, s]
+        total = total + lengths[s, r]
         ends.append(total)
     return ends
 
@@ -451,14 +461,14 @@
     return top, functools.reduce(jnp.add, [jnp.exp(v - top) for v in terms])
 
 
-def lattice(peers, ints, terms, skewed, hist, grads, loss, dims):
+def lattice(peers, lengths, counts, terms, skewed, hist, grads, loss, dims):
     frames, rows, segs, own_u, labs = dims
     wide = (frames, 128)
     lane = lane_ids(wide)
     group = rows * own_u
     j, row, u = lane % own_u, (lane % group) // own_u, (lane // group) * own_u + lane % own_u
     t = row_ids(wide)
-    all_ends = [scalar_ends(ints, r, segs) for r in range(rows)]
+    all_ends = [scalar_ends(lengths, r, segs) for r in range(rows)]
 
     def per_lane(values):
         out = jnp.zeros(wide, jnp.int32)
@@ -467,7 +477,7 @@
         return out
 
     ends = [per_lane([all_ends[r][s] for r in range(rows)]) for s in range(segs)]
-    labels_in = [per_lane([ints[r, segs + s] for r in range(rows)]) for s in range(segs)]
+    labels_in = [per_lane([counts[s, r] for r in range(rows)]) for s in range(segs)]
     seg = seg_of(t, ends)
     stop = pick(seg, ends)
     begin = pick(seg, [jnp.zeros(wide, jnp.int32)] + ends[:-1])
@@ -616,10 +626,10 @@
 
 def joint_kernel(
     dims,
-    enc_own, pred, ints, predx, tok, tail, bias,
+    enc_own, predictor, lengths, counts, labels, predx, tok, tail, bias_out,
     g_enc, g_predictor, g_pack, g_mix, g_bias, loss,
-    enc_all, proj, hid, slope, prob, prob_tail, mine, terms, skewed, hist, grads, g_pred, part, came,
-    send, recv,
+    enc_all, pred_wide, pred, proj, hid, slope, wide, back_w, prob, prob_tail, mine, terms, skewed, hist, grads, g_pred,
+    part, came, send, recv,
 ):
     frames, rows, segs, own_u, labs = dims
     micro = rows // labs
@@ -638,7 +648,30 @@
     for j in range(1, labs):
         enc_copy(j, peers.lab).start()
     enc_all[own_rows] = enc_own[...]
+    features = predictor.shape[-1]
+    for r in range(rows):
+        for s in range(segs):
+            first = (r * segs + s) * own_u
+            pred_wide[first : first + own_u, :] = predictor[r, s].astype(F32)
+    pred[:, :features] = pred_wide[...].astype(BF)
+    pred[:, features:] = (lane_ids((pred.shape[0], 128)) == BIAS_LANE).astype(BF)
     proj[...] = mm_t(pred[...], predx[...])
+    wide[:width, :TOK] = tok[...]
+    wide[:width, TOK:VOCAB] = tail[...]
+    top_row = row_ids((128, TOK)) == 0
+    wide[width:, :TOK] = jnp.where(top_row, bias_out[:, :TOK].astype(F32), 0.0).astype(BF)
+    mine[:, :128] = jnp.zeros((frames, 128), F32)
+    mine[:1, : bias_out.shape[1] - TOK] = bias_out[:, TOK:].astype(F32)
+    wide[width:, TOK:VOCAB] = jnp.where(row_ids((128, 128)) == 0, mine[:1, :128], 0.0).astype(BF)
+    lane_1 = lane_ids((1, 128))
+    wanted = jnp.zeros((1, 128), jnp.int32)
+    for r in range(rows):
+        for s in range(segs):
+            for u in range(own_u):
+                wanted = jnp.where(lane_1 == (r * segs + s) * own_u + u, labels[s, u, r], wanted)
+    wide[:, VOCAB:] = mm(wide[:, :TOK], (row_ids((TOK, 128)) == wanted).astype(BF)).astype(BF)
+    back_w[...] = wide[:width, :VOCAB].astype(F32).T.astype(BF)
+    hid[:, :, width:] = (lane_ids((rows, span, 128)) == 0).astype(BF)
     lane_t = lane_ids((frames, 128))
     lane_w = lane_ids((frames, TOK))
     group = rows * own_u
@@ -647,27 +680,24 @@
     def row_of(k):
         return peers.owner(k // micro) * micro + k % micro
 
-    def forward(k, _):
-        for j in range(1, labs):
-            @pl.when(k == j * micro)
-            def _():
-                enc_copy(j, peers.owner(j)).wait_recv()
+    def forward(k):
         r = row_of(k)
-        seg = seg_of(row_ids((frames, width)), scalar_ends(ints, r, segs))
+        ends = scalar_ends(lengths, r, segs)
+        seg = seg_of(row_ids((frames, width)), ends)
         enc = enc_all[r].astype(F32)
         for u in range(own_u):
+            at = slice(u * frames, (u + 1) * frames)
             per_frame = pick(
                 seg, [proj[pl.ds(r * segs * own_u + s * own_u + u, 1), :] for s in range(segs)]
             )
             value = jnp.tanh(enc + per_frame)
-            hid[r, u * frames : (u + 1) * frames, :] = value.astype(BF)
-            slope[r, u * frames : (u + 1) * frames, :] = (1.0 - value * value).astype(BF)
-        h = hid[r]
-        end = mm(h, tail[...]) + bias[:, TOK:]
-        wide = mm(h, tok[...]) + bias[:, :TOK]
-        seg_l = seg_of(row_ids((frames, TOK)), scalar_ends(ints, r, segs))
+            hid[r, at, :width] = value.astype(BF)
+            slope[r, at, :] = (1.0 - value * value).astype(BF)
+        logits = mm(hid[r], wide[...])
+        seg_l = seg_of(row_ids((frames, 128)), ends)
         for u in range(own_u):
-            logit, last = wide[u * frames : (u + 1) * frames], end[u * frames : (u + 1) * frames]
+            at = slice(u * frames, (u + 1) * frames)
+            logit, last, named = logits[at, :TOK], logits[at, TOK:VOCAB], logits[at, VOCAB:]
             top = jnp.maximum(jnp.max(logit, axis=1, keepdims=True), last[:, 0:1])
             top_dur = jnp.max(
                 jnp.where((lane_t >= 1) & (lane_t <= 5), last, -jnp.inf), axis=1, keepdims=True
@@ -679,21 +709,33 @@
             e = jnp.exp(logit - top)
             total = jnp.sum(e, axis=1, keepdims=True) + e_last[:, 0:1]
             total_dur = jnp.sum(jnp.where(is_tok, 0.0, e_last), axis=1, keepdims=True)
-            prob[r, u * frames : (u + 1) * frames, :] = (e * (1.0 / total)).astype(BF)
-            prob_tail[r, u * frames : (u + 1) * frames, :] = e_last * (1.0 / jnp.where(is_tok, total, total_dur))
+            prob[r, at, :TOK] = e.astype(BF)
+            over = 1.0 / total
+            prob_tail[r, at, :] = jnp.where(lane_t == 6, over, e_last * jnp.where(is_tok, over, 1.0 / total_dur))
             norm_tok, norm_dur = top + jnp.log(total), top_dur + jnp.log(total_dur)
-            label = pick(seg_l, [ints[r, 2 * segs + s * own_u + u] for s in range(segs)])
-            at_label = jnp.sum(jnp.where(lane_w == label, logit, 0.0), axis=1, keepdims=True) - norm_tok
+            column = r * segs * own_u + seg_l * own_u + u
+            at_label = jnp.sum(jnp.where(lane_t == column, named, 0.0), axis=1, keepdims=True) - norm_tok
             lp = last - jnp.where(is_tok, norm_tok, norm_dur)
-            for kind in range(KINDS):
-                column = at_label if kind == 6 else lp[:, kind : kind + 1]
-                cols = slice((kind // per_vreg) * 128, (kind // per_vreg) * 128 + 128)
-                place = (kind % per_vreg) * group + r * own_u + u
-                mine[:, cols] = jnp.where(lane_t == place, column, mine[:, cols])
+            for half in range(2):
+                cols = slice(half * 128, half * 128 + 128)
+                value = mine[:, cols]
+                for kind in range(half * per_vreg, min(KINDS, (half + 1) * per_vreg)):
+                    column = at_label if kind == 6 else lp[:, kind : kind + 1]
+                    value = jnp.where(lane_t == (kind % per_vreg) * group + r * own_u + u, column, value)
+                mine[:, cols] = value
+
+    mine[...] = jnp.zeros(mine.shape, F32)
+
+    def forward_step(i, _):
+        for j in range(1, labs):
+            @pl.when(i * STEP == j * micro)
+            def _():
+                enc_copy(j, peers.owner(j)).wait_recv()
+        for k in range(STEP):
+            forward(i * STEP + k)
         return 0
 
-    mine[...] = jnp.zeros(mine.shape, F32)
-    lax.fori_loop(0, rows, forward, 0)
+    lax.fori_loop(0, rows // STEP, forward_step, 0)
     terms[peers.lab] = mine[...]
 
     def term_copy(j, source):
@@ -703,68 +745,68 @@
         term_copy(j, peers.lab).start()
     for j in range(1, labs):
         term_copy(j, peers.owner(j)).wait_recv()
-    lattice(peers, ints, terms, skewed, hist, grads, loss, dims)
+    lattice(peers, lengths, counts, terms, skewed, hist, grads, loss, dims)
 
     def part_copy(j):
         return remote(part.at[j], came.at[j], send.at[2, j], recv.at[2, j], peers.device(j))
 
-    def backward(i, sums):
-        k = rows - 1 - i
+    def backward(k):
         r = row_of(k)
+        ends = scalar_ends(lengths, r, segs)
         shift = (256 - peers.lab * group - r * own_u) % 128
         rolled = [pltpu.roll(grads[kind], shift, 1) for kind in range(KINDS)]
-        seg_l = seg_of(row_ids((frames, TOK)), scalar_ends(ints, r, segs))
-        sum_tok, sum_tail = sums
+        seg_l = seg_of(row_ids((frames, TOK)), ends)
         for u in range(own_u):
             at = slice(u * frames, (u + 1) * frames)
             a, b = rolled[6][:, u : u + 1], rolled[0][:, u : u + 1]
             both = a + b
-            label = pick(seg_l, [ints[r, 2 * segs + s * own_u + u] for s in range(segs)])
-            g = (jnp.where(lane_w == label, a, 0.0) - prob[r, at, :].astype(F32) * both).astype(BF)
-            prob[r, at, :] = g
+            label = pick(seg_l, [labels[s, u, r] for s in range(segs)])
+            tails = prob_tail[r, at, :]
+            scaled = both * tails[:, 6:7]
+            prob[r, at, :TOK] = (jnp.where(lane_w == label, a, 0.0) - prob[r, at, :TOK].astype(F32) * scaled).astype(BF)
             aim = jnp.zeros((frames, 128), F32)
             for kind in range(6):
                 aim = jnp.where(lane_t == kind, rolled[kind][:, u : u + 1], aim)
-            gt = (aim - prob_tail[r, at, :] * both).astype(BF)
-            prob_tail[r, at, :] = gt.astype(F32)
-            sum_tok = sum_tok + jnp.sum(g.astype(F32).reshape(frames // 8, 8, TOK), axis=0)
-            sum_tail = sum_tail + jnp.sum(gt.astype(F32).reshape(frames // 8, 8, 128), axis=0)
-        back = mm_t(prob[r], tok[...]) + mm_t(prob_tail[r].astype(BF), tail[...])
-        back = back * slope[r].astype(F32)
+            prob[r, at, TOK:] = jnp.where(lane_t < 6, aim - tails * both, 0.0).astype(BF)
+        back = mm(prob[r], back_w[...]) * slope[r].astype(F32)
         summed = back[:frames]
         for u in range(1, own_u):
             summed = summed + back[u * frames : (u + 1) * frames]
         part[k // micro, k % micro] = summed.astype(BF)
         shape = (segs * own_u, span)
         lanes = lane_ids(shape)
-        seg_t = seg_of(lanes % frames, scalar_ends(ints, r, segs))
+        seg_t = seg_of(lanes % frames, ends)
         hit = (row_ids(shape) == seg_t * own_u + lanes // frames).astype(BF)
         g_pred[pl.ds(r * segs * own_u, segs * own_u), :] = mm(hit, back.astype(BF)).astype(BF)
+
+    def backward_step(i, _):
+        first = rows - (i + 1) * STEP
+        for k in range(STEP - 1, -1, -1):
+            backward(first + k)
         for j in range(1, labs):
-            @pl.when(k == j * micro)
+            @pl.when(first == j * micro)
             def _():
                 part_copy(j).start()
-        return sum_tok, sum_tail
-
-    zero = (jnp.zeros((8, TOK), F32), jnp.zeros((8, 128), F32))
-    sum_tok, sum_tail = lax.fori_loop(0, rows, backward, zero)
-    sum_tok = jnp.sum(sum_tok, axis=0, keepdims=True).astype(BF)
-    sum_tail = jnp.sum(sum_tail, axis=0, keepdims=True).astype(BF)
-    g_bias[...] = jnp.zeros(g_bias.shape, F32)
-    for i in range(4):
-        g_bias[i : i + 1, :] = sum_tok[:, 256 * i : 256 * i + 256].astype(F32)
-    g_bias[4:5, :128] = sum_tail.astype(F32)
+        return 0
+
+    lax.fori_loop(0, rows // STEP, backward_step, 0)
     gp = g_pred[...]
-    g_predictor[...] = mm(gp, predx[:, : g_predictor.shape[1]])
+    g_predictor[...] = mm(gp, predx[:, :features])
     shards = lax.axis_size("dp")
     block = width // shards
-    h_all = hid[...].reshape(rows * span, width)
+    h_all = hid[...].reshape(rows * span, width + 128)
+    g_bias[...] = jnp.zeros(g_bias.shape, F32)
     from_pred = t_mm(gp, pred[...])
     for i in range(2):
-        piece = t_mm(h_all, prob[:, :, i * 512 : i * 512 + 512].reshape(rows * span, 512)).astype(BF)
+        piece = t_mm(h_all, prob[:, :, i * 512 : i * 512 + 512].reshape(rows * span, 512))
+        for q in range(2):
+            g_bias[2 * i + q : 2 * i + q + 1, :] = piece[width : width + 1, 256 * q : 256 * q + 256]
         for d in range(shards):
-            g_pack[d * 3 * block + (i + 1) * block : d * 3 * block + (i + 2) * block, :] = piece[d * block : (d + 1) * block]
-    ends_w = t_mm(h_all, prob_tail[...].reshape(rows * span, 128).astype(BF)) + from_pred[:, 640:768]
+            first = d * 3 * block + (i + 1) * block
+            g_pack[first : first + block, :] = piece[d * block : (d + 1) * block].astype(BF)
+    ends_w = t_mm(h_all, prob[:, :, TOK:].reshape(rows * span, 128))
+    g_bias[4:5, :128] = ends_w[width : width + 1]
+    ends_w = ends_w[:width] + from_pred[:, 640:768]
     for d in range(shards):
         at = slice(d * block, (d + 1) * block)
         g_pack[d * 3 * block : d * 3 * block + block, :] = from_pred[at, :512].astype(BF)
@@ -782,7 +824,11 @@
         part_copy(j).wait_send()
 
 
-def joint_call(enc_own, pred, ints, predx, tok, tail, bias, dims):
+VOCAB = TOK + 128
+STEP = 2
+
+
+def joint_call(enc_own, predictor, ints, predx, tok, tail, bias_out, dims):
     frames, rows, segs, own_u, labs = dims
     width = enc_own.shape[-1]
     span = own_u * frames
@@ -799,14 +845,18 @@
             jax.ShapeDtypeStruct((16, 256), F32),
             jax.ShapeDtypeStruct((8, 128), F32),
         ],
-        in_specs=[vm, vm, sm, vm, vm, vm, vm],
+        in_specs=[vm, vm, sm, sm, sm, vm, vm, vm, vm],
         out_specs=[vm] * 6,
         scratch_shapes=[
             pltpu.VMEM((rows, frames, width), BF),
+            pltpu.VMEM((rows * segs * own_u, 640), F32),
+            pltpu.VMEM((rows * segs * own_u, 768), BF),
             pltpu.VMEM((rows * segs * own_u, width), F32),
+            pltpu.VMEM((rows, span, width + 128), BF),
             pltpu.VMEM((rows, span, width), BF),
-            pltpu.VMEM((rows, span, width), BF),
-            pltpu.VMEM((rows, span, TOK), BF),
+            pltpu.VMEM((width + 128, VOCAB + 128), BF),
+            pltpu.VMEM((VOCAB, width), BF),
+            pltpu.VMEM((rows, span, VOCAB), BF),
             pltpu.VMEM((rows, span, 128), F32),
             pltpu.VMEM((frames, 256), F32),
             pltpu.VMEM((labs, frames, 256), F32),
@@ -822,7 +872,7 @@
         compiler_params=pltpu.CompilerParams(
             collective_id=2, has_side_effects=True, vmem_limit_bytes=60 * 2**20
         ),
-    )(enc_own, pred, ints, predx, tok, tail, bias)
+    )(enc_own, predictor, *ints, predx, tok, tail, bias_out)
 
 
 HEADS = 8
@@ -941,10 +991,11 @@
         at = slice(part * half * z.ff, (part + 1) * half * z.ff)
         st["act"][:, at] = (pre * sg).astype(BF)
         st["slope"][:, at] = (sg * (1.0 + pre * (1.0 - sg))).astype(BF)
-    yield
+        yield
     after_ffn = x + 0.5 * mm(st["act"][...], rows_of(full[1], n, 0, z.ff))
     att_in = norm(after_ffn, "n_att", 1).astype(BF)
     st["qkv"][...] = mm_t(att_in, rows_of(full[1], n, z.ff, z.qk)).astype(BF)
+    yield
     same = ids_r == ids_c
     low_half = lane_ids((count, 128)) < 64
     for pair in range(HEADS // 2):
@@ -1070,29 +1121,46 @@
     yield
 
 
+ORDER = (
+    (-2, 0), (-2, 1), (-1, 0), (1, 0), (0, 0), (-2, 2), (-1, 1), (0, 0), (-2, 3), (1, 1), (0, 0), (-1, 2), (0, 0), (-1, 3),
+    (1, 2), (0, 0), (1, 3),
+)
+
+
 def encode_kernel(
-    z, dims, x_ref, ints, w_in, w_out, w_qkv, w_att, w_pin, w_pout, w_enc, w_pred, tail, small_in, w_joint,
+    z, dims, x_ref, ints, w_in, w_out, w_qkv, w_att, w_pin, w_pout, w_enc, w_pred, w_joint, bias_joint, w_depth,
+    gain0, gain1, gain2, gain3, gain4,
     full0, full1, full2, predx, tok, tail_out, small_out, encoded, enc_proj, *rest,
 ):
     k = len(STATE)
     st = {name: ref for (name, _, _), ref in zip(STATE, rest[:k])}
     probs, rest = rest[k], rest[k + 1 :]
     sources, full = rest[0:4], rest[4:8]
-    ring_recv, x_recv, sems, out_sem = rest[8:]
+    small_in, tail, ring_recv, x_recv, sems, out_sem = rest[8:]
     n = z.n
     w = Where(n)
     w.greet()
-    jr, js, ds = z.jr, w_pred.shape[1], z.ds
+    jr, js, ds = z.jr, w_pred.shape[0], z.ds
+    small_in[...] = jnp.zeros(small_in.shape, F32)
+    small_in[:TAPS, :ds] = w_depth[...].astype(F32)
+    for i, gain in enumerate((gain0, gain1, gain2, gain3, gain4)):
+        small_in[GAIN_ROW + i : GAIN_ROW + i + 1, :ds] = gain[...].astype(F32)
+    tail[...] = jnp.zeros(tail.shape, F32)
+    tail[:1, :js] = bias_joint[...].astype(F32)
+    column = tail[:8, :].T[:jr, :1]
+    tail[:8, :] = jnp.zeros((8, 128), F32)
+    tail[:js, : w_joint.shape[1] - 1024] = w_joint[:, 1024:].astype(F32)
+    tail[...] = jnp.where(lane_ids((jr, 128)) == BIAS_LANE, column, tail[...])
 
     def down(value, count):
         return jnp.concatenate([value, jnp.zeros((count - value.shape[0],) + value.shape[1:], value.dtype)], 0) if count > value.shape[0] else value
 
-    pred_t = down(w_pred[...].astype(F32).T.astype(BF), jr)
+    pred_t = down(w_pred[...], jr)
     sources[0][jr:, :] = w_in[...].astype(F32).T.astype(BF)
     sources[0][:jr, 0:128] = pred_t[:, 512:]
-    sources[0][:jr, 128:256] = tail[...]
+    sources[0][:jr, 128:256] = tail[...].astype(BF)
     sources[0][:jr, 256:] = jnp.zeros((jr, 256), BF)
-    sources[0][:16, 256:384] = small_in[...]
+    sources[0][:16, 256:384] = small_in[...].astype(BF)
     parts = [
         Gather(w, sources[i], full[i], z.rows[i], ring_recv.at[i], x_recv.at[i], sems.at[i]) for i in range(4)
     ]
@@ -1102,42 +1170,38 @@
     def fill(g):
         if g == 1:
             sources[1][: z.ff, :] = w_out[...]
-            sources[1][z.ff :, :] = w_qkv[...].astype(F32).T.astype(BF)
+            sources[1][z.ff :, :] = w_qkv[...]
         elif g == 2:
             sources[2][:ds, :] = w_att[...]
             sources[2][ds : ds + z.pi, :] = w_pin[...].astype(F32).T.astype(BF)
             sources[2][ds + z.pi : 2 * ds + z.pi, :] = w_pout[...]
-            sources[2][2 * ds + z.pi :, :] = down(w_enc[...].astype(F32).T.astype(BF), jr)
+            sources[2][2 * ds + z.pi :, :] = down(w_enc[...], jr)
         elif g == 3:
             sources[3][:jr, :] = pred_t[:, :512]
             sources[3][jr : 2 * jr, :] = down(w_joint[:, :512], jr)
             sources[3][2 * jr :, :] = down(w_joint[:, 512:1024], jr)
 
-    def tick(i):
-        for s in range(turns - 1, -1, -1):
-            g = i - skew * s
-            if 0 <= g < 4:
-                if s == 0:
-                    fill(g)
-                parts[g].step(s)
-
     outs = (full0, full1, full2)
+    compute = forward_pieces(z, x_ref, ints, dims, full, small_out, st, probs, encoded, enc_proj)
 
     def finish(g):
         parts[g].whole()
         if g < 3:
             pltpu.make_async_copy(full[g], outs[g], out_sem.at[g]).start()
 
-    last = 4 + skew * (turns - 1)
-    compute = forward_pieces(z, x_ref, ints, dims, full, small_out, st, probs, encoded, enc_proj)
-    done = 0
-    for i in range(last):
-        tick(i)
-        g = i - skew * (turns - 1)
-        if g >= 0:
+    for s in range(turns - 2):
+        for g in range(4):
+            if s == 0:
+                fill(g)
+            parts[g].step(s)
+    for what, g in ORDER:
+        if what == 0:
+            next(compute)
+        elif what == 1:
             finish(g)
-            if g < 3:
-                next(compute)
+        else:
+            parts[g].step(turns + what)
+
     predx[:, :512] = rows_of(full[3], n, 0, jr)
     tok[:, :512] = rows_of(full[3], n, jr, jr)
     tok[:, 512:] = rows_of(full[3], n, 2 * jr, jr)
@@ -1150,7 +1214,7 @@
         pltpu.make_async_copy(full[g], outs[g], out_sem.at[g]).wait()
 
 
-def encode_call(z, dims, x, ints, w_in, w_out, w_qkv, w_att, w_pin, w_pout, w_enc, w_pred, tail, small, w_joint):
+def encode_call(z, dims, x, lengths, *params):
     frames, rows, segs, own_u, labs = dims
     n, micro = z.n, rows // labs
     count, width = micro * frames, n * z.jr
@@ -1164,18 +1228,20 @@
     return pl.pallas_call(
         functools.partial(encode_kernel, z, dims),
         out_shape=outs,
-        in_specs=[vm, sm] + [vm] * 11,
+        in_specs=[vm, sm] + [vm] * len(params),
         out_specs=[hbm] * 3 + [vm] * (len(outs) - 3),
         scratch_shapes=[pltpu.VMEM((r, 512), BF) for r in z.rows]
         + [pltpu.VMEM((n * r, 512), BF) for r in z.rows]
         + [
+            pltpu.VMEM((16, 128), F32),
+            pltpu.VMEM((z.jr, 128), F32),
             pltpu.SemaphoreType.DMA((4, n - 1)),
             pltpu.SemaphoreType.DMA((4, n - 1)),
             pltpu.SemaphoreType.DMA((4, 5)),
             pltpu.SemaphoreType.DMA((3,)),
         ],
         compiler_params=pltpu.CompilerParams(collective_id=0, has_side_effects=True, vmem_limit_bytes=60 * 2**20),
-    )(x, ints, w_in, w_out, w_qkv, w_att, w_pin, w_pout, w_enc, w_pred, tail, small, w_joint)
+    )(x, lengths, *params)
 
 
 def grad_kernel(z, dims, skew, *refs):
@@ -1188,7 +1254,7 @@
     outs, grad_frames, refs = refs[:4], refs[4], refs[5:]
     full, refs = refs[:3], refs[3:]
     grads, refs = list(refs[:3]) + [g_pack], refs[3:]
-    small_grad, bufs, (send, recv, in_sem) = refs[0], refs[1:17], refs[17:]
+    small_grad, bufs, (send, recv, in_sem) = refs[0], refs[1:21], refs[21:]
     n = z.n
     w = Where(n)
     w.far_back = (ring_device(w.place + 2 * w.core - 1, n), w.lab)
@@ -1197,9 +1263,9 @@
     w.greet()
     order = (3, 2, 1, 0)
     parts = [
-        Scatter(w, grads[g], outs[g], z.rows[g], bufs[4 * g : 4 * g + 4], send.at[g], recv.at[g]) for g in order
+        Scatter(w, grads[g], outs[g], z.rows[g], bufs[5 * g : 5 * g + 5], send.at[g], recv.at[g], SHARES[3 - g])
+        for g in order
     ]
-    stages = n // 2 + 5
     compute = backward_pieces(z, g_enc, ints, dims, full, small_ref, st, probs, grads, small_grad, grad_frames)
 
     def load(g):
@@ -1227,15 +1293,19 @@
                 grads[0][at : at + 16, 384:] = jnp.zeros((16, 128), BF)
                 grads[0][at + 16 : at + 32, 256:] = g_bias[...].astype(BF)
 
-    for tick in range(4 + skew * (stages - 1)):
-        for s in range(stages - 1, -1, -1):
-            g = tick - skew * s
-            if 0 <= g < 4:
-                if s == 0:
-                    work(g)
-                parts[g].stage(s)
-    for part in parts:
-        part.drain()
+    sum_up(parts, work, ORDER_SUMS)
+
+
+SHARES = (0.2, 0.2, 0.3, 0.25)
+ORDER_SUMS = (
+    (0, 0, 0), (0, 1, 0), (0, 2, 0), (1, 0, 0), (3, 0, 0), (2, 0, 1), (0, 3, 0), (1, 1, 0), (2, 1, 1), (2, 0, 2),
+    (3, 1, 0), (1, 2, 0), (2, 2, 1), (2, 1, 2), (1, 3, 0), (3, 2, 0), (3, 0, 1), (2, 0, 3), (2, 2, 2), (3, 3, 0),
+    (2, 3, 1), (2, 1, 3), (3, 0, 2), (3, 1, 1), (2, 0, 4), (2, 2, 3), (2, 3, 2), (2, 1, 4), (3, 0, 3), (3, 1, 2),
+    (2, 0, 5), (2, 2, 4), (3, 2, 1), (2, 3, 3), (2, 1, 5), (3, 0, 4), (3, 1, 3), (3, 3, 1), (2, 2, 5), (3, 2, 2),
+    (2, 0, 6), (2, 3, 4), (3, 0, 5), (2, 1, 6), (3, 3, 2), (2, 0, 7), (3, 1, 4), (3, 2, 3), (2, 2, 6), (3, 0, 6),
+    (2, 1, 7), (2, 3, 5), (3, 3, 3), (2, 2, 7), (3, 0, 7), (3, 1, 5), (3, 2, 4), (3, 3, 4), (2, 3, 6), (3, 1, 6),
+    (3, 2, 5), (3, 1, 7), (2, 3, 7), (3, 3, 5), (3, 2, 6), (3, 3, 6), (3, 2, 7), (3, 3, 7),
+)
 
 
 def grad_call(z, dims, g_enc, ints, small, g_pack, g_mix, g_bias, full, state, probs, skew=1):
@@ -1244,8 +1314,8 @@
     vm, sm, hbm = (pl.BlockSpec(memory_space=m) for m in (pltpu.VMEM, pltpu.SMEM, pl.ANY))
     shape = jax.ShapeDtypeStruct
     scratch = [pltpu.VMEM((n * z.rows[g], 512), BF) for g in range(3)] * 2 + [pltpu.VMEM((16, z.model), F32)]
-    for r in z.rows:
-        scratch += scatter_scratch(n, r, 512)
+    for g, r in enumerate(z.rows):
+        scratch += scatter_scratch(n, r, 512, SHARES[3 - g])
     return pl.pallas_call(
         functools.partial(grad_kernel, z, dims, skew),
         out_shape=[shape((r, 512), BF) for r in z.rows] + [shape((micro, frames, z.model), F32)],
@@ -1255,9 +1325,68 @@
         compiler_params=pltpu.CompilerParams(collective_id=1, has_side_effects=True, vmem_limit_bytes=60 * 2**20),
     )(g_enc, ints, small, g_pack, g_mix, g_bias, *full, *state, probs)
 
-def pad_to(value, rows, lanes):
-    return jnp.pad(value, ((0, rows - value.shape[0]), (0, lanes - value.shape[1])))
-
+
+def unpack_kernel(z, dims, js, own0, own1, own2, own3, grads, encoded, loss, g_predictor, *outs):
+    frames, rows, segs, own_u, labs = dims
+    ds, ff, pi, jr = z.ds, z.ff, z.pi, z.jr
+    (
+        loss_o, enc_o, grads_o, pred_o, gg0, g_in, g_out, gg1, g_qkv, g_att, gg2, g_pin, g_depth, gg3, g_pout, gg4,
+        g_enc, g_pred, g_bias, g_joint, g_bias_out,
+    ) = outs
+    hit = (row_ids((128, rows)) == lane_ids((128, rows)) * own_u).astype(F32)
+    loss_o[...] = lax.dot_general(
+        loss[...], hit, (((1,), (0,)), ((), ())), precision=lax.Precision.HIGHEST, preferred_element_type=F32
+    )[:segs]
+    enc_o[...] = encoded[...]
+    grads_o[...] = grads[...]
+    for r in range(rows):
+        for s in range(segs):
+            first = (r * segs + s) * own_u
+            pred_o[r, s] = g_predictor[first : first + own_u, :]
+    small = own0[:32, 256:].astype(F32)
+    for i, out in enumerate((gg0, gg1, gg2, gg3, gg4)):
+        out[...] = small[GAIN_ROW + i : GAIN_ROW + i + 1, :ds]
+    g_depth[...] = small[:TAPS, :ds]
+    for i in range(4):
+        g_bias_out[:, 256 * i : 256 * i + 256] = small[16 + i : 17 + i, :]
+    g_bias_out[:, 1024:] = small[20:21, : g_bias_out.shape[1] - 1024]
+    g_in[...] = own0[jr:, :].astype(F32).T
+    g_out[...] = own1[:ff, :].astype(F32)
+    g_qkv[...] = own1[ff:, :].astype(F32)
+    g_att[...] = own2[:ds, :].astype(F32)
+    g_pin[...] = own2[ds : ds + pi, :].astype(F32).T
+    g_pout[...] = own2[ds + pi : 2 * ds + pi, :].astype(F32)
+    g_enc[...] = own2[2 * ds + pi :, :].astype(F32)[:js]
+    g_pred[:, :512] = own3[:jr, :].astype(F32)[:js]
+    g_pred[:, 512:] = own0[:jr, :128].astype(F32)[:js]
+    tail = own0[:jr, 128:256].astype(F32)
+    wide = jnp.concatenate([tail, jnp.zeros((128 - jr, 128), F32)], axis=0) if jr < 128 else tail
+    g_bias[...] = wide.T[BIAS_LANE : BIAS_LANE + 1, :js]
+    g_joint[:, :512] = own3[jr : 2 * jr, :].astype(F32)[:js]
+    g_joint[:, 512:1024] = own3[2 * jr :, :].astype(F32)[:js]
+    g_joint[:, 1024:] = tail[:js, : g_joint.shape[1] - 1024]
+
+
+def unpack_call(z, dims, js, out_width, own, grads, encoded, loss, g_predictor):
+    frames, rows, segs, own_u, labs = dims
+    shape = jax.ShapeDtypeStruct
+    row = shape((1, z.ds), F32)
+    line, features = z.model, g_predictor.shape[1]
+    outs = [
+        shape((segs, rows), F32), shape(encoded.shape, BF), shape(grads.shape, F32),
+        shape((rows, segs, own_u, features), F32), row, shape((line, z.ff), F32), shape((z.ff, line), F32), row,
+        shape((z.qk, line), F32), shape((z.ds, line), F32), row, shape((line, z.pi), F32), shape((TAPS, z.ds), F32),
+        row, shape((z.ds, line), F32), row, shape((js, line), F32), shape((js, features), F32), shape((1, js), F32),
+        shape((js, out_width), F32), shape((1, out_width), F32),
+    ]
+    vm = pl.BlockSpec(memory_space=pltpu.VMEM)
+    return pl.pallas_call(
+        functools.partial(unpack_kernel, z, dims, js),
+        out_shape=outs,
+        in_specs=[vm] * 8,
+        out_specs=[vm] * len(outs),
+        compiler_params=pltpu.CompilerParams(vmem_limit_bytes=60 * 2**20),
+    )(*own, grads, encoded, loss, g_predictor)
 
 def local(
     frames_in, predictor, seg_lengths, label_counts, label_ids, gain_ffn, w_ffn_in, w_ffn_out, gain_att, w_qkv,
@@ -1271,37 +1400,25 @@
     jr = max(-(-js // TILE), 2) * TILE
     z = Sizes(n, ds, w_ffn_in.shape[1], w_qkv.shape[1], w_point_in.shape[1], jr)
     dims = (frames, rows, segs, own_u, labs)
-    tail = pad_to(jnp.concatenate([w_joint_out[:, TOK:], bias_joint[:, None]], axis=1), jr, 128)
-    gains = jnp.stack([gain_ffn, gain_att, gain_conv, gain_depth, gain_out])
-    small = pad_to(jnp.concatenate([w_depth, gains]), 16, 128)
-    ints = jnp.concatenate([seg_lengths, label_counts, label_ids.reshape(rows, segs * own_u)], axis=1)
+    lengths, counts, labels = seg_lengths.T, label_counts.T, label_ids.transpose(1, 2, 0)
+    gains = [g[None] for g in (gain_ffn, gain_att, gain_conv, gain_depth, gain_out)]
     out = encode_call(
-        z, dims, frames_in, ints, w_ffn_in, w_ffn_out, w_qkv, w_att_out, w_point_in, w_point_out, w_enc, w_pred,
-        tail, small, w_joint_out,
+        z, dims, frames_in, lengths, w_ffn_in, w_ffn_out, w_qkv.T, w_att_out, w_point_in, w_point_out, w_enc.T, w_pred.T,
+        w_joint_out, bias_joint[None], w_depth, *gains,
     )
     full, (predx, tok, tail_w, small_w, encoded, enc_proj) = out[:3], out[3:9]
     state, probs = out[9:-1], out[-1]
-    pred_ext = pad_to(predictor.reshape(-1, joint), rows * segs * own_u, 768)
-    pred_ext = jnp.where(lax.broadcasted_iota(jnp.int32, pred_ext.shape, 1) == joint + BIAS_LANE, 1.0, pred_ext).astype(BF)
-    bias = jnp.pad(bias_out.astype(F32), (0, TOK + 128 - bias_out.shape[0]))[None]
     g_enc, g_predictor, g_pack, g_mix, g_bias, loss = joint_call(
-        enc_proj, pred_ext, ints, predx, tok, tail_w, bias, dims
+        enc_proj, predictor, (lengths, counts, labels), predx, tok, tail_w, bias_out[None], dims
     )
-    own0, own1, own2, own3, grad_frames = grad_call(
-        z, dims, g_enc, ints, small_w, g_pack, g_mix, g_bias, full, state, probs
-    )
-    ff, pi = z.ff, z.pi
-    own0, own1, own2, own3 = (g.astype(F32) for g in (own0, own1, own2, own3))
-    g_small = own0[:16, 256 : 256 + ds]
-    g_pred_t = jnp.concatenate([own3[:js], own0[:js, :128]], axis=1)
-    g_joint = jnp.concatenate([own3[jr : jr + js], own3[2 * jr : 2 * jr + js], own0[:js, 128:134]], axis=1)
-    g_bias_out = jnp.concatenate([own0[16:20, 256:].reshape(-1), own0[20, 256:262]])
-    loss_out = loss[:segs, : rows * own_u : own_u].T
+    *own, grad_frames = grad_call(z, dims, g_enc, lengths, small_w, g_pack, g_mix, g_bias, full, state, probs)
+    (
+        loss, encoded, grad_frames, g_predictor, gg0, g_in, g_out, gg1, g_qkv, g_att, gg2, g_pin, g_depth, gg3, g_pout,
+        gg4, g_enc, g_pred, g_bias, g_joint, g_bias_out,
+    ) = unpack_call(z, dims, js, bias_out.shape[0], own, grad_frames, encoded, loss, g_predictor)
     return (
-        loss_out, encoded, grad_frames, g_predictor.reshape(predictor.shape),
-        g_small[9], own0[jr:].T, own1[:ff], g_small[10], own1[ff:].T, own2[:ds], g_small[11],
-        own2[ds : ds + pi].T, g_small[:9], g_small[12], own2[ds + pi : 2 * ds + pi], g_small[13],
-        own2[2 * ds + pi : 2 * ds + pi + js].T, g_pred_t.T, own0[:js, 128 + BIAS_LANE], g_joint, g_bias_out,
+        loss.T, encoded, grad_frames, g_predictor, gg0[0], g_in, g_out, gg1[0], g_qkv.T, g_att, gg2[0], g_pin, g_depth,
+        gg3[0], g_pout, gg4[0], g_enc.T, g_pred.T, g_bias[0], g_joint, g_bias_out[0],
     )
 
 

time: 213 us -> 173 us (0.81)
  local copies, waits for them, and re-layouts: 25.2 us -> 1.28 us
  Pallas kernels: 181 us -> 169 us
  other arithmetic: 6.07 us -> 1.31 us
    pallas_call x1, Pallas kernels: 75.9 us -> 65.2 us  [grad_call(): pl.pallas_call(functools.partial(grad_kernel, z, dims, skew), out_shape=[...]
    unnamed x26 -> x0, local copies, waits for them, and re-layouts: 9.93 us -> none
    slice x9 -> x0, local copies, waits for them, and re-layouts: 7.32 us -> none  [the longest x1 1.6 us: local(): own2[ds + pi:2 * ds + pi]]
    pallas_call x0 -> x1, Pallas kernels: none -> 3.47 us  [unpack_call(): pl.pallas_call(functools.partial(unpack_kernel, z, dims, js), out_shape=o...]
    pallas_call x1, Pallas kernels: 47.5 us -> 44.1 us  [joint_call(): pl.pallas_call(functools.partial(joint_kernel, dims), out_shape=[jax.Shap...]
    concatenate x4 -> x0, other arithmetic: 2.72 us -> none  [the longest x1 0.77 us: local(): jnp.concatenate([own3[jr:jr + js], own3[2 * jr:2 * jr + js], own0[:js, 12...]
    reshape x3 -> x0, local copies, waits for them, and re-layouts: 2.54 us -> none  [the longest x1 0.96 us: local(): pred_ext = pad_to(predictor.reshape(-1, joint), rows * segs * own_u, 768)]
where the time goes in v2:
time: 173 us; the launch traced here: 172 us
  Pallas kernels  169 us (98%)
    pallas_call x1, Pallas kernels, grad_call(): pl.pallas_call(functools.partial(grad_kernel, z, dims, skew), out_shape=[...  65.2 us
    pallas_call x1, Pallas kernels, encode_call(): pl.pallas_call(functools.partial(encode_kernel, z, dims), out_shape=outs,...  56.2 us
    pallas_call x1, Pallas kernels, joint_call(): pl.pallas_call(functools.partial(joint_kernel, dims), out_shape=[jax.Shap...  44.1 us
    pallas_call x1, Pallas kernels, unpack_call(): pl.pallas_call(functools.partial(unpack_kernel, z, dims, js), out_shape=o...  3.47 us

profile of v2, /device:TPU:0, one launch (start us, length us, event | category | flops | bytes accessed | tf_op | source)
XLA Modules:
  0.0 172.3 jit_solution(10868414306319650262)
XLA Ops:
  0.7 1.3 broadcast_in_dim.27.bias_out
  1.9 56.2 %shard_map.373 = (bf16[2688,512]{1,0:T(8,128)(2,1)}, bf16[3584,512]{1,0:T(8,128)(2,1)}, bf16[2688,512]{1,0:T(8,128)(2,1)}, bf16[640,768]{1,0:T(8,128)(2,1)}, bf1...) custom-call(bf16[2,64,512]{2,1,0:T(8,128)(2,1)} %x_ref.1, ...), custom_call_target="tpu_custom_call" | custom-call | tf_op jit(solution)/shard_map/pallas_call | solution.py:1228
  58.2 44.1 %shard_map.374 = (bf16[2,64,640]{2,1,0:T(8,128)(2,1)}, f32[128,640]{1,0:T(8,128)}, bf16[1920,512]{1,0:T(8,128)(2,1)}, bf16[640,256]{1,0:T(8,128)(2,1)}, f32[16,256]{1,0:T(8,128)}, /*index=5*/f32[8,128]{1,0:T(8,128)}) custom-call(bf16[2,64,640]{2,1,0:T(8,128)(2,1)} %get-tuple-element.75.enc_own, bf16[8,4,4,640]{3,2,1,0:T(4,128)(2,1)} %predictor.1, ...), custom_call_target="tpu_custom_call" | custom-call | tf_op jit(solution)/shard_map/pallas_call | solution.py:838
  102.3 65.2 %shard_map.375 = (bf16[336,512]{1,0:T(8,128)(2,1)}, bf16[448,512]{1,0:T(8,128)(2,1)}, bf16[336,512]{1,0:T(8,128)(2,1)}, bf16[240,512]{1,0:T(8,128)(2,1)}, f32[2,64,512]{2,1,0:T(8,128)}) custom-call(bf16[2,64,640]{2,1,0:T(8,128)(2,1)} %get-tuple-element.79.refs_0_, s32[4,8]{1,0:T(4,128)} %bitcast.27, f32[16,512]{1,0:T(8,128)} %get-tuple-element.80.refs_2_, ...), custom_call_target="tpu_custom_call" | custom-call | tf_op jit(solution)/shard_map/pallas_call | solution.py:1319
  167.5 3.5 %shard_map.376 = (f32[4,8]{1,0:T(4,128)}, bf16[2,64,512]{2,1,0:T(8,128)(2,1)}, f32[2,64,512]{2,1,0:T(8,128)}, f32[8,4,4,640]{3,2,1,0:T(4,128)}, f32[1,64]{1,0:T(...) custom-call(bf16[336,512]{1,0:T(8,128)(2,1)} %get-tuple-element.100., ...), custom_call_target="tpu_custom_call" | custom-call | tf_op jit(solution)/shard_map/pallas_call | solution.py:1383
  171.0 1.3 reduce

commit v3 on v2

--- a/solution.py
+++ b/solution.py
@@ -42,19 +42,19 @@
         self.left = (ring_device(self.place - 1, n), self.lab)
         self.twin = (self.dp, self.side * 2 + 1 - self.core)
         self.across = (self.dp, (1 - self.side) * 2 + self.core)
-        self.far = (
-            ring_device(self.place + 1 - 2 * self.core, n),
-            self.lab,
-        )
+        self.far = (ring_device(self.place + 1 - 2 * self.core, n), self.lab)
+        self.far_back = (ring_device(self.place + 2 * self.core - 1, n), self.lab)
+        self.corner = (self.dp, (1 - self.side) * 2 + 1 - self.core)
 
     def at(self, distance):
         return ring_device(self.place + distance, self.n)
 
     def greet(self):
         barrier = pltpu.get_barrier_semaphore()
-        for other in (self.right, self.left, self.twin, self.across):
+        others = (self.right, self.left, self.twin, self.across, self.corner)
+        for other in others:
             pl.semaphore_signal(barrier, inc=1, device_id=other, device_id_type=MESH)
-        pl.semaphore_wait(barrier, 4)
+        pl.semaphore_wait(barrier, len(others))
 
 
 def remote(src, dst, send_sem, recv_sem, device):
@@ -174,46 +174,6 @@
             self.crossed(s - 1)
         if s == self.steps + 1:
             self.crossed(self.steps)
-
-
-def gather_kernel(n, rows_list, *refs):
-    k = len(rows_list)
-    sources, targets = refs[:k], refs[k : 2 * k]
-    ring_recv, x_recv, sems = refs[2 * k :]
-    w = Where(n)
-    w.greet()
-    parts = [
-        Gather(w, sources[i], targets[i], rows_list[i], ring_recv.at[i], x_recv.at[i], sems.at[i])
-        for i in range(k)
-    ]
-    turns = n // 2 + 2
-    for tick in range(k + turns - 1):
-        for s in range(turns - 1, -1, -1):
-            g = tick - s
-            if 0 <= g < k:
-                parts[g].step(s)
-    for part in parts:
-        part.whole()
-        part.drain()
-
-
-def gather_all(n, shards):
-    k = len(shards)
-    rows_list = [s.shape[0] for s in shards]
-    return pl.pallas_call(
-        functools.partial(gather_kernel, n, rows_list),
-        out_shape=[jax.ShapeDtypeStruct((n * s.shape[0], s.shape[1]), s.dtype) for s in shards],
-        in_specs=[pl.BlockSpec(memory_space=pltpu.VMEM)] * k,
-        out_specs=[pl.BlockSpec(memory_space=pltpu.VMEM)] * k,
-        scratch_shapes=[
-            pltpu.SemaphoreType.DMA((k, n - 1)),
-            pltpu.SemaphoreType.DMA((k, n - 1)),
-            pltpu.SemaphoreType.DMA((k, 5)),
-        ],
-        compiler_params=pltpu.CompilerParams(
-            collective_id=0, has_side_effects=True, vmem_limit_bytes=56 * 2**20
-        ),
-    )(*shards)
 
 
 class Pair:
@@ -425,18 +385,6 @@
     return lax.broadcasted_iota(jnp.int32, shape, 0)
 
 
-class Peers:
-    def __init__(self):
-        self.dp, self.lab = lax.axis_index("dp"), lax.axis_index("lab")
-        self.core, self.side = self.lab % 2, self.lab // 2
-
-    def owner(self, j):
-        return ((self.side + j // 2) % 2) * 2 + (self.core + j % 2) % 2
-
-    def device(self, j):
-        return (self.dp, self.owner(j))
-
-
 def seg_of(t, ends):
     return sum((t >= e).astype(jnp.int32) for e in ends[:-1])
 
@@ -461,7 +409,7 @@
     return top, functools.reduce(jnp.add, [jnp.exp(v - top) for v in terms])
 
 
-def lattice(peers, lengths, counts, terms, skewed, hist, grads, loss, dims):
+def lattice(lengths, counts, terms, skewed, hist, grads, loss, dims):
     frames, rows, segs, own_u, labs = dims
     wide = (frames, 128)
     lane = lane_ids(wide)
@@ -624,40 +572,114 @@
     grads[6] = total_a
 
 
-def joint_kernel(
-    dims,
-    enc_own, predictor, lengths, counts, labels, predx, tok, tail, bias_out,
-    g_enc, g_predictor, g_pack, g_mix, g_bias, loss,
-    enc_all, pred_wide, pred, proj, hid, slope, wide, back_w, prob, prob_tail, mine, terms, skewed, hist, grads, g_pred,
-    part, came, send, recv,
+def joint_scratch(dims, width):
+    frames, rows, segs, own_u, labs = dims
+    span, inner = own_u * frames, rows * segs * own_u
+    return [
+        pltpu.VMEM((inner, width), F32),
+        pltpu.VMEM((rows, span, width + 128), BF),
+        pltpu.VMEM((rows, span, width) if width <= ROOMY else (8, 128), BF),
+        pltpu.VMEM((width + 128, VOCAB + 128), BF),
+        pltpu.VMEM((VOCAB, width) if width <= ROOMY else (8, 128), BF),
+        pltpu.VMEM((rows, span, VOCAB), BF),
+        pltpu.VMEM((rows, span, 128), F32),
+        pltpu.VMEM((16, frames + 24, 128), F32),
+        pltpu.VMEM((2, frames + 16, 128), F32),
+        pltpu.VMEM((KINDS, frames, 128), F32),
+        pltpu.VMEM((inner, width), BF),
+    ]
+
+
+def joint_shared(dims, width):
+    frames, rows, segs, own_u, labs = dims
+    micro, inner = rows // labs, rows * segs * own_u
+    return [
+        pltpu.VMEM((micro, frames, width), BF),
+        pltpu.VMEM((rows, frames, width), BF),
+        pltpu.VMEM((inner, 640), F32),
+        pltpu.VMEM((inner, 768), BF),
+        pltpu.VMEM((frames, 256), F32),
+        pltpu.VMEM((labs, frames, 256), F32),
+        pltpu.VMEM((labs, micro, frames, width), BF),
+        pltpu.VMEM((labs, micro, frames, width), BF),
+        pltpu.VMEM((micro, frames, width), BF),
+        pltpu.VMEM((width, 256), BF),
+        pltpu.VMEM((16, 256), F32),
+        pltpu.SemaphoreType.DMA((3, labs)),
+        pltpu.SemaphoreType.DMA((3, labs)),
+    ]
+
+
+class Joint:
+    def __init__(self, z, w, dims, predictor, lengths, counts, labels, bias_out, g_predictor, g_pack, loss, shared):
+        self.z, self.w, self.dims = z, w, dims
+        self.predictor, self.lengths, self.counts, self.labels = predictor, lengths, counts, labels
+        self.bias_out, self.g_predictor, self.g_pack, self.loss = bias_out, g_predictor, g_pack, loss
+        (
+            self.enc_own, self.enc_all, self.pred_wide, self.pred, self.mine, self.terms, self.part, self.came,
+            self.g_enc, self.g_mix, self.g_bias, self.send, self.recv,
+        ) = shared
+        self.micro = dims[1] // dims[4]
+
+    def owner(self, j):
+        return ((self.w.side + j // 2) % 2) * 2 + (self.w.core + j % 2) % 2
+
+    def device(self, j):
+        return (self.w.dp, self.owner(j))
+
+    def enc_copy(self, j, source):
+        to = self.enc_all.at[pl.ds(source * self.micro, self.micro)]
+        return remote(self.enc_own, to, self.send.at[0, j], self.recv.at[0, j], self.device(j))
+
+    def term_copy(self, j, source):
+        return remote(self.mine, self.terms.at[source], self.send.at[1, j], self.recv.at[1, j], self.device(j))
+
+    def part_copy(self, j):
+        return remote(self.part.at[j], self.came.at[j], self.send.at[2, j], self.recv.at[2, j], self.device(j))
+
+    def prepare(self):
+        frames, rows, segs, own_u, labs = self.dims
+        features = self.predictor.shape[-1]
+        for r in range(rows):
+            for s in range(segs):
+                first = (r * segs + s) * own_u
+                self.pred_wide[first : first + own_u, :] = self.predictor[r, s].astype(F32)
+        self.pred[:, :features] = self.pred_wide[...].astype(BF)
+        self.pred[:, features:] = (lane_ids((self.pred.shape[0], 128)) == BIAS_LANE).astype(BF)
+
+    def share(self):
+        for j in range(1, self.dims[4]):
+            self.enc_copy(j, self.w.lab).start()
+        self.enc_all[pl.ds(self.w.lab * self.micro, self.micro)] = self.enc_own[...]
+
+    def drain(self):
+        for j in range(1, self.dims[4]):
+            self.enc_copy(j, self.w.lab).wait_send()
+            self.term_copy(j, self.w.lab).wait_send()
+            self.part_copy(j).wait_send()
+
+    def run(self, full, *scratch):
+        joint_run(self, full, *scratch)
+
+
+def joint_run(
+    job, full, proj, hid, slope, wide, back_w, prob, prob_tail, skewed, hist, grads, g_pred
 ):
+    z, dims, lengths, counts, labels, bias_out = job.z, job.dims, job.lengths, job.counts, job.labels, job.bias_out
     frames, rows, segs, own_u, labs = dims
     micro = rows // labs
-    peers = Peers()
-    barrier = pltpu.get_barrier_semaphore()
-    for j in range(1, labs):
-        pl.semaphore_signal(barrier, inc=1, device_id=peers.device(j), device_id_type=MESH)
-    pl.semaphore_wait(barrier, labs - 1)
-    width = enc_own.shape[-1]
-    span = own_u * frames
-    own_rows = pl.ds(peers.lab * micro, micro)
-
-    def enc_copy(j, source):
-        return remote(enc_own, enc_all.at[pl.ds(source * micro, micro)], send.at[0, j], recv.at[0, j], peers.device(j))
-
-    for j in range(1, labs):
-        enc_copy(j, peers.lab).start()
-    enc_all[own_rows] = enc_own[...]
-    features = predictor.shape[-1]
-    for r in range(rows):
-        for s in range(segs):
-            first = (r * segs + s) * own_u
-            pred_wide[first : first + own_u, :] = predictor[r, s].astype(F32)
-    pred[:, :features] = pred_wide[...].astype(BF)
-    pred[:, features:] = (lane_ids((pred.shape[0], 128)) == BIAS_LANE).astype(BF)
-    proj[...] = mm_t(pred[...], predx[...])
-    wide[:width, :TOK] = tok[...]
-    wide[:width, TOK:VOCAB] = tail[...]
+    n, width, span, features = z.n, z.n * z.jr, own_u * frames, job.predictor.shape[-1]
+    pred, mine, terms, enc_all, part, came = job.pred, job.mine, job.terms, job.enc_all, job.part, job.came
+    enc_copy, term_copy, part_copy, owner = job.enc_copy, job.term_copy, job.part_copy, job.owner
+    g_predictor, g_pack, g_mix, g_bias, g_enc, loss = (
+        job.g_predictor, job.g_pack, job.g_mix, job.g_bias, job.g_enc, job.loss
+    )
+    turn = STEP if width <= ROOMY else 1
+    mixes = rows_of(full[0], n, 0, z.jr)
+    proj[...] = mm_t(pred[:, :512], rows_of(full[3], n, 0, z.jr)) + mm_t(pred[:, 512:], mixes[:, :256])
+    wide[:width, :512] = rows_of(full[3], n, z.jr, z.jr)
+    wide[:width, 512:TOK] = rows_of(full[3], n, 2 * z.jr, z.jr)
+    wide[:width, TOK:VOCAB] = mixes[:, 128:256]
     top_row = row_ids((128, TOK)) == 0
     wide[width:, :TOK] = jnp.where(top_row, bias_out[:, :TOK].astype(F32), 0.0).astype(BF)
     mine[:, :128] = jnp.zeros((frames, 128), F32)
@@ -670,7 +692,9 @@
             for u in range(own_u):
                 wanted = jnp.where(lane_1 == (r * segs + s) * own_u + u, labels[s, u, r], wanted)
     wide[:, VOCAB:] = mm(wide[:, :TOK], (row_ids((TOK, 128)) == wanted).astype(BF)).astype(BF)
-    back_w[...] = wide[:width, :VOCAB].astype(F32).T.astype(BF)
+    roomy = width <= ROOMY
+    if roomy:
+        back_w[...] = wide[:width, :VOCAB].astype(F32).T.astype(BF)
     hid[:, :, width:] = (lane_ids((rows, span, 128)) == 0).astype(BF)
     lane_t = lane_ids((frames, 128))
     lane_w = lane_ids((frames, TOK))
@@ -678,7 +702,7 @@
     per_vreg = 128 // group
 
     def row_of(k):
-        return peers.owner(k // micro) * micro + k % micro
+        return owner(k // micro) * micro + k % micro
 
     def forward(k):
         r = row_of(k)
@@ -692,7 +716,8 @@
             )
             value = jnp.tanh(enc + per_frame)
             hid[r, at, :width] = value.astype(BF)
-            slope[r, at, :] = (1.0 - value * value).astype(BF)
+            if roomy:
+                slope[r, at, :] = (1.0 - value * value).astype(BF)
         logits = mm(hid[r], wide[...])
         seg_l = seg_of(row_ids((frames, 128)), ends)
         for u in range(own_u):
@@ -728,32 +753,26 @@
 
     def forward_step(i, _):
         for j in range(1, labs):
-            @pl.when(i * STEP == j * micro)
+            @pl.when(i * turn == j * micro)
             def _():
-                enc_copy(j, peers.owner(j)).wait_recv()
-        for k in range(STEP):
-            forward(i * STEP + k)
+                enc_copy(j, owner(j)).wait_recv()
+        for k in range(turn):
+            forward(i * turn + k)
         return 0
 
-    lax.fori_loop(0, rows // STEP, forward_step, 0)
-    terms[peers.lab] = mine[...]
-
-    def term_copy(j, source):
-        return remote(mine, terms.at[source], send.at[1, j], recv.at[1, j], peers.device(j))
+    lax.fori_loop(0, rows // turn, forward_step, 0)
+    terms[job.w.lab] = mine[...]
 
     for j in range(1, labs):
-        term_copy(j, peers.lab).start()
+        term_copy(j, job.w.lab).start()
     for j in range(1, labs):
-        term_copy(j, peers.owner(j)).wait_recv()
-    lattice(peers, lengths, counts, terms, skewed, hist, grads, loss, dims)
-
-    def part_copy(j):
-        return remote(part.at[j], came.at[j], send.at[2, j], recv.at[2, j], peers.device(j))
+        term_copy(j, owner(j)).wait_recv()
+    lattice(lengths, counts, terms, skewed, hist, grads, loss, dims)
 
     def backward(k):
         r = row_of(k)
         ends = scalar_ends(lengths, r, segs)
-        shift = (256 - peers.lab * group - r * own_u) % 128
+        shift = (256 - job.w.lab * group - r * own_u) % 128
         rolled = [pltpu.roll(grads[kind], shift, 1) for kind in range(KINDS)]
         seg_l = seg_of(row_ids((frames, TOK)), ends)
         for u in range(own_u):
@@ -768,7 +787,11 @@
             for kind in range(6):
                 aim = jnp.where(lane_t == kind, rolled[kind][:, u : u + 1], aim)
             prob[r, at, TOK:] = jnp.where(lane_t < 6, aim - tails * both, 0.0).astype(BF)
-        back = mm(prob[r], back_w[...]) * slope[r].astype(F32)
+        if roomy:
+            back = mm(prob[r], back_w[...]) * slope[r].astype(F32)
+        else:
+            value = hid[r, :, :width].astype(F32)
+            back = mm_t(prob[r], wide[:width, :VOCAB]) * (1.0 - value * value)
         summed = back[:frames]
         for u in range(1, own_u):
             summed = summed + back[u * frames : (u + 1) * frames]
@@ -780,8 +803,8 @@
         g_pred[pl.ds(r * segs * own_u, segs * own_u), :] = mm(hit, back.astype(BF)).astype(BF)
 
     def backward_step(i, _):
-        first = rows - (i + 1) * STEP
-        for k in range(STEP - 1, -1, -1):
+        first = rows - (i + 1) * turn
+        for k in range(turn - 1, -1, -1):
             backward(first + k)
         for j in range(1, labs):
             @pl.when(first == j * micro)
@@ -789,11 +812,11 @@
                 part_copy(j).start()
         return 0
 
-    lax.fori_loop(0, rows // STEP, backward_step, 0)
+    lax.fori_loop(0, rows // turn, backward_step, 0)
     gp = g_pred[...]
-    g_predictor[...] = mm(gp, predx[:, :features])
-    shards = lax.axis_size("dp")
-    block = width // shards
+    g_predictor[:, :512] = mm(gp, rows_of(full[3], n, 0, z.jr))
+    g_predictor[:, 512:] = mm(gp, rows_of(full[0], n, 0, z.jr)[:, : features - 512])
+    shards, block = n, z.jr
     h_all = hid[...].reshape(rows * span, width + 128)
     g_bias[...] = jnp.zeros(g_bias.shape, F32)
     from_pred = t_mm(gp, pred[...])
@@ -818,61 +841,11 @@
     for j in range(1, labs):
         total = total + came[j].astype(F32)
     g_enc[...] = total.astype(BF)
-    for j in range(1, labs):
-        enc_copy(j, peers.lab).wait_send()
-        term_copy(j, peers.lab).wait_send()
-        part_copy(j).wait_send()
 
 
 VOCAB = TOK + 128
 STEP = 2
-
-
-def joint_call(enc_own, predictor, ints, predx, tok, tail, bias_out, dims):
-    frames, rows, segs, own_u, labs = dims
-    width = enc_own.shape[-1]
-    span = own_u * frames
-    micro = rows // labs
-    vm = pl.BlockSpec(memory_space=pltpu.VMEM)
-    sm = pl.BlockSpec(memory_space=pltpu.SMEM)
-    return pl.pallas_call(
-        functools.partial(joint_kernel, dims),
-        out_shape=[
-            jax.ShapeDtypeStruct((micro, frames, width), BF),
-            jax.ShapeDtypeStruct((rows * segs * own_u, 640), F32),
-            jax.ShapeDtypeStruct((3 * width, 512), BF),
-            jax.ShapeDtypeStruct((width, 256), BF),
-            jax.ShapeDtypeStruct((16, 256), F32),
-            jax.ShapeDtypeStruct((8, 128), F32),
-        ],
-        in_specs=[vm, vm, sm, sm, sm, vm, vm, vm, vm],
-        out_specs=[vm] * 6,
-        scratch_shapes=[
-            pltpu.VMEM((rows, frames, width), BF),
-            pltpu.VMEM((rows * segs * own_u, 640), F32),
-            pltpu.VMEM((rows * segs * own_u, 768), BF),
-            pltpu.VMEM((rows * segs * own_u, width), F32),
-            pltpu.VMEM((rows, span, width + 128), BF),
-            pltpu.VMEM((rows, span, width), BF),
-            pltpu.VMEM((width + 128, VOCAB + 128), BF),
-            pltpu.VMEM((VOCAB, width), BF),
-            pltpu.VMEM((rows, span, VOCAB), BF),
-            pltpu.VMEM((rows, span, 128), F32),
-            pltpu.VMEM((frames, 256), F32),
-            pltpu.VMEM((labs, frames, 256), F32),
-            pltpu.VMEM((16, frames + 24, 128), F32),
-            pltpu.VMEM((2, frames + 16, 128), F32),
-            pltpu.VMEM((KINDS, frames, 128), F32),
-            pltpu.VMEM((rows * segs * own_u, width), BF),
-            pltpu.VMEM((labs, micro, frames, width), BF),
-            pltpu.VMEM((labs, micro, frames, width), BF),
-            pltpu.SemaphoreType.DMA((3, labs)),
-            pltpu.SemaphoreType.DMA((3, labs)),
-        ],
-        compiler_params=pltpu.CompilerParams(
-            collective_id=2, has_side_effects=True, vmem_limit_bytes=60 * 2**20
-        ),
-    )(enc_own, predictor, *ints, predx, tok, tail, bias_out)
+ROOMY = 768
 
 
 HEADS = 8
@@ -1127,20 +1100,21 @@
 )
 
 
-def encode_kernel(
-    z, dims, x_ref, ints, w_in, w_out, w_qkv, w_att, w_pin, w_pout, w_enc, w_pred, w_joint, bias_joint, w_depth,
-    gain0, gain1, gain2, gain3, gain4,
-    full0, full1, full2, predx, tok, tail_out, small_out, encoded, enc_proj, *rest,
+def pass_kernel(
+    z, dims, x_ref, lengths, counts, labels, w_in, w_out, w_qkv, w_att, w_pin, w_pout, w_enc, w_pred, w_joint,
+    bias_joint, w_depth, gain0, gain1, gain2, gain3, gain4, predictor, bias_out,
+    own0, own1, own2, own3, grad_frames, encoded, loss, g_predictor, *rest,
 ):
     k = len(STATE)
     st = {name: ref for (name, _, _), ref in zip(STATE, rest[:k])}
-    probs, rest = rest[k], rest[k + 1 :]
-    sources, full = rest[0:4], rest[4:8]
-    small_in, tail, ring_recv, x_recv, sems, out_sem = rest[8:]
+    probs, small_in, tail, small_ref, small_grad, g_pack = rest[k : k + 6]
+    rest = rest[k + 6 :]
+    sources, full, bufs, rest = rest[:4], rest[4:8], rest[8:28], rest[28:]
+    shared, (ring_recv, x_recv, sems, send, recv) = rest[:-5], rest[-5:]
     n = z.n
     w = Where(n)
-    w.greet()
     jr, js, ds = z.jr, w_pred.shape[0], z.ds
+    job = Joint(z, w, dims, predictor, lengths, counts, labels, bias_out, g_predictor, g_pack, loss, shared)
     small_in[...] = jnp.zeros(small_in.shape, F32)
     small_in[:TAPS, :ds] = w_depth[...].astype(F32)
     for i, gain in enumerate((gain0, gain1, gain2, gain3, gain4)):
@@ -1153,22 +1127,19 @@
     tail[...] = jnp.where(lane_ids((jr, 128)) == BIAS_LANE, column, tail[...])
 
     def down(value, count):
-        return jnp.concatenate([value, jnp.zeros((count - value.shape[0],) + value.shape[1:], value.dtype)], 0) if count > value.shape[0] else value
+        rows = value.shape[0]
+        return jnp.concatenate([value, jnp.zeros((count - rows,) + value.shape[1:], value.dtype)], 0) if count > rows else value
 
     pred_t = down(w_pred[...], jr)
-    sources[0][jr:, :] = w_in[...].astype(F32).T.astype(BF)
-    sources[0][:jr, 0:128] = pred_t[:, 512:]
-    sources[0][:jr, 128:256] = tail[...].astype(BF)
-    sources[0][:jr, 256:] = jnp.zeros((jr, 256), BF)
-    sources[0][:16, 256:384] = small_in[...].astype(BF)
-    parts = [
-        Gather(w, sources[i], full[i], z.rows[i], ring_recv.at[i], x_recv.at[i], sems.at[i]) for i in range(4)
-    ]
-    turns = n // 2 + 2
-    skew = 2
 
     def fill(g):
-        if g == 1:
+        if g == 0:
+            sources[0][jr:, :] = w_in[...].astype(F32).T.astype(BF)
+            sources[0][:jr, 0:128] = pred_t[:, 512:]
+            sources[0][:jr, 128:256] = tail[...].astype(BF)
+            sources[0][:jr, 256:] = jnp.zeros((jr, 256), BF)
+            sources[0][:16, 256:384] = small_in[...].astype(BF)
+        elif g == 1:
             sources[1][: z.ff, :] = w_out[...]
             sources[1][z.ff :, :] = w_qkv[...]
         elif g == 2:
@@ -1181,119 +1152,90 @@
             sources[3][jr : 2 * jr, :] = down(w_joint[:, :512], jr)
             sources[3][2 * jr :, :] = down(w_joint[:, 512:1024], jr)
 
-    outs = (full0, full1, full2)
-    compute = forward_pieces(z, x_ref, ints, dims, full, small_out, st, probs, encoded, enc_proj)
-
-    def finish(g):
-        parts[g].whole()
-        if g < 3:
-            pltpu.make_async_copy(full[g], outs[g], out_sem.at[g]).start()
-
+    parts = [
+        Gather(w, sources[i], full[i], z.rows[i], ring_recv.at[i], x_recv.at[i], sems.at[i]) for i in range(4)
+    ]
+    turns = n // 2 + 2
+    fill(0)
+    w.greet()
+    compute = forward_pieces(z, x_ref, lengths, dims, full, small_ref, st, probs, encoded, job.enc_own)
     for s in range(turns - 2):
         for g in range(4):
-            if s == 0:
+            if s == 0 and g:
                 fill(g)
             parts[g].step(s)
+        if s == 0:
+            job.prepare()
+    pieces = 0
     for what, g in ORDER:
         if what == 0:
             next(compute)
+            pieces += 1
+            if pieces == 5:
+                job.share()
         elif what == 1:
-            finish(g)
+            parts[g].whole()
         else:
             parts[g].step(turns + what)
-
-    predx[:, :512] = rows_of(full[3], n, 0, jr)
-    tok[:, :512] = rows_of(full[3], n, jr, jr)
-    tok[:, 512:] = rows_of(full[3], n, 2 * jr, jr)
-    mixes = rows_of(full[0], n, 0, jr)
-    predx[:, 512:] = mixes[:, :256]
-    tail_out[...] = mixes[:, 128:256]
+    pl.run_scoped(lambda *scratch: job.run(full, *scratch), *joint_scratch(dims, n * jr))
+    outs = (own0, own1, own2, own3)
+
+    def finish(*grads):
+        packs = list(grads) + [g_pack]
+        sums = [
+            Scatter(w, packs[g], outs[g], z.rows[g], bufs[5 * g : 5 * g + 5], send.at[g], recv.at[g], SHARES[3 - g])
+            for g in (3, 2, 1, 0)
+        ]
+        pieces = backward_pieces(
+            z, job.g_enc, lengths, dims, full, small_ref, st, probs, packs, small_grad, grad_frames
+        )
+
+        def work(i):
+            for _ in range((0, 2, 2, 1)[i]):
+                next(pieces)
+            if i == 3:
+                for d in range(n):
+                    at = d * z.rows[0]
+                    packs[0][at : at + jr, :256] = job.g_mix[d * jr : (d + 1) * jr, :]
+                    if jr > 32:
+                        packs[0][at + 32 : at + jr, 256:] = jnp.zeros((jr - 32, 256), BF)
+                    packs[0][at : at + 16, 256:384] = split_small(small_grad[...], d, ds).astype(BF)
+                    packs[0][at : at + 16, 384:] = jnp.zeros((16, 128), BF)
+                    packs[0][at + 16 : at + 32, 256:] = job.g_bias[...].astype(BF)
+
+        sum_up(sums, work, ORDER_SUMS)
+
+    pl.run_scoped(finish, *[pltpu.VMEM((n * z.rows[g], 512), BF) for g in range(3)])
+    job.drain()
     for part in parts:
         part.drain()
-    for g in range(3):
-        pltpu.make_async_copy(full[g], outs[g], out_sem.at[g]).wait()
-
-
-def encode_call(z, dims, x, lengths, *params):
+
+
+def pass_call(z, dims, x, ints, params, predictor, bias_out):
     frames, rows, segs, own_u, labs = dims
     n, micro = z.n, rows // labs
     count, width = micro * frames, n * z.jr
-    vm, sm, hbm = (pl.BlockSpec(memory_space=m) for m in (pltpu.VMEM, pltpu.SMEM, pl.ANY))
+    vm, sm = (pl.BlockSpec(memory_space=m) for m in (pltpu.VMEM, pltpu.SMEM))
     shape = jax.ShapeDtypeStruct
-    outs = [shape((n * z.rows[i], 512), BF) for i in range(3)]
-    outs += [shape((width, 768), BF), shape((width, 1024), BF), shape((width, 128), BF), shape((16, z.model), F32)]
-    outs += [shape((micro, frames, z.model), BF), shape((micro, frames, width), BF)]
-    outs += [shape((count, lanes), dtype) for _, lanes, dtype in STATE]
-    outs += [shape((HEADS, count, count), BF)]
+    outs = [shape((r, 512), BF) for r in z.rows]
+    outs += [shape((micro, frames, z.model), F32), shape((micro, frames, z.model), BF), shape((8, 128), F32)]
+    outs += [shape((rows * segs * own_u, predictor.shape[-1]), F32)]
+    scratch = [pltpu.VMEM((count, lanes), dtype) for _, lanes, dtype in STATE]
+    scratch += [pltpu.VMEM((HEADS, count, count), BF), pltpu.VMEM((16, 128), F32), pltpu.VMEM((z.jr, 128), F32)]
+    scratch += [pltpu.VMEM((16, z.model), F32)] * 2 + [pltpu.VMEM((3 * width, 512), BF)]
+    scratch += [pltpu.VMEM((r, 512), BF) for r in z.rows] + [pltpu.VMEM((n * r, 512), BF) for r in z.rows]
+    for g, r in enumerate(z.rows):
+        scratch += scatter_scratch(n, r, 512, SHARES[3 - g])
+    scratch += joint_shared(dims, width)
+    scratch += [pltpu.SemaphoreType.DMA((4, n - 1))] * 2 + [pltpu.SemaphoreType.DMA((4, 5))] + scatter_sems(n, 4)
     return pl.pallas_call(
-        functools.partial(encode_kernel, z, dims),
+        functools.partial(pass_kernel, z, dims),
         out_shape=outs,
-        in_specs=[vm, sm] + [vm] * len(params),
-        out_specs=[hbm] * 3 + [vm] * (len(outs) - 3),
-        scratch_shapes=[pltpu.VMEM((r, 512), BF) for r in z.rows]
-        + [pltpu.VMEM((n * r, 512), BF) for r in z.rows]
-        + [
-            pltpu.VMEM((16, 128), F32),
-            pltpu.VMEM((z.jr, 128), F32),
-            pltpu.SemaphoreType.DMA((4, n - 1)),
-            pltpu.SemaphoreType.DMA((4, n - 1)),
-            pltpu.SemaphoreType.DMA((4, 5)),
-            pltpu.SemaphoreType.DMA((3,)),
-        ],
-        compiler_params=pltpu.CompilerParams(collective_id=0, has_side_effects=True, vmem_limit_bytes=60 * 2**20),
-    )(x, lengths, *params)
-
-
-def grad_kernel(z, dims, skew, *refs):
-    g_enc, ints, small_ref, g_pack, g_mix, g_bias = refs[:6]
-    hbm = refs[6:9]
-    refs = refs[9:]
-    k = len(STATE)
-    st = {name: ref for (name, _, _), ref in zip(STATE, refs[:k])}
-    probs, refs = refs[k], refs[k + 1 :]
-    outs, grad_frames, refs = refs[:4], refs[4], refs[5:]
-    full, refs = refs[:3], refs[3:]
-    grads, refs = list(refs[:3]) + [g_pack], refs[3:]
-    small_grad, bufs, (send, recv, in_sem) = refs[0], refs[1:21], refs[21:]
-    n = z.n
-    w = Where(n)
-    w.far_back = (ring_device(w.place + 2 * w.core - 1, n), w.lab)
-    for g in (2, 1, 0):
-        pltpu.make_async_copy(hbm[g], full[g], in_sem.at[g]).start()
-    w.greet()
-    order = (3, 2, 1, 0)
-    parts = [
-        Scatter(w, grads[g], outs[g], z.rows[g], bufs[5 * g : 5 * g + 5], send.at[g], recv.at[g], SHARES[3 - g])
-        for g in order
-    ]
-    compute = backward_pieces(z, g_enc, ints, dims, full, small_ref, st, probs, grads, small_grad, grad_frames)
-
-    def load(g):
-        pltpu.make_async_copy(hbm[g], full[g], in_sem.at[g]).wait()
-
-    def work(i):
-        if i == 1:
-            load(2)
-            next(compute)
-            next(compute)
-        elif i == 2:
-            load(1)
-            next(compute)
-            next(compute)
-        elif i == 3:
-            load(0)
-            next(compute)
-            per, ds = z.rows[0], z.ds
-            for d in range(n):
-                at = d * per
-                grads[0][at : at + z.jr, :256] = g_mix[d * z.jr : (d + 1) * z.jr, :]
-                if z.jr > 32:
-                    grads[0][at + 32 : at + z.jr, 256:] = jnp.zeros((z.jr - 32, 256), BF)
-                grads[0][at : at + 16, 256:384] = split_small(small_grad[...], d, ds).astype(BF)
-                grads[0][at : at + 16, 384:] = jnp.zeros((16, 128), BF)
-                grads[0][at + 16 : at + 32, 256:] = g_bias[...].astype(BF)
-
-    sum_up(parts, work, ORDER_SUMS)
+        in_specs=[vm] + [sm] * 3 + [vm] * (len(params) + 2),
+        out_specs=[vm] * len(outs),
+        scratch_shapes=scratch,
+        compiler_params=pltpu.CompilerParams(collective_id=0, has_side_effects=True, vmem_limit_bytes=62 * 2**20),
+    )(x, *ints, *params, predictor, bias_out)
 
 
 SHARES = (0.2, 0.2, 0.3, 0.25)
@@ -1306,24 +1248,6 @@
     (2, 1, 7), (2, 3, 5), (3, 3, 3), (2, 2, 7), (3, 0, 7), (3, 1, 5), (3, 2, 4), (3, 3, 4), (2, 3, 6), (3, 1, 6),
     (3, 2, 5), (3, 1, 7), (2, 3, 7), (3, 3, 5), (3, 2, 6), (3, 3, 6), (3, 2, 7), (3, 3, 7),
 )
-
-
-def grad_call(z, dims, g_enc, ints, small, g_pack, g_mix, g_bias, full, state, probs, skew=1):
-    frames, rows, segs, own_u, labs = dims
-    n, micro = z.n, rows // labs
-    vm, sm, hbm = (pl.BlockSpec(memory_space=m) for m in (pltpu.VMEM, pltpu.SMEM, pl.ANY))
-    shape = jax.ShapeDtypeStruct
-    scratch = [pltpu.VMEM((n * z.rows[g], 512), BF) for g in range(3)] * 2 + [pltpu.VMEM((16, z.model), F32)]
-    for g, r in enumerate(z.rows):
-        scratch += scatter_scratch(n, r, 512, SHARES[3 - g])
-    return pl.pallas_call(
-        functools.partial(grad_kernel, z, dims, skew),
-        out_shape=[shape((r, 512), BF) for r in z.rows] + [shape((micro, frames, z.model), F32)],
-        in_specs=[vm, sm, vm, vm, vm, vm] + [hbm] * 3 + [vm] * (len(STATE) + 1),
-        out_specs=[vm] * 5,
-        scratch_shapes=scratch + scatter_sems(n, 4) + [pltpu.SemaphoreType.DMA((3,))],
-        compiler_params=pltpu.CompilerParams(collective_id=1, has_side_effects=True, vmem_limit_bytes=60 * 2**20),
-    )(g_enc, ints, small, g_pack, g_mix, g_bias, *full, *state, probs)
 
 
 def unpack_kernel(z, dims, js, own0, own1, own2, own3, grads, encoded, loss, g_predictor, *outs):
@@ -1402,16 +1326,13 @@
     dims = (frames, rows, segs, own_u, labs)
     lengths, counts, labels = seg_lengths.T, label_counts.T, label_ids.transpose(1, 2, 0)
     gains = [g[None] for g in (gain_ffn, gain_att, gain_conv, gain_depth, gain_out)]
-    out = encode_call(
-        z, dims, frames_in, lengths, w_ffn_in, w_ffn_out, w_qkv.T, w_att_out, w_point_in, w_point_out, w_enc.T, w_pred.T,
-        w_joint_out, bias_joint[None], w_depth, *gains,
+    params = (
+        w_ffn_in, w_ffn_out, w_qkv.T, w_att_out, w_point_in, w_point_out, w_enc.T, w_pred.T, w_joint_out,
+        bias_joint[None], w_depth, *gains,
     )
-    full, (predx, tok, tail_w, small_w, encoded, enc_proj) = out[:3], out[3:9]
-    state, probs = out[9:-1], out[-1]
-    g_enc, g_predictor, g_pack, g_mix, g_bias, loss = joint_call(
-        enc_proj, predictor, (lengths, counts, labels), predx, tok, tail_w, bias_out[None], dims
+    *own, grad_frames, encoded, loss, g_predictor = pass_call(
+        z, dims, frames_in, (lengths, counts, labels), params, predictor, bias_out[None]
     )
-    *own, grad_frames = grad_call(z, dims, g_enc, lengths, small_w, g_pack, g_mix, g_bias, full, state, probs)
     (
         loss, encoded, grad_frames, g_predictor, gg0, g_in, g_out, gg1, g_qkv, g_att, gg2, g_pin, g_depth, gg3, g_pout,
         gg4, g_enc, g_pred, g_bias, g_joint, g_bias_out,

time: 173 us -> 163 us (0.942)
  Pallas kernels: 169 us -> 159 us
    pallas_call x3 -> x1, Pallas kernels: 166 us -> 156 us  [pass_call(): pl.pallas_call(functools.partial(pass_kernel, z, dims), out_shape=outs, i...]
where the time goes in v3:
time: 163 us
  Pallas kernels  159 us (98%)
  local copies, waits for them, and re-layouts  1.96 us (1%)
    pallas_call x1, Pallas kernels, pass_call(): pl.pallas_call(functools.partial(pass_kernel, z, dims), out_shape=outs, i...  156 us
    pallas_call x1, Pallas kernels, unpack_call(): pl.pallas_call(functools.partial(unpack_kernel, z, dims, js), out_shape=o...  3.47 us

profile of v3, /device:TPU:0, one launch (start us, length us, event | category | flops | bytes accessed | tf_op | source)
XLA Modules:
  0.0 162.6 jit_solution(10889470228150991916)
XLA Ops:
  0.7 0.0 copy-start.1
  0.7 0.7 copy-done.1
  1.3 0.6 broadcast_in_dim.27.bias_out
  1.9 155.9 %shard_map.373 = (bf16[336,512]{1,0:T(8,128)(2,1)}, bf16[448,512]{1,0:T(8,128)(2,1)}, bf16[336,512]{1,0:T(8,128)(2,1)}, bf16[240,512]{1,0:T(8,128)(2,1)}, f32[2,...) custom-call(bf16[2,64,512]{2,1,0:T(8,128)(2,1)} %x_ref.1, ...), custom_call_target="tpu_custom_call" | custom-call | tf_op jit(solution)/shard_map/pallas_call | solution.py:1231
  157.8 3.5 %shard_map.374 = (f32[4,8]{1,0:T(4,128)}, bf16[2,64,512]{2,1,0:T(8,128)(2,1)}, f32[2,64,512]{2,1,0:T(8,128)}, f32[8,4,4,640]{3,2,1,0:T(4,128)}, f32[1,64]{1,0:T(...) custom-call(bf16[336,512]{1,0:T(8,128)(2,1)} %get-tuple-element.50.o, ...), custom_call_target="tpu_custom_call" | custom-call | tf_op jit(solution)/shard_map/pallas_call | solution.py:1307
  161.3 0.0 copy-start
  161.3 0.7 copy-done
  162.0 0.6 reduce
Async XLA Ops:
  0.7 0.7 copy-start.1
  161.3 0.7 copy-start

commit v4 on v3

--- a/solution.py
+++ b/solution.py
@@ -69,11 +69,11 @@
 
 
 class Gather:
-    def __init__(self, where, source, target, rows, ring_recv, x_recv, sems):
+    def __init__(self, where, source, target, rows, ring_recv, x_recv, sems, share):
         self.w, self.source, self.target, self.rows = where, source, target, rows
         self.width = target.shape[1]
         self.half = self.width // 2
-        self.cut = x_rows(rows, 0.3)
+        self.cut = x_rows(rows, share)
         self.ring_recv, self.x_recv, self.sems = ring_recv, x_recv, sems
         self.steps = where.n // 2
 
@@ -151,29 +151,31 @@
                 part = self.target.at[pl.ds(0, count * rows), pl.ds(0, self.half)]
                 remote(part, part, self.sems.at[sem], self.sems.at[sem], self.w.twin).wait_send()
 
-    def step(self, s):
-        if s == 0:
-            self.own()
-        if 1 <= s < self.steps:
-            self.arrived(-s)
-            self.arrived(s)
-        if s == self.steps:
-            self.arrived(self.steps)
-        if s < self.steps - 1:
-            self.hop(-s - 1, s == 0)
-            self.hop(s + 1, s == 0)
-        elif s == self.steps - 1:
+    def begin(self):
+        self.own()
+        self.hop(-1, True)
+        self.hop(1, True)
+
+    def distances(self, named):
+        sign, last = (1 if named > 0 else -1), self.steps
+        if abs(named) == 2:
+            return [sign * d for d in range(2, last - 1)]
+        return [sign * (abs(named) if abs(named) < 2 else last + abs(named) - 4)]
+
+    def take(self, distance):
+        if distance == self.steps:
+            self.arrived(distance)
+            self.spread(distance)
+        elif distance == self.steps - 1:
+            self.arrived(-distance)
+            self.arrived(distance)
             self.hop(self.steps, False)
-        if 1 <= s < self.steps:
-            self.spread(-s)
-            self.spread(s)
-        if s == self.steps:
-            self.spread(self.steps)
-        if 2 <= s <= self.steps:
-            self.crossed(-s + 1)
-            self.crossed(s - 1)
-        if s == self.steps + 1:
-            self.crossed(self.steps)
+            self.spread(-distance)
+            self.spread(distance)
+        else:
+            self.arrived(distance)
+            self.hop(distance + (1 if distance > 0 else -1), False)
+            self.spread(distance)
 
 
 class Pair:
@@ -496,7 +498,7 @@
         keep(9 + d, next_up(value, tall_j))
     keep(14, skew(start))
     keep(15, skew(closing))
-    waves = frames + last_u
+    waves = frames + last_u + 1
     one_j = lane_ids((1, 128)) % own_u
     low_row = skewed[0, 0:1, :]
 
@@ -537,7 +539,7 @@
 
     hist[...] = jnp.full(hist.shape, LOW, F32)
     lax.fori_loop(
-        0, waves, wave, ((low_row,) * 4, (low_row,) * 5, (low_row,) * 4, (low_row,) * 5)
+        0, waves, wave, ((low_row,) * 4, (low_row,) * 5, (low_row,) * 4, (low_row,) * 5), unroll=UNROLL
     )
     alpha, beta = unskew(hist[0]), unskew(hist[1])
     ahead = next_down(beta, j)
@@ -647,14 +649,20 @@
         self.pred[:, :features] = self.pred_wide[...].astype(BF)
         self.pred[:, features:] = (lane_ids((self.pred.shape[0], 128)) == BIAS_LANE).astype(BF)
 
+    def hand_on(self):
+        rows = self.enc_all.at[pl.ds(self.owner(2) * self.micro, self.micro)]
+        return remote(rows, rows, self.send.at[0, 3], self.recv.at[0, 3], self.device(1))
+
     def share(self):
-        for j in range(1, self.dims[4]):
+        for j in (1, 2):
             self.enc_copy(j, self.w.lab).start()
         self.enc_all[pl.ds(self.w.lab * self.micro, self.micro)] = self.enc_own[...]
 
     def drain(self):
+        self.hand_on().wait_send()
         for j in range(1, self.dims[4]):
-            self.enc_copy(j, self.w.lab).wait_send()
+            if j < 3:
+                self.enc_copy(j, self.w.lab).wait_send()
             self.term_copy(j, self.w.lab).wait_send()
             self.part_copy(j).wait_send()
 
@@ -668,6 +676,7 @@
     z, dims, lengths, counts, labels, bias_out = job.z, job.dims, job.lengths, job.counts, job.labels, job.bias_out
     frames, rows, segs, own_u, labs = dims
     micro = rows // labs
+    bias_out = bias_out[...].astype(F32).reshape(1, -1)
     n, width, span, features = z.n, z.n * z.jr, own_u * frames, job.predictor.shape[-1]
     pred, mine, terms, enc_all, part, came = job.pred, job.mine, job.terms, job.enc_all, job.part, job.came
     enc_copy, term_copy, part_copy, owner = job.enc_copy, job.term_copy, job.part_copy, job.owner
@@ -756,6 +765,8 @@
             @pl.when(i * turn == j * micro)
             def _():
                 enc_copy(j, owner(j)).wait_recv()
+                if j == 2:
+                    job.hand_on().start()
         for k in range(turn):
             forward(i * turn + k)
         return 0
@@ -844,6 +855,7 @@
 
 
 VOCAB = TOK + 128
+UNROLL = 8
 STEP = 2
 ROOMY = 768
 
@@ -1094,9 +1106,15 @@
     yield
 
 
+GATHER_SHARES = (0.4, 0.4, 0.2, 0.4)
 ORDER = (
-    (-2, 0), (-2, 1), (-1, 0), (1, 0), (0, 0), (-2, 2), (-1, 1), (0, 0), (-2, 3), (1, 1), (0, 0), (-1, 2), (0, 0), (-1, 3),
-    (1, 2), (0, 0), (1, 3),
+    (0, 0, 0), (0, 1, 0), (0, 2, 0), (0, 3, 0), (1, 0, -1), (1, 0, 1), (1, 1, 1), (2, 0, -1), (1, 1, -1), (2, 0, 1),
+    (1, 2, -1), (1, 2, 1), (1, 3, 1), (2, 1, 1), (1, 3, -1), (1, 0, 2), (1, 0, -2), (2, 1, -1), (2, 3, 1),
+    (2, 3, -1), (1, 1, -2), (2, 0, 2), (1, 1, 2), (2, 0, -2), (1, 2, -2), (1, 2, 2), (1, 3, -2), (1, 3, 2),
+    (2, 1, -2), (2, 2, -1), (2, 2, 1), (1, 0, 3), (2, 1, 2), (2, 2, 2), (2, 2, -2), (2, 3, -2), (1, 1, 3),
+    (2, 0, -3), (2, 3, 2), (1, 2, 3), (2, 0, 3), (2, 1, -3), (1, 0, 4), (2, 1, 3), (2, 2, -3), (1, 1, 4), (1, 2, 4),
+    (2, 0, 4), (1, 3, 3), (2, 2, 3), (2, 1, 4), (3, 0, 0), (4, 0, 0), (1, 3, 4), (4, 1, 0), (2, 2, 4), (2, 3, -3),
+    (2, 3, 3), (3, 1, 0), (4, 2, 0), (2, 3, 4), (3, 2, 0), (4, 3, 0), (4, 4, 0), (3, 3, 0),
 )
 
 
@@ -1153,30 +1171,28 @@
             sources[3][2 * jr :, :] = down(w_joint[:, 512:1024], jr)
 
     parts = [
-        Gather(w, sources[i], full[i], z.rows[i], ring_recv.at[i], x_recv.at[i], sems.at[i]) for i in range(4)
+        Gather(w, sources[i], full[i], z.rows[i], ring_recv.at[i], x_recv.at[i], sems.at[i], GATHER_SHARES[i])
+        for i in range(4)
     ]
-    turns = n // 2 + 2
     fill(0)
     w.greet()
     compute = forward_pieces(z, x_ref, lengths, dims, full, small_ref, st, probs, encoded, job.enc_own)
-    for s in range(turns - 2):
-        for g in range(4):
-            if s == 0 and g:
+    for what, g, distance in ORDER:
+        if what == 0:
+            if g:
                 fill(g)
-            parts[g].step(s)
-        if s == 0:
-            job.prepare()
-    pieces = 0
-    for what, g in ORDER:
-        if what == 0:
+            parts[g].begin()
+            if g == 3:
+                job.prepare()
+        elif what == 3:
+            parts[g].whole()
+        elif what == 4:
             next(compute)
-            pieces += 1
-            if pieces == 5:
+            if g == 4:
                 job.share()
-        elif what == 1:
-            parts[g].whole()
         else:
-            parts[g].step(turns + what)
+            for d in parts[g].distances(distance):
+                (parts[g].take if what == 1 else parts[g].crossed)(d)
     pl.run_scoped(lambda *scratch: job.run(full, *scratch), *joint_scratch(dims, n * jr))
     outs = (own0, own1, own2, own3)
 
@@ -1238,15 +1254,15 @@
     )(x, *ints, *params, predictor, bias_out)
 
 
-SHARES = (0.2, 0.2, 0.3, 0.25)
+SHARES = (0.15, 0.35, 0.2, 0.15)
 ORDER_SUMS = (
-    (0, 0, 0), (0, 1, 0), (0, 2, 0), (1, 0, 0), (3, 0, 0), (2, 0, 1), (0, 3, 0), (1, 1, 0), (2, 1, 1), (2, 0, 2),
-    (3, 1, 0), (1, 2, 0), (2, 2, 1), (2, 1, 2), (1, 3, 0), (3, 2, 0), (3, 0, 1), (2, 0, 3), (2, 2, 2), (3, 3, 0),
-    (2, 3, 1), (2, 1, 3), (3, 0, 2), (3, 1, 1), (2, 0, 4), (2, 2, 3), (2, 3, 2), (2, 1, 4), (3, 0, 3), (3, 1, 2),
-    (2, 0, 5), (2, 2, 4), (3, 2, 1), (2, 3, 3), (2, 1, 5), (3, 0, 4), (3, 1, 3), (3, 3, 1), (2, 2, 5), (3, 2, 2),
-    (2, 0, 6), (2, 3, 4), (3, 0, 5), (2, 1, 6), (3, 3, 2), (2, 0, 7), (3, 1, 4), (3, 2, 3), (2, 2, 6), (3, 0, 6),
-    (2, 1, 7), (2, 3, 5), (3, 3, 3), (2, 2, 7), (3, 0, 7), (3, 1, 5), (3, 2, 4), (3, 3, 4), (2, 3, 6), (3, 1, 6),
-    (3, 2, 5), (3, 1, 7), (2, 3, 7), (3, 3, 5), (3, 2, 6), (3, 3, 6), (3, 2, 7), (3, 3, 7),
+    (0, 0, 0), (0, 1, 0), (0, 2, 0), (1, 0, 0), (3, 0, 0), (2, 0, 1), (0, 3, 0), (1, 1, 0), (3, 1, 0), (2, 1, 1),
+    (2, 0, 2), (1, 2, 0), (3, 2, 0), (2, 2, 1), (2, 1, 2), (1, 3, 0), (3, 3, 0), (2, 3, 1), (3, 0, 1), (2, 0, 3),
+    (2, 2, 2), (2, 1, 3), (2, 3, 2), (3, 0, 2), (3, 1, 1), (2, 0, 4), (2, 2, 3), (2, 1, 4), (3, 1, 2), (3, 2, 1),
+    (2, 3, 3), (3, 0, 3), (2, 0, 5), (3, 3, 1), (2, 2, 4), (2, 1, 5), (3, 2, 2), (3, 1, 3), (2, 0, 6), (3, 3, 2),
+    (2, 3, 4), (2, 1, 6), (3, 0, 4), (2, 2, 5), (3, 2, 3), (3, 1, 4), (3, 3, 3), (2, 1, 7), (2, 0, 7), (2, 3, 5),
+    (3, 2, 4), (3, 1, 5), (3, 3, 4), (2, 2, 6), (3, 0, 5), (3, 2, 5), (3, 3, 5), (3, 1, 6), (2, 2, 7), (2, 3, 6),
+    (3, 0, 6), (3, 2, 6), (3, 3, 6), (3, 1, 7), (2, 3, 7), (3, 0, 7), (3, 2, 7), (3, 3, 7),
 )
 
 
@@ -1331,7 +1347,7 @@
         bias_joint[None], w_depth, *gains,
     )
     *own, grad_frames, encoded, loss, g_predictor = pass_call(
-        z, dims, frames_in, (lengths, counts, labels), params, predictor, bias_out[None]
+        z, dims, frames_in, (lengths, counts, labels), params, predictor, bias_out
     )
     (
         loss, encoded, grad_frames, g_predictor, gg0, g_in, g_out, gg1, g_qkv, g_att, gg2, g_pin, g_depth, gg3, g_pout,

time: 163 us -> 158 us (0.969)
  Pallas kernels: 159 us -> 156 us
    pallas_call x1, Pallas kernels: 156 us -> 152 us  [pass_call(): pl.pallas_call(functools.partial(pass_kernel, z, dims), out_shape=outs, i...]
where the time goes in v4:
time: 158 us
  Pallas kernels  156 us (99%)
    pallas_call x1, Pallas kernels, pass_call(): pl.pallas_call(functools.partial(pass_kernel, z, dims), out_shape=outs, i...  152 us
    pallas_call x1, Pallas kernels, unpack_call(): pl.pallas_call(functools.partial(unpack_kernel, z, dims, js), out_shape=o...  3.47 us

profile of v4, /device:TPU:0, one launch (start us, length us, event | category | flops | bytes accessed | tf_op | source)
XLA Modules:
  0.0 157.6 jit_solution(1473673412224965536)
XLA Ops:
  0.7 152.2 %shard_map.373 = (bf16[336,512]{1,0:T(8,128)(2,1)}, bf16[448,512]{1,0:T(8,128)(2,1)}, bf16[336,512]{1,0:T(8,128)(2,1)}, bf16[240,512]{1,0:T(8,128)(2,1)}, f32[2,...) custom-call(bf16[2,64,512]{2,1,0:T(8,128)(2,1)} %x_ref.1, ...), custom_call_target="tpu_custom_call" | custom-call | tf_op jit(solution)/shard_map/pallas_call | solution.py:1247
  152.8 3.5 %shard_map.374 = (f32[4,8]{1,0:T(4,128)}, bf16[2,64,512]{2,1,0:T(8,128)(2,1)}, f32[2,64,512]{2,1,0:T(8,128)}, f32[8,4,4,640]{3,2,1,0:T(4,128)}, f32[1,64]{1,0:T(...) custom-call(bf16[336,512]{1,0:T(8,128)(2,1)} %get-tuple-element.50.o, ...), custom_call_target="tpu_custom_call" | custom-call | tf_op jit(solution)/shard_map/pallas_call | solution.py:1323
  156.3 0.0 copy-start
  156.3 0.7 copy-done
  157.0 0.6 reduce
Async XLA Ops:
  156.3 0.7 copy-start

commit v5 on v4

--- a/solution.py
+++ b/solution.py
@@ -49,11 +49,12 @@
     def at(self, distance):
         return ring_device(self.place + distance, self.n)
 
-    def greet(self):
+    def greet(self, meanwhile):
         barrier = pltpu.get_barrier_semaphore()
         others = (self.right, self.left, self.twin, self.across, self.corner)
         for other in others:
             pl.semaphore_signal(barrier, inc=1, device_id=other, device_id_type=MESH)
+        meanwhile()
         pl.semaphore_wait(barrier, len(others))
 
 
@@ -1133,25 +1134,23 @@
     w = Where(n)
     jr, js, ds = z.jr, w_pred.shape[0], z.ds
     job = Joint(z, w, dims, predictor, lengths, counts, labels, bias_out, g_predictor, g_pack, loss, shared)
-    small_in[...] = jnp.zeros(small_in.shape, F32)
-    small_in[:TAPS, :ds] = w_depth[...].astype(F32)
-    for i, gain in enumerate((gain0, gain1, gain2, gain3, gain4)):
-        small_in[GAIN_ROW + i : GAIN_ROW + i + 1, :ds] = gain[...].astype(F32)
-    tail[...] = jnp.zeros(tail.shape, F32)
-    tail[:1, :js] = bias_joint[...].astype(F32)
-    column = tail[:8, :].T[:jr, :1]
-    tail[:8, :] = jnp.zeros((8, 128), F32)
-    tail[:js, : w_joint.shape[1] - 1024] = w_joint[:, 1024:].astype(F32)
-    tail[...] = jnp.where(lane_ids((jr, 128)) == BIAS_LANE, column, tail[...])
-
     def down(value, count):
         rows = value.shape[0]
         return jnp.concatenate([value, jnp.zeros((count - rows,) + value.shape[1:], value.dtype)], 0) if count > rows else value
 
-    pred_t = down(w_pred[...], jr)
-
     def fill(g):
+        pred_t = down(w_pred[...], jr)
         if g == 0:
+            small_in[...] = jnp.zeros(small_in.shape, F32)
+            small_in[:TAPS, :ds] = w_depth[...].astype(F32)
+            for i, gain in enumerate((gain0, gain1, gain2, gain3, gain4)):
+                small_in[GAIN_ROW + i : GAIN_ROW + i + 1, :ds] = gain[...].astype(F32)
+            tail[...] = jnp.zeros(tail.shape, F32)
+            tail[:1, :js] = bias_joint[...].astype(F32)
+            column = tail[:8, :].T[:jr, :1]
+            tail[:8, :] = jnp.zeros((8, 128), F32)
+            tail[:js, : w_joint.shape[1] - 1024] = w_joint[:, 1024:].astype(F32)
+            tail[...] = jnp.where(lane_ids((jr, 128)) == BIAS_LANE, column, tail[...])
             sources[0][jr:, :] = w_in[...].astype(F32).T.astype(BF)
             sources[0][:jr, 0:128] = pred_t[:, 512:]
             sources[0][:jr, 128:256] = tail[...].astype(BF)
@@ -1174,8 +1173,7 @@
         Gather(w, sources[i], full[i], z.rows[i], ring_recv.at[i], x_recv.at[i], sems.at[i], GATHER_SHARES[i])
         for i in range(4)
     ]
-    fill(0)
-    w.greet()
+    w.greet(lambda: fill(0))
     compute = forward_pieces(z, x_ref, lengths, dims, full, small_ref, st, probs, encoded, job.enc_own)
     for what, g, distance in ORDER:
         if what == 0:
@@ -1288,8 +1286,8 @@
         out[...] = small[GAIN_ROW + i : GAIN_ROW + i + 1, :ds]
     g_depth[...] = small[:TAPS, :ds]
     for i in range(4):
-        g_bias_out[:, 256 * i : 256 * i + 256] = small[16 + i : 17 + i, :]
-    g_bias_out[:, 1024:] = small[20:21, : g_bias_out.shape[1] - 1024]
+        g_bias_out[256 * i : 256 * i + 256] = small[16 + i, :]
+    g_bias_out[1024:] = small[20, : g_bias_out.shape[0] - 1024]
     g_in[...] = own0[jr:, :].astype(F32).T
     g_out[...] = own1[:ff, :].astype(F32)
     g_qkv[...] = own1[ff:, :].astype(F32)
@@ -1317,7 +1315,7 @@
         shape((rows, segs, own_u, features), F32), row, shape((line, z.ff), F32), shape((z.ff, line), F32), row,
         shape((z.qk, line), F32), shape((z.ds, line), F32), row, shape((line, z.pi), F32), shape((TAPS, z.ds), F32),
         row, shape((z.ds, line), F32), row, shape((js, line), F32), shape((js, features), F32), shape((1, js), F32),
-        shape((js, out_width), F32), shape((1, out_width), F32),
+        shape((js, out_width), F32), shape((out_width,), F32),
     ]
     vm = pl.BlockSpec(memory_space=pltpu.VMEM)
     return pl.pallas_call(
@@ -1355,7 +1353,7 @@
     ) = unpack_call(z, dims, js, bias_out.shape[0], own, grad_frames, encoded, loss, g_predictor)
     return (
         loss.T, encoded, grad_frames, g_predictor, gg0[0], g_in, g_out, gg1[0], g_qkv.T, g_att, gg2[0], g_pin, g_depth,
-        gg3[0], g_pout, gg4[0], g_enc.T, g_pred.T, g_bias[0], g_joint, g_bias_out[0],
+        gg3[0], g_pout, gg4[0], g_enc.T, g_pred.T, g_bias[0], g_joint, g_bias_out,
     )
 
 

time: 158 us -> 156 us (0.987)
  no operation moved by 1% of the time
where the time goes in v5:
time: 156 us
  Pallas kernels  155 us (99%)
    pallas_call x1, Pallas kernels, pass_call(): pl.pallas_call(functools.partial(pass_kernel, z, dims), out_shape=outs, i...  152 us
    pallas_call x1, Pallas kernels, unpack_call(): pl.pallas_call(functools.partial(unpack_kernel, z, dims, js), out_shape=o...  3.47 us

profile of v5, /device:TPU:0, one launch (start us, length us, event | category | flops | bytes accessed | tf_op | source)
XLA Modules:
  0.0 156.3 jit_solution(13350829636694983821)
XLA Ops:
  0.7 152.0 %shard_map.373 = (bf16[336,512]{1,0:T(8,128)(2,1)}, bf16[448,512]{1,0:T(8,128)(2,1)}, bf16[336,512]{1,0:T(8,128)(2,1)}, bf16[240,512]{1,0:T(8,128)(2,1)}, f32[2,...) custom-call(bf16[2,64,512]{2,1,0:T(8,128)(2,1)} %x_ref.1, ...), custom_call_target="tpu_custom_call" | custom-call | tf_op jit(solution)/shard_map/pallas_call | solution.py:1245
  152.6 3.5 %shard_map.374 = (f32[4,8]{1,0:T(4,128)}, bf16[2,64,512]{2,1,0:T(8,128)(2,1)}, f32[2,64,512]{2,1,0:T(8,128)}, f32[8,4,4,640]{3,2,1,0:T(4,128)}, f32[1,64]{1,0:T(...) custom-call(bf16[336,512]{1,0:T(8,128)(2,1)} %get-tuple-element.50.o, ...), custom_call_target="tpu_custom_call" | custom-call | tf_op jit(solution)/shard_map/pallas_call | solution.py:1321
